TPU v7x, 256 devices: a whole 4x4x8 slice. The times are simulated.
256 devices in a mesh: ctx: 16 (over z, core), head: 4 (over x), dp: 4 (over y).
Axes of the slice: x: 4, y: 4, z: 8, core: 2. Of those that a mesh axis runs over, the one named last changes fastest.
Arguments:
- queries: bfloat16 [32768, 4096], P(('dp', 'ctx'), 'head'), parts along dimension 0, may hold values from -6 to 6
- keys: bfloat16 [32768, 4096], P(('dp', 'ctx'), 'head'), parts along dimension 0, may hold values from -6 to 6
- values: bfloat16 [32768, 4096], P(('dp', 'ctx'), 'head'), parts along dimension 0, may hold values from -6 to 6
- out_grad: bfloat16 [32768, 4096], P(('dp', 'ctx'), 'head'), parts along dimension 0, may hold values from -1.1953125 to 1.1953125
- forward_out: bfloat16 [32768, 4096], P(('dp', 'ctx'), 'head'), parts along dimension 0, may hold values from -6 to 6
- log_norm: float32 [32, 32768], P('head', ('dp', 'ctx')), parts along dimension 1, may hold values from 6 to 8
- beacon_keys: bfloat16 [4096, 4096], P(('dp', 'ctx'), 'head'), parts along dimension 0, may hold values from -6 to 6
- beacon_values: bfloat16 [4096, 4096], P(('dp', 'ctx'), 'head'), parts along dimension 0, may hold values from -6 to 6
- beacon_reach: int32 [64], P(('dp', 'ctx')), parts along dimension 0, may hold values from 1 to 16
Outputs:
- query_grad: bfloat16 [32768, 4096], P(('dp', 'ctx'), 'head'), parts along dimension 0
- key_grad: bfloat16 [32768, 4096], P(('dp', 'ctx'), 'head'), parts along dimension 0
- value_grad: bfloat16 [32768, 4096], P(('dp', 'ctx'), 'head'), parts along dimension 0
- beacon_key_grad: bfloat16 [4096, 4096], P(('dp', 'ctx'), 'head'), parts along dimension 0
- beacon_value_grad: bfloat16 [4096, 4096], P(('dp', 'ctx'), 'head'), parts along dimension 0
There are 4 independent parts, one for each index of `dp`. A program takes and returns all parts, laid end to end along the dimension named above; each array names one. Nothing has to cross between parts.
All inputs are finite; a program needn't handle non-finite values.
Results may differ from a plain program's by a relative error of at most 0.0054.
Values may be sent and summed in bfloat16 or wider, within the bound.
No kernel may reach another device: no remote copies, remote signals or barrier semaphores. Data moves between devices by JAX's collectives and lax.ppermute only.
A program may use at most 128 MiB of HBM per device.

v0:
```python
import math

import jax
import jax.numpy as jnp
from jax import lax
from jax.sharding import PartitionSpec as P

HD = 128
GROUP = 512
BPC = 64


def beacon_block(key_rows, value_rows, offset, context):
    query_heads, grad_heads, norm_rows, delta_rows, row_group, row_reach = context
    piece_rows = key_rows.shape[0]
    scaling = 1.0 / math.sqrt(HD)
    key_heads = key_rows.reshape(piece_rows, -1, HD)
    value_heads = value_rows.reshape(piece_rows, -1, HD)
    col_group = (offset + jnp.arange(piece_rows, dtype=jnp.int32)) // BPC
    allowed = (col_group[None, :] <= row_group[:, None]) & (
        col_group[None, :] > (row_group - row_reach)[:, None]
    )
    scores = (
        jnp.einsum("qhd,khd->hqk", query_heads, key_heads, preferred_element_type=jnp.float32)
        * scaling
    )
    probs = jnp.where(allowed[None], jnp.exp(scores - norm_rows[:, :, None]), 0.0)
    dprobs = jnp.einsum("qhd,khd->hqk", grad_heads, value_heads, preferred_element_type=jnp.float32)
    dscores = (probs * (dprobs - delta_rows[:, :, None])).astype(jnp.bfloat16)
    results = ()
    query_part = (
        jnp.einsum("hqk,khd->qhd", dscores, key_heads, preferred_element_type=jnp.float32) * scaling
    )
    results = results + (query_part,)
    weights = probs.astype(jnp.bfloat16)
    key_part = (
        jnp.einsum("hqk,qhd->khd", dscores, query_heads, preferred_element_type=jnp.float32)
        * scaling
    )
    value_part = jnp.einsum("hqk,qhd->khd", weights, grad_heads, preferred_element_type=jnp.float32)
    results = results + (key_part.reshape(piece_rows, -1), value_part.reshape(piece_rows, -1))
    return results


def guarded(key_rows, value_rows, offset, context):
    return beacon_block(key_rows, value_rows, offset, context)


def sweep(query_total, key_rows, value_rows, context):
    piece_rows = key_rows.shape[0]
    feature_width = key_rows.shape[1]
    block_rows = math.gcd(piece_rows, 256)
    block_count = piece_rows // block_rows
    key_blocks = key_rows.reshape(block_count, block_rows, feature_width)
    value_blocks = value_rows.reshape(block_count, block_rows, feature_width)
    starts = jnp.arange(block_count, dtype=jnp.int32) * block_rows

    def step(carried, pieces_in):
        key_block, value_block, block_start = pieces_in
        parts = guarded(key_block, value_block, block_start, context)
        return (carried + parts[0], parts[1:])

    query_total, side_terms = lax.scan(step, query_total, (key_blocks, value_blocks, starts))
    side_rows = tuple((term.reshape(piece_rows, feature_width) for term in side_terms))
    return (query_total,) + side_rows


def local(
    queries, keys, values, out_grad, forward_out, log_norm, beacon_keys, beacon_values, beacon_reach
):
    row_count = queries.shape[0]
    feature_width = queries.shape[1]
    head_count = log_norm.shape[0]
    per_device = row_count // GROUP
    scaling = 1.0 / math.sqrt(HD)
    query_heads = queries.reshape(row_count, head_count, HD)
    grad_heads = out_grad.reshape(row_count, head_count, HD)
    output_heads = forward_out.reshape(row_count, head_count, HD)
    delta = jnp.einsum("qhd,qhd->hq", grad_heads, output_heads, preferred_element_type=jnp.float32)
    group_ids = lax.axis_index("ctx") * per_device + jnp.arange(per_device, dtype=jnp.int32)
    row_group = jnp.repeat(group_ids, GROUP)
    row_reach = jnp.repeat(beacon_reach, GROUP)
    context = (query_heads, grad_heads, log_norm, delta, row_group, row_reach)
    query_start = jnp.zeros((row_count, head_count, HD), jnp.float32)
    whole_keys, whole_values = (
        lax.all_gather(beacon_keys, "ctx", axis=0, tiled=True),
        lax.all_gather(beacon_values, "ctx", axis=0, tiled=True),
    )
    query_beacon, key_terms, value_terms = sweep(query_start, whole_keys, whole_values, context)
    beacon_key_sum, beacon_value_sum = (
        lax.psum_scatter(key_terms, "ctx", scatter_dimension=0, tiled=True),
        lax.psum_scatter(value_terms, "ctx", scatter_dimension=0, tiled=True),
    )
    query4 = queries.reshape(per_device, GROUP, head_count, HD)
    key4 = keys.reshape(per_device, GROUP, head_count, HD)
    value4 = values.reshape(per_device, GROUP, head_count, HD)
    grad4 = out_grad.reshape(per_device, GROUP, head_count, HD)
    norm4 = log_norm.reshape(head_count, per_device, GROUP).transpose(1, 0, 2)
    delta4 = delta.reshape(head_count, per_device, GROUP).transpose(1, 0, 2)
    causal = jnp.arange(GROUP)[:, None] >= jnp.arange(GROUP)[None, :]
    raw_scores = (
        jnp.einsum("cqhd,ckhd->chqk", query4, key4, preferred_element_type=jnp.float32) * scaling
    )
    raw_probs = jnp.where(causal[None, None], jnp.exp(raw_scores - norm4[:, :, :, None]), 0.0)
    raw_dprobs = jnp.einsum("cqhd,ckhd->chqk", grad4, value4, preferred_element_type=jnp.float32)
    raw_ds = (raw_probs * (raw_dprobs - delta4[:, :, :, None])).astype(jnp.bfloat16)
    raw_weights = raw_probs.astype(jnp.bfloat16)
    query_raw = (
        jnp.einsum("chqk,ckhd->cqhd", raw_ds, key4, preferred_element_type=jnp.float32) * scaling
    )
    key_raw = (
        jnp.einsum("chqk,cqhd->ckhd", raw_ds, query4, preferred_element_type=jnp.float32) * scaling
    )
    value_raw = jnp.einsum(
        "chqk,cqhd->ckhd", raw_weights, grad4, preferred_element_type=jnp.float32
    )
    query_total = query_beacon + query_raw.reshape(row_count, head_count, HD)
    query_grad = query_total.reshape(row_count, feature_width).astype(jnp.bfloat16)
    key_grad = key_raw.reshape(row_count, feature_width).astype(jnp.bfloat16)
    value_grad = value_raw.reshape(row_count, feature_width).astype(jnp.bfloat16)
    return (
        query_grad,
        key_grad,
        value_grad,
        beacon_key_sum.astype(jnp.bfloat16),
        beacon_value_sum.astype(jnp.bfloat16),
    )


def solution(mesh):
    in_specs = (
        P(("dp", "ctx"), "head"),
        P(("dp", "ctx"), "head"),
        P(("dp", "ctx"), "head"),
        P(("dp", "ctx"), "head"),
        P(("dp", "ctx"), "head"),
        P("head", ("dp", "ctx")),
        P(("dp", "ctx"), "head"),
        P(("dp", "ctx"), "head"),
        P(("dp", "ctx")),
    )
    out_specs = (
        P(("dp", "ctx"), "head"),
        P(("dp", "ctx"), "head"),
        P(("dp", "ctx"), "head"),
        P(("dp", "ctx"), "head"),
        P(("dp", "ctx"), "head"),
    )
    return jax.shard_map(local, mesh=mesh, in_specs=in_specs, out_specs=out_specs, check_vma=False)
```

profile of v0, /device:TPU:6, one launch (start us, length us, event | category | flops | bytes accessed | tf_op | source)
XLA Modules:
  0.0 339.5 jit_solution(8497237824220500597)
XLA Ops:
  8.8 1.5 copy.58
  10.3 2.3 copy.59
  12.5 2.6 copy.84
  15.4 2.3 multiply_reduce_fusion
  18.5 34.0 %all-gather.3.cloned.1.call-done = bf16[1024,1024]{1,0:T(8,128)(2,1)} async-done(((bf16[64,1024]{1,0:T(8,128)(2,1)}), bf16[1024,1024]{1,0:T(8,128)(2,1)}) %all-gather.3.cloned.1.call-update) | async-done | bytes 2097168 | tf_op jit(solution)/shard_map/all_gather | solution.py:86
  52.5 39.9 %all-gather.5.cloned.1.call-done = bf16[1024,1024]{1,0:T(8,128)(2,1)} async-done(((bf16[64,1024]{1,0:T(8,128)(2,1)}), bf16[1024,1024]{1,0:T(8,128)(2,1)}) %all-gather.5.cloned.1.call-update) | async-done | bytes 2097168 | tf_op jit(solution)/shard_map/all_gather | solution.py:87
  92.4 113.9 %while.17 = (s32[]{:T(128)}, f32[512,8,128]{0,2,1:T(8,128)}, f32[4,256,1024]{2,1,0:T(8,128)}, f32[4,256,1024]{2,1,0:T(8,128)}, bf16[4,256,1024]{2,1,0:T(8,128)(2...) while((s32[]{:T(128)}, f32[512,8,128]{0,2,1:T(8,128)}, ...), condition=%wide.region_1.2_spmd.clone, body=%wide.region_0.1_spmd.clone.sunk | while | flops 1354502912 | bytes 70829104 | solution.py:63
  92.4 1.4 constant_dynamic-slice_fusion.4
  94.1 2.7 fusion.72
  96.8 1.1 constant_dynamic-slice_fusion.5
  97.9 1.0 copy.107
  100.0 4.2 %fusion.73 = bf16[8,512,256]{1,2,0:T(8,128)(2,1)S(1)} fusion(f32[8,256,512]{2,1,0:T(8,128)} %fusion.72, bf16[256,8,128]{0,2,1:T(8,128)(2,1)} %bitcast.128, bf16[512,8,128]{0,2,1:T(8,128)(2,1)} %get-tuple-element.409, f32[8,512]{1,0:T(8,128)S(1)} %get-tuple-element.410, f32[8,512]{1,0:T(8,128)S(1)} %get-tuple-element.407, ...), kind=kOutput, calls=%fused_computation.3.clone.1 | convolution fusion | flops 274726912 | bytes 7897344 | tf_op jit(solution)/shard_map/while/body/eval_jaxpr/qhd,khd->hqk/dot_general | solution.py:28
  104.2 3.0 bitcast_add_fusion.3
  107.2 3.2 fusion.74
  110.4 2.5 copy.108
  113.0 3.0 convolution_multiply_fusion.2
  116.0 1.6 copy.109
  117.6 2.8 constant_dynamic-update-slice_fusion.3
  120.4 1.4 constant_dynamic-slice_fusion.4
  122.1 2.7 fusion.72
  124.8 1.1 constant_dynamic-slice_fusion.5
  125.9 1.0 copy.107
  128.0 4.2 %fusion.73 = bf16[8,512,256]{1,2,0:T(8,128)(2,1)S(1)} fusion(f32[8,256,512]{2,1,0:T(8,128)} %fusion.72, bf16[256,8,128]{0,2,1:T(8,128)(2,1)} %bitcast.128, bf16[512,8,128]{0,2,1:T(8,128)(2,1)} %get-tuple-element.409, f32[8,512]{1,0:T(8,128)S(1)} %get-tuple-element.410, f32[8,512]{1,0:T(8,128)S(1)} %get-tuple-element.407, ...), kind=kOutput, calls=%fused_computation.3.clone.1 | convolution fusion | flops 274726912 | bytes 7897344 | tf_op jit(solution)/shard_map/while/body/eval_jaxpr/qhd,khd->hqk/dot_general | solution.py:28
  132.2 3.7 %bitcast_add_fusion.3 = f32[512,8,128]{0,2,1:T(8,128)} fusion(f32[512,8,128]{0,2,1:T(8,128)} %get-tuple-element.386, bf16[256,8,128]{0,2,1:T(8,128)(2,1)} %bitcast.125, bf16[8,512,256]{1,2,0:T(8,128)(2,1)S(1)} %fusion.73, pred[]{:T(512)S(6)} %compare.14), kind=kOutput, calls=%fused_computation.7.clone.1 | convolution fusion | flops 270008320 | bytes 6815745 | tf_op jit(solution)/shard_map/while/body/eval_jaxpr/hqk,khd->qhd/dot_general | solution.py:32
  135.9 3.2 fusion.74
  139.1 2.5 copy.108
  141.7 3.0 convolution_multiply_fusion.2
  144.7 1.6 copy.109
  146.3 2.7 constant_dynamic-update-slice_fusion.3
  149.1 1.4 constant_dynamic-slice_fusion.4
  150.7 2.7 fusion.72
  153.4 1.1 constant_dynamic-slice_fusion.5
  154.5 1.0 copy.107
  156.6 4.2 %fusion.73 = bf16[8,512,256]{1,2,0:T(8,128)(2,1)S(1)} fusion(f32[8,256,512]{2,1,0:T(8,128)} %fusion.72, bf16[256,8,128]{0,2,1:T(8,128)(2,1)} %bitcast.128, bf16[512,8,128]{0,2,1:T(8,128)(2,1)} %get-tuple-element.409, f32[8,512]{1,0:T(8,128)S(1)} %get-tuple-element.410, f32[8,512]{1,0:T(8,128)S(1)} %get-tuple-element.407, ...), kind=kOutput, calls=%fused_computation.3.clone.1 | convolution fusion | flops 274726912 | bytes 7897344 | tf_op jit(solution)/shard_map/while/body/eval_jaxpr/qhd,khd->hqk/dot_general | solution.py:28
  160.8 3.7 %bitcast_add_fusion.3 = f32[512,8,128]{0,2,1:T(8,128)} fusion(f32[512,8,128]{0,2,1:T(8,128)} %get-tuple-element.386, bf16[256,8,128]{0,2,1:T(8,128)(2,1)} %bitcast.125, bf16[8,512,256]{1,2,0:T(8,128)(2,1)S(1)} %fusion.73, pred[]{:T(512)S(6)} %compare.14), kind=kOutput, calls=%fused_computation.7.clone.1 | convolution fusion | flops 270008320 | bytes 6815745 | tf_op jit(solution)/shard_map/while/body/eval_jaxpr/hqk,khd->qhd/dot_general | solution.py:32
  164.6 3.2 fusion.74
  167.8 2.5 copy.108
  170.3 3.0 convolution_multiply_fusion.2
  173.3 1.6 copy.109
  175.0 2.7 constant_dynamic-update-slice_fusion.3
  177.7 1.4 constant_dynamic-slice_fusion.4
  179.3 2.7 fusion.72
  182.1 1.1 constant_dynamic-slice_fusion.5
  183.1 1.0 copy.107
  185.3 4.2 %fusion.73 = bf16[8,512,256]{1,2,0:T(8,128)(2,1)S(1)} fusion(f32[8,256,512]{2,1,0:T(8,128)} %fusion.72, bf16[256,8,128]{0,2,1:T(8,128)(2,1)} %bitcast.128, bf16[512,8,128]{0,2,1:T(8,128)(2,1)} %get-tuple-element.409, f32[8,512]{1,0:T(8,128)S(1)} %get-tuple-element.410, f32[8,512]{1,0:T(8,128)S(1)} %get-tuple-element.407, ...), kind=kOutput, calls=%fused_computation.3.clone.1 | convolution fusion | flops 274726912 | bytes 7897344 | tf_op jit(solution)/shard_map/while/body/eval_jaxpr/qhd,khd->hqk/dot_general | solution.py:28
  189.4 3.7 %bitcast_add_fusion.3 = f32[512,8,128]{0,2,1:T(8,128)} fusion(f32[512,8,128]{0,2,1:T(8,128)} %get-tuple-element.386, bf16[256,8,128]{0,2,1:T(8,128)(2,1)} %bitcast.125, bf16[8,512,256]{1,2,0:T(8,128)(2,1)S(1)} %fusion.73, pred[]{:T(512)S(6)} %compare.14), kind=kOutput, calls=%fused_computation.7.clone.1 | convolution fusion | flops 270008320 | bytes 6815745 | tf_op jit(solution)/shard_map/while/body/eval_jaxpr/hqk,khd->qhd/dot_general | solution.py:32
  193.2 3.2 fusion.74
  196.4 2.5 copy.108
  198.9 3.0 convolution_multiply_fusion.2
  201.9 1.6 copy.109
  203.6 2.8 constant_dynamic-update-slice_fusion.3
  207.0 1.5 copy.95
  208.6 1.3 fusion.30
  209.9 5.0 %multiply_convert_fusion = bf16[8,512,512]{2,1,0:T(8,128)(2,1)S(1)} fusion(f32[8,512,512]{2,1,0:T(8,128)S(1)} %fusion.30, f32[8,512]{1,0:T(8,128)S(1)} %get-tuple-element.432, f32[8,512]{1,0:T(8,128)S(1)} %get-tuple-element.433, pred[512,512]{1,0:T(8,128)(4,1)S(1)} %iota_compare_fusion, bf16[512,8,128]{0,2,1:T(8,128)(2,1)} %bitcast.5, ...), kind=kOutput, calls=%fused_computation.24 | convolution fusion | flops 549453824 | bytes 14974976 | tf_op jit(solution)/shard_map/cqhd,ckhd->chqk/dot_general | solution.py:105
  215.6 1.2 copy-done.6
  216.9 1.3 copy.70
  218.2 6.9 %fusion.22 = bf16[8,512,128]{1,2,0:T(8,128)(2,1)} fusion(bf16[512,8,128]{0,2,1:T(8,128)(2,1)} %bitcast.5, f32[8,512,512]{2,1,0:T(8,128)} %copy-done.8, f32[8,512]{1,0:T(8,128)S(1)} %get-tuple-element.433, pred[512,512]{1,0:T(8,128)(4,1)S(1)} %iota_compare_fusion), kind=kOutput, calls=%fused_computation.36 | convolution fusion | flops 545783808 | bytes 10764288 | tf_op jit(solution)/shard_map/chqk,cqhd->ckhd/dot_general | solution.py:114
  225.0 2.3 copy.71
  227.3 5.0 %fusion.21 = bf16[512,8,128]{0,2,1:T(8,128)(2,1)} fusion(f32[512,8,128]{0,2,1:T(8,128)S(1)} %copy-done.5, bf16[8,512,512]{2,1,0:T(8,128)(2,1)} %copy-done.6, bf16[512,8,128]{0,2,1:T(8,128)(2,1)} %bitcast.130), kind=kOutput, calls=%fused_computation.33 | convolution fusion | flops 538443776 | bytes 8388608 | tf_op jit(solution)/shard_map/chqk,ckhd->cqhd/dot_general | solution.py:109
  232.3 2.3 copy.69
  234.6 33.1 %reduce-scatter.3.cloned.1.call-done = f32[64,1024]{1,0:T(8,128)} async-done(((f32[1024,1024]{1,0:T(8,128)}), f32[64,1024]{1,0:T(8,128)}) %reduce-scatter.3.cloned.1.call-update) | async-done | bytes 262160 | tf_op jit(solution)/shard_map/reduce_scatter | solution.py:91
  267.7 1.6 convert_element_type.76
  269.3 62.0 %reduce-scatter.5.cloned.1.call-done = f32[64,1024]{1,0:T(8,128)} async-done(((f32[1024,1024]{1,0:T(8,128)}), f32[64,1024]{1,0:T(8,128)}) %reduce-scatter.5.cloned.1.call-update) | async-done | bytes 262160 | tf_op jit(solution)/shard_map/reduce_scatter | solution.py:92
  331.3 1.6 convert_element_type.77
  (73 shorter events, 8.6 us)
Async XLA Ops:
  7.2 202.7 %copy-start = (bf16[512,1024]{1,0:T(8,128)(2,1)S(1)}, bf16[512,1024]{1,0:T(8,128)(2,1)}, u32[]{:S(2)}) copy-start(bf16[512,1024]{1,0:T(8,128)(2,1)} %param.13) | copy-start | bytes 3145732
  7.2 8.0 %copy-start.9 = (bf16[512,1024]{1,0:T(8,128)(2,1)S(1)}, bf16[512,1024]{1,0:T(8,128)(2,1)}, u32[]{:S(2)}) copy-start(bf16[512,1024]{1,0:T(8,128)(2,1)} %param.15) | copy-start | bytes 3145732
  7.2 45.3 %all-gather.3.cloned.1.call-start = ((), (), s32[]{:S(2)}) async-start(), calls=%async_computation.2 | async-start | bytes 2228224 | tf_op jit(solution)/shard_map/all_gather | solution.py:86
  7.9 84.5 %all-gather.5.cloned.1.call-start = ((), (), s32[]{:S(2)}) async-start(), calls=%async_computation.3 | async-start | bytes 2228224 | tf_op jit(solution)/shard_map/all_gather | solution.py:87
  8.7 259.0 %reduce-scatter.3.cloned.1.call-start = ((), (), s32[]{:S(2)}) async-start(), calls=%async_computation.4 | async-start | bytes 4456448 | tf_op jit(solution)/shard_map/reduce_scatter | solution.py:91
  12.5 79.9 %copy-start.10 = (f32[8,512]{1,0:T(8,128)S(1)}, f32[8,512]{1,0:T(8,128)}, u32[]{:S(2)}) copy-start(f32[8,512]{1,0:T(8,128)} %param.16) | copy-start | bytes 49156
  92.4 5.5 %copy-start.1 = (bf16[512,8,128]{0,2,1:T(8,128)(2,1)}, bf16[512,8,128]{0,2,1:T(8,128)(2,1)S(1)}, u32[]{:S(2)}) copy-start(bf16[512,8,128]{0,2,1:T(8,128)(2,1)S(1)} %get-tuple-element.406) | copy-start | bytes 3145732 | tf_op jit(solution)/shard_map/while
  94.1 5.4 %copy-start.3 = (bf16[1,256,1024]{1,2,0:T(8,128)(2,1)}, bf16[1,256,1024]{1,2,0:T(8,128)(2,1)S(1)}, u32[]{:S(2)}) copy-start(bf16[1,256,1024]{1,2,0:T(8,128)(2,1)S(1)} %copy.106) | copy-start | bytes 1572868 | tf_op jit(solution)/shard_map/while
  104.2 3.0 copy-start.4
  116.0 4.4 %copy-start.2 = (bf16[512,8,128]{0,2,1:T(8,128)(2,1)S(1)}, bf16[512,8,128]{0,2,1:T(8,128)(2,1)}, u32[]{:S(2)}) copy-start(bf16[512,8,128]{0,2,1:T(8,128)(2,1)} %copy-done.1) | copy-start | bytes 3145732 | tf_op jit(solution)/shard_map/while
  120.4 5.5 %copy-start.1 = (bf16[512,8,128]{0,2,1:T(8,128)(2,1)}, bf16[512,8,128]{0,2,1:T(8,128)(2,1)S(1)}, u32[]{:S(2)}) copy-start(bf16[512,8,128]{0,2,1:T(8,128)(2,1)S(1)} %get-tuple-element.406) | copy-start | bytes 3145732 | tf_op jit(solution)/shard_map/while
  122.1 5.4 %copy-start.3 = (bf16[1,256,1024]{1,2,0:T(8,128)(2,1)}, bf16[1,256,1024]{1,2,0:T(8,128)(2,1)S(1)}, u32[]{:S(2)}) copy-start(bf16[1,256,1024]{1,2,0:T(8,128)(2,1)S(1)} %copy.106) | copy-start | bytes 1572868 | tf_op jit(solution)/shard_map/while
  132.2 3.8 %copy-start.4 = (f32[8,256,512]{2,1,0:T(8,128)S(1)}, f32[8,256,512]{2,1,0:T(8,128)}, u32[]{:S(2)}) copy-start(f32[8,256,512]{2,1,0:T(8,128)} %fusion.72) | copy-start | bytes 12582916 | tf_op jit(solution)/shard_map/while
  144.7 4.4 %copy-start.2 = (bf16[512,8,128]{0,2,1:T(8,128)(2,1)S(1)}, bf16[512,8,128]{0,2,1:T(8,128)(2,1)}, u32[]{:S(2)}) copy-start(bf16[512,8,128]{0,2,1:T(8,128)(2,1)} %copy-done.1) | copy-start | bytes 3145732 | tf_op jit(solution)/shard_map/while
  149.1 5.5 %copy-start.1 = (bf16[512,8,128]{0,2,1:T(8,128)(2,1)}, bf16[512,8,128]{0,2,1:T(8,128)(2,1)S(1)}, u32[]{:S(2)}) copy-start(bf16[512,8,128]{0,2,1:T(8,128)(2,1)S(1)} %get-tuple-element.406) | copy-start | bytes 3145732 | tf_op jit(solution)/shard_map/while
  150.7 5.4 %copy-start.3 = (bf16[1,256,1024]{1,2,0:T(8,128)(2,1)}, bf16[1,256,1024]{1,2,0:T(8,128)(2,1)S(1)}, u32[]{:S(2)}) copy-start(bf16[1,256,1024]{1,2,0:T(8,128)(2,1)S(1)} %copy.106) | copy-start | bytes 1572868 | tf_op jit(solution)/shard_map/while
  160.8 3.8 %copy-start.4 = (f32[8,256,512]{2,1,0:T(8,128)S(1)}, f32[8,256,512]{2,1,0:T(8,128)}, u32[]{:S(2)}) copy-start(f32[8,256,512]{2,1,0:T(8,128)} %fusion.72) | copy-start | bytes 12582916 | tf_op jit(solution)/shard_map/while
  173.3 4.4 %copy-start.2 = (bf16[512,8,128]{0,2,1:T(8,128)(2,1)S(1)}, bf16[512,8,128]{0,2,1:T(8,128)(2,1)}, u32[]{:S(2)}) copy-start(bf16[512,8,128]{0,2,1:T(8,128)(2,1)} %copy-done.1) | copy-start | bytes 3145732 | tf_op jit(solution)/shard_map/while
  177.7 5.5 %copy-start.1 = (bf16[512,8,128]{0,2,1:T(8,128)(2,1)}, bf16[512,8,128]{0,2,1:T(8,128)(2,1)S(1)}, u32[]{:S(2)}) copy-start(bf16[512,8,128]{0,2,1:T(8,128)(2,1)S(1)} %get-tuple-element.406) | copy-start | bytes 3145732 | tf_op jit(solution)/shard_map/while
  179.3 5.4 %copy-start.3 = (bf16[1,256,1024]{1,2,0:T(8,128)(2,1)}, bf16[1,256,1024]{1,2,0:T(8,128)(2,1)S(1)}, u32[]{:S(2)}) copy-start(bf16[1,256,1024]{1,2,0:T(8,128)(2,1)S(1)} %copy.106) | copy-start | bytes 1572868 | tf_op jit(solution)/shard_map/while
  189.4 3.8 %copy-start.4 = (f32[8,256,512]{2,1,0:T(8,128)S(1)}, f32[8,256,512]{2,1,0:T(8,128)}, u32[]{:S(2)}) copy-start(f32[8,256,512]{2,1,0:T(8,128)} %fusion.72) | copy-start | bytes 12582916 | tf_op jit(solution)/shard_map/while
  201.9 4.4 %copy-start.2 = (bf16[512,8,128]{0,2,1:T(8,128)(2,1)S(1)}, bf16[512,8,128]{0,2,1:T(8,128)(2,1)}, u32[]{:S(2)}) copy-start(bf16[512,8,128]{0,2,1:T(8,128)(2,1)} %copy-done.1) | copy-start | bytes 3145732 | tf_op jit(solution)/shard_map/while
  206.4 124.9 %reduce-scatter.5.cloned.1.call-start = ((), (), s32[]{:S(2)}) async-start(), calls=%async_computation.5 | async-start | bytes 4456448 | tf_op jit(solution)/shard_map/reduce_scatter | solution.py:92
  208.5 1.4 copy-start.7
  209.9 5.0 %copy-start.8 = (f32[8,512,512]{2,1,0:T(8,128)}, f32[8,512,512]{2,1,0:T(8,128)S(1)}, u32[]{:S(2)}) copy-start(f32[8,512,512]{2,1,0:T(8,128)S(1)} %fusion.30) | copy-start | bytes 25165828
  214.9 2.0 copy-start.6
  218.2 9.1 %copy-start.5 = (f32[512,8,128]{0,2,1:T(8,128)S(1)}, f32[512,8,128]{0,2,1:T(8,128)}, u32[]{:S(2)}) copy-start(f32[512,8,128]{0,2,1:T(8,128)} %get-tuple-element.180) | copy-start | bytes 6291460
Sparse Core Ops, SparseCore 0:
  9.9 42.6 all-gather.2
  54.3 38.0 all-gather.4
  206.5 61.1 reduce-scatter.2
  270.1 61.1 reduce-scatter.4
where the time goes:
time: 341 us; the launch traced here: 339 us
  waiting for transfers between devices  171 us (50%)
  matrix products  85.5 us (25%)
  local copies, waits for them, and re-layouts  60.1 us (18%)
  between operations  14.6 us (4%)
  other arithmetic  7.82 us (2%)
    reduce_scatter x1, waiting for transfers between devices, local(): lax.psum_scatter(value_terms, 'ctx', scatter_dimension=0, tiled=True)  62 us
    all_gather x1, waiting for transfers between devices, local(): lax.all_gather(beacon_values, 'ctx', axis=0, tiled=True)  39.9 us
    all_gather x1, waiting for transfers between devices, local(): lax.all_gather(beacon_keys, 'ctx', axis=0, tiled=True)  34 us
    reduce_scatter x1, waiting for transfers between devices, local(): lax.psum_scatter(key_terms, 'ctx', scatter_dimension=0, tiled=True)  33.1 us
    dynamic_update_slice x12, local copies, waits for them, and re-layouts, sweep(): lax.scan(step, query_total, (key_blocks, value_blocks, starts))  27.7 us
    dynamic_slice x20, local copies, waits for them, and re-layouts, sweep(): lax.scan(step, query_total, (key_blocks, value_blocks, starts))  17 us
    dot_general x4, matrix products, beacon_block(): jnp.einsum('qhd,khd->hqk', grad_heads, value_heads, preferred_element_typ...  16.6 us
    dot_general x4, matrix products, beacon_block(): jnp.einsum('hqk,khd->qhd', dscores, key_heads, preferred_element_type=jnp...  14.3 us
  transfers between devices with their start and end apart: 4, of which 4 were waited for; matrix products, arithmetic and copies ran while one was open for 11% of the time, Pallas kernels for 0%

commit v1 on v0

v1 whole, which is shorter than its diff:
```python
import functools
import math

import jax
import jax.numpy as jnp
from jax import lax
from jax.experimental import pallas as pl
from jax.experimental.pallas import tpu as pltpu
from jax.sharding import PartitionSpec as P

HD = 128
GROUP = 512
BPC = 64
CHIPS = 8
SCALE = 1.0 / math.sqrt(HD)
LOG2E = math.log2(math.e)
HIDDEN = 1e30
BF = jnp.bfloat16
F32 = jnp.float32


def nt(a, b):
    return lax.dot_general(a, b, (((1,), (1,)), ((), ())), preferred_element_type=F32)


def nn(a, b):
    return lax.dot_general(a, b, (((1,), (0,)), ((), ())), preferred_element_type=F32)


def tn(a, b):
    return lax.dot_general(a, b, (((0,), (0,)), ((), ())), preferred_element_type=F32)


def raw_kernel(place, q_ref, k_ref, v_ref, g_ref, o_ref, ln_ref, dq_ref, dk_ref, dv_ref, st_ref):
    h = pl.program_id(0)
    q, k, v, g = q_ref[...], k_ref[...], v_ref[...], g_ref[...]
    prod = g.astype(F32) * o_ref[...].astype(F32)
    delta = jnp.sum(prod.T, axis=0, keepdims=True)
    ln = ln_ref[pl.ds(h, 1), :] * LOG2E
    st_ref[0, pl.ds(h, 1), :] = ln
    st_ref[1, pl.ds(h, 1), :] = delta
    st_ref[2, pl.ds(h, 1), :] = jnp.full((1, GROUP), place[2], jnp.int32).astype(F32)
    block = 128
    tri = lax.broadcasted_iota(jnp.int32, (block, block), 0) <= lax.broadcasted_iota(
        jnp.int32, (block, block), 1
    )
    stripes = []
    for lo in range(0, GROUP, block):
        hi = lo + block
        s = nt(k[lo:hi], q[lo:])
        p = jnp.exp2(s * (SCALE * LOG2E) - ln[:, lo:])
        head = jnp.where(tri, p[:, :block], 0.0)
        p = head if hi == GROUP else jnp.concatenate([head, p[:, block:]], axis=1)
        dp = nt(v[lo:hi], g[lo:])
        ds = (p * (dp - delta[:, lo:])).astype(BF)
        dv_ref[lo:hi, :] = nn(p.astype(BF), g[lo:]).astype(BF)
        dk_ref[lo:hi, :] = (nn(ds, q[lo:]) * SCALE).astype(BF)
        stripes.append(ds)
    for lo in range(0, GROUP, block):
        hi = lo + block
        parts = [stripe[:, lo - i * block : hi - i * block] for i, stripe in enumerate(stripes[: hi // block])]
        ds = parts[0] if len(parts) == 1 else jnp.concatenate(parts, axis=0)
        dq_ref[lo:hi, :] = tn(ds, k[:hi]) * SCALE


def raw_call(place, queries, keys, values, out_grad, forward_out, log_norm):
    heads = log_norm.shape[0]
    column = pl.BlockSpec((GROUP, HD), lambda h: (0, h))
    whole = pl.BlockSpec((heads, GROUP), lambda h: (0, 0))
    width = heads * HD
    return pl.pallas_call(
        raw_kernel,
        grid=(heads,),
        in_specs=[pl.BlockSpec(memory_space=pltpu.SMEM)] + [column] * 5 + [whole],
        out_specs=[column] * 3 + [pl.BlockSpec((3, heads, GROUP), lambda h: (0, 0, 0))],
        out_shape=[
            jax.ShapeDtypeStruct((GROUP, width), F32),
            jax.ShapeDtypeStruct((GROUP, width), BF),
            jax.ShapeDtypeStruct((GROUP, width), BF),
            jax.ShapeDtypeStruct((3, heads, GROUP), F32),
        ],
        compiler_params=pltpu.CompilerParams(vmem_limit_bytes=48 << 20),
        cost_estimate=pl.CostEstimate(
            flops=10 * heads * GROUP * GROUP * HD, bytes_accessed=10 << 20, transcendentals=heads * GROUP * GROUP
        ),
        name="raw_tokens",
    )(place, queries, keys, values, out_grad, forward_out, log_norm)


def beacon_kernel(step, count, place, qh_ref, qp_ref, gh_ref, gp_ref, sh_ref, sp_ref, *refs):
    pieces, outs, ds_ref = refs[:count], refs[count : 2 * count], refs[2 * count]
    h = pl.program_id(0)
    z, core = place[0], place[1]
    chunk = jnp.where(core == 0, z - step, z + step - CHIPS) if step else z
    valid = (chunk >= 0) & ((core == 0) | (step < CHIPS // 2))
    owners = [2 * chunk + core, 2 * chunk + 1 - core][:count]

    def work():
        kk = pieces[0][0] if count == 1 else jnp.concatenate([ref[0] for ref in pieces], axis=0)
        vv = pieces[0][1] if count == 1 else jnp.concatenate([ref[1] for ref in pieces], axis=0)
        dk = dv = None
        for side, (q_ref, g_ref, st_ref, group) in enumerate(
            ((qh_ref, gh_ref, sh_ref, 2 * z + core), (qp_ref, gp_ref, sp_ref, 2 * z + 1 - core))
        ):
            q, g = q_ref[...], g_ref[...]
            ln, delta = st_ref[0, pl.ds(h, 1), :], st_ref[1, pl.ds(h, 1), :]
            reach = st_ref[2, pl.ds(h, 1), :]
            rows = []
            for owner in owners:
                far = jnp.where(owner <= group, group - owner, 2 * CHIPS)
                row = jnp.where(reach > jnp.full((1, GROUP), far, jnp.int32).astype(F32), ln, HIDDEN)
                rows.append(jnp.broadcast_to(row, (BPC, GROUP)))
            bias = rows[0] if count == 1 else jnp.concatenate(rows, axis=0)
            p = jnp.exp2(nt(kk, q) * (SCALE * LOG2E) - bias)
            ds = (p * (nt(vv, g) - delta)).astype(BF)
            ds_ref[0, :, side * GROUP : (side + 1) * GROUP] = ds
            dv_part, dk_part = nn(p.astype(BF), g), nn(ds, q)
            dk, dv = (dk_part, dv_part) if dk is None else (dk + dk_part, dv + dv_part)
        dk = dk * SCALE
        for i, ref in enumerate(outs):
            ref[0] = dk[i * BPC : (i + 1) * BPC].astype(ref.dtype)
            ref[1] = dv[i * BPC : (i + 1) * BPC].astype(ref.dtype)

    if step == 0:
        work()
        return
    pl.when(valid)(work)

    @pl.when(jnp.logical_not(valid))
    def _():
        for ref in outs:
            ref[...] = jnp.zeros_like(ref)
        ds_ref[...] = jnp.zeros_like(ds_ref)


def beacon_call(step, place, sides, pieces, kind):
    heads = sides[4].shape[1]
    count = len(pieces)
    column = pl.BlockSpec((GROUP, HD), lambda h: (0, h))
    stats = pl.BlockSpec((3, heads, GROUP), lambda h: (0, 0, 0))
    piece = pl.BlockSpec((2, BPC, HD), lambda h: (0, 0, h))
    items = heads * 2 * GROUP * count * BPC
    return pl.pallas_call(
        functools.partial(beacon_kernel, step, count),
        grid=(heads,),
        in_specs=[pl.BlockSpec(memory_space=pltpu.SMEM)] + [column] * 4 + [stats] * 2 + [piece] * count,
        out_specs=[piece] * count + [pl.BlockSpec((1, count * BPC, 2 * GROUP), lambda h: (h, 0, 0))],
        out_shape=[jax.ShapeDtypeStruct((2, BPC, heads * HD), kind)] * count
        + [jax.ShapeDtypeStruct((heads, count * BPC, 2 * GROUP), BF)],
        compiler_params=pltpu.CompilerParams(vmem_limit_bytes=48 << 20),
        cost_estimate=pl.CostEstimate(flops=8 * items * HD, bytes_accessed=8 << 20, transcendentals=items),
        name="beacon_step" + str(step),
    )(place, *sides, *pieces)


def query_kernel(steps, raw_ref, *refs):
    ds_refs, k_refs, (home_ref, other_ref) = refs[:steps], refs[steps:-2], refs[-2:]
    kk = jnp.concatenate([ref[0] for ref in k_refs], axis=0)
    home = jnp.concatenate([ref[0, :, :GROUP] for ref in ds_refs], axis=0)
    home_ref[...] = raw_ref[...] + tn(home, kk) * SCALE
    other = jnp.concatenate([ref[0, :, GROUP:] for ref in ds_refs], axis=0)
    other_ref[...] = tn(other, kk) * SCALE


def query_call(raw, ds_list, pieces):
    heads = ds_list[0].shape[0]
    column = pl.BlockSpec((GROUP, HD), lambda h: (0, h))
    piece = pl.BlockSpec((1, BPC, HD), lambda h: (0, 0, h))
    rows = sum(ds.shape[1] for ds in ds_list)
    return pl.pallas_call(
        functools.partial(query_kernel, len(ds_list)),
        grid=(heads,),
        in_specs=[column]
        + [pl.BlockSpec((1, ds.shape[1], 2 * GROUP), lambda h: (h, 0, 0)) for ds in ds_list]
        + [piece] * len(pieces),
        out_specs=[column] * 2,
        out_shape=[jax.ShapeDtypeStruct((GROUP, heads * HD), F32)] * 2,
        compiler_params=pltpu.CompilerParams(vmem_limit_bytes=48 << 20),
        cost_estimate=pl.CostEstimate(
            flops=2 * heads * rows * 2 * GROUP * HD, bytes_accessed=16 << 20, transcendentals=0
        ),
        name="query_grad",
    )(raw, *ds_list, *pieces)


def at(z, core):
    return 2 * (z % CHIPS) + core


SWAP = [(at(z, core), at(z, 1 - core)) for z in range(CHIPS) for core in (0, 1)]


def gather_pairs(cross):
    pairs = []
    for z in range(CHIPS):
        pairs.append((at(z, 1 if cross else 0), at(z + 1, 0)))
        pairs.append((at(z, 0 if cross else 1), at(z - 1, 1)))
    return pairs


def reduce_pairs(cross):
    pairs = []
    for z in range(CHIPS):
        pairs.append((at(z, 0), at(z - 1, 1 if cross else 0)))
        pairs.append((at(z, 1), at(z + 1, 0 if cross else 1)))
    return pairs


def local(
    queries, keys, values, out_grad, forward_out, log_norm, beacon_keys, beacon_values, beacon_reach
):
    ctx = lax.axis_index("ctx").astype(jnp.int32)
    place = jnp.stack([ctx // 2, ctx % 2, beacon_reach[0].astype(jnp.int32)])
    own = jnp.stack([beacon_keys, beacon_values])
    hops = [
        (lax.ppermute(own, "ctx", gather_pairs(False)), lax.ppermute(own, "ctx", gather_pairs(True)))
    ]
    queries_other = lax.ppermute(queries, "ctx", SWAP)
    grad_other = lax.ppermute(out_grad, "ctx", SWAP)
    dq_raw, key_grad, value_grad, stats = raw_call(
        place, queries, keys, values, out_grad, forward_out, log_norm
    )
    stats_other = lax.ppermute(stats, "ctx", SWAP)
    sides = (queries, queries_other, out_grad, grad_other, stats, stats_other)
    for _ in range(CHIPS // 2 - 1):
        hops.append(tuple(lax.ppermute(piece, "ctx", gather_pairs(False)) for piece in hops[-1]))
    own_term, own_ds = beacon_call(0, place, sides, (own,), F32)
    terms, ds_list, pieces = [], [own_ds], [own]
    for step, arrived in enumerate(hops, 1):
        kind = BF if step == len(hops) else F32
        term_a, term_b, ds = beacon_call(step, place, sides, arrived, kind)
        terms.append((term_a, term_b))
        ds_list.append(ds)
        pieces.extend(arrived)
    carried = terms[-1]
    for hop in range(len(hops) - 1, 0, -1):
        carried = tuple(lax.ppermute(piece, "ctx", reduce_pairs(False)) for piece in carried)
        carried = tuple(
            (piece.astype(F32) + term).astype(BF) for piece, term in zip(carried, terms[hop - 1], strict=True)
        )
    end_a = lax.ppermute(carried[0], "ctx", reduce_pairs(False))
    end_b = lax.ppermute(carried[1], "ctx", reduce_pairs(True))
    total = (own_term + (end_a.astype(F32) + end_b.astype(F32))).astype(BF)
    dq_home, dq_other = query_call(dq_raw, ds_list, pieces)
    query_grad = (dq_home + lax.ppermute(dq_other, "ctx", SWAP)).astype(BF)
    return query_grad, key_grad, value_grad, total[0], total[1]


def solution(mesh):
    tokens = P(("dp", "ctx"), "head")
    in_specs = (tokens,) * 5 + (P("head", ("dp", "ctx")), tokens, tokens, P(("dp", "ctx")))
    return jax.shard_map(local, mesh=mesh, in_specs=in_specs, out_specs=(tokens,) * 5, check_vma=False)
```

time: 341 us -> 124 us (0.36)
  waiting for transfers between devices: 171 us -> 32 us
  matrix products: 85.5 us -> 0 us
  local copies, waits for them, and re-layouts: 60.1 us -> 7.56 us
  Pallas kernels: 0 us -> 44.9 us
  starting transfers between devices: 0.34 us -> 33.9 us
  between operations: 14.6 us -> 1.41 us
  other arithmetic: 7.82 us -> 2.77 us
    reduce_scatter x2 -> x0, waiting for transfers between devices: 95.1 us -> none  [the longest x1 62 us: local(): lax.psum_scatter(value_terms, 'ctx', scatter_dimension=0, tiled=True)]
    dot_general x25 -> x0, matrix products: 85.5 us -> none  [the longest x4 16.6 us: beacon_block(): jnp.einsum('qhd,khd->hqk', grad_heads, value_heads, preferred_element_typ...]
    all_gather x2 -> x0, waiting for transfers between devices: 73.9 us -> none  [the longest x1 39.9 us: local(): lax.all_gather(beacon_values, 'ctx', axis=0, tiled=True)]
    pallas_call x0 -> x7, Pallas kernels: none -> 44.9 us  [the longest x5 24.4 us: beacon_call(): pl.pallas_call(functools.partial(beacon_kernel, step, count), grid=(heads...]
    ppermute x0 -> x20, starting transfers between devices: none -> 33.9 us  [the longest x6 23.2 us: local(): lax.ppermute(piece, 'ctx', reduce_pairs(False))]
    ppermute x0 -> x20, waiting for transfers between devices: none -> 32 us  [the longest x6 16 us: local(): lax.ppermute(piece, 'ctx', gather_pairs(False))]
    dynamic_update_slice x12 -> x0, local copies, waits for them, and re-layouts: 27.7 us -> none  [sweep(): lax.scan(step, query_total, (key_blocks, value_blocks, starts))]
    dynamic_slice x20 -> x0, local copies, waits for them, and re-layouts: 17 us -> none  [sweep(): lax.scan(step, query_total, (key_blocks, value_blocks, starts))]
  transfers between devices with their start and end apart: 4 -> 20, of which waited for: 4 -> 11; matrix products, arithmetic and copies ran while one was open for 11% -> 1% of each run, Pallas kernels for 0% -> 33%
where the time goes in v1:
time: 124 us; the launch traced here: 123 us
  Pallas kernels  44.9 us (36%)
  starting transfers between devices  33.9 us (27%)
  waiting for transfers between devices  32 us (26%)
  local copies, waits for them, and re-layouts  7.56 us (6%)
  other arithmetic  2.77 us (2%)
  between operations  1.41 us (1%)
    pallas_call x5, Pallas kernels, beacon_call(): pl.pallas_call(functools.partial(beacon_kernel, step, count), grid=(heads...  24.4 us
    ppermute x6, starting transfers between devices, local(): lax.ppermute(piece, 'ctx', reduce_pairs(False))  23.2 us
    ppermute x6, waiting for transfers between devices, local(): lax.ppermute(piece, 'ctx', gather_pairs(False))  16 us
    pallas_call x1, Pallas kernels, raw_call(): pl.pallas_call(raw_kernel, grid=(heads,), in_specs=[pl.BlockSpec(memory_s...  11.1 us
    pallas_call x1, Pallas kernels, query_call(): pl.pallas_call(functools.partial(query_kernel, len(ds_list)), grid=(heads...  9.37 us
    unnamed x14, local copies, waits for them, and re-layouts  6.84 us
    ppermute x1, waiting for transfers between devices, local(): lax.ppermute(own, 'ctx', gather_pairs(True))  5.7 us
    ppermute x1, starting transfers between devices, local(): lax.ppermute(own, 'ctx', gather_pairs(True))  5.38 us
  transfers between devices with their start and end apart: 20, of which 11 were waited for; matrix products, arithmetic and copies ran while one was open for 1% of the time, Pallas kernels for 33%

profile of v1, /device:TPU:6, one launch (start us, length us, event | category | flops | bytes accessed | tf_op | source)
XLA Modules:
  0.0 122.5 jit_solution(712324361030638814)
XLA Ops:
  0.6 1.0 pad_maximum_fusion.refs_0_.refs_5_
  1.6 5.4 %collective-permute-start.4 = (bf16[2,64,1024]{2,1,0:T(8,128)(2,1)S(1)}, bf16[2,64,1024]{2,1,0:T(8,128)(2,1)S(1)}, u32[]{:S(2)}, u32[]{:S(2)}) collective-permute-start(bf16[2,64,1024]{2,1,0:T(8,128)(2,1)S(1)} %pad_maximum_fusion.refs_0_.refs_5_), channel_id=1, source_target_pairs={{16,32},{0,240},{48,64},{32,16},{80,96},{64,48},{112,128},{96,80},... | collective-permute-start | bytes 786440 | tf_op jit(solution)/shard_map/ppermute | solution.py:216
  7.0 0.0 collective-permute-start.3
  7.0 0.2 collective-permute-start
  7.2 0.3 collective-permute-start.1
  7.5 5.7 %collective-permute-done.4.refs_1_.refs_7_ = bf16[2,64,1024]{2,1,0:T(8,128)(2,1)S(1)} collective-permute-done((bf16[2,64,1024]{2,1,0:T(8,128)(2,1)S(1)}, bf16[2,64,1024]{2,1,0:T(8,128)(2,1)S(1)}, u32[]{:S(2)}, u32[]{:S(2)}) %collective-permute-start.4) | collective-permute-done | bytes 262176 | tf_op jit(solution)/shard_map/ppermute | solution.py:216
  13.2 0.0 collective-permute-start.6
  13.2 1.4 %collective-permute-done.3.refs_0_.refs_6_ = bf16[2,64,1024]{2,1,0:T(8,128)(2,1)S(1)} collective-permute-done((bf16[2,64,1024]{2,1,0:T(8,128)(2,1)S(1)}, bf16[2,64,1024]{2,1,0:T(8,128)(2,1)S(1)}, u32[]{:S(2)}, u32[]{:S(2)}) %collective-permute-start.3) | collective-permute-done | bytes 262176 | tf_op jit(solution)/shard_map/ppermute | solution.py:216
  14.6 0.0 collective-permute-start.5
  14.6 6.2 %collective-permute-done.6.refs_1_.refs_9_ = bf16[2,64,1024]{2,1,0:T(8,128)(2,1)S(1)} collective-permute-done((bf16[2,64,1024]{2,1,0:T(8,128)(2,1)S(1)}, bf16[2,64,1024]{2,1,0:T(8,128)(2,1)S(1)}, u32[]{:S(2)}, u32[]{:S(2)}) %collective-permute-start.6) | collective-permute-done | bytes 262176 | tf_op jit(solution)/shard_map/ppermute | solution.py:226
  20.8 0.0 collective-permute-start.8
  20.8 2.8 %collective-permute-done.5.refs_0_.refs_8_ = bf16[2,64,1024]{2,1,0:T(8,128)(2,1)S(1)} collective-permute-done((bf16[2,64,1024]{2,1,0:T(8,128)(2,1)S(1)}, bf16[2,64,1024]{2,1,0:T(8,128)(2,1)S(1)}, u32[]{:S(2)}, u32[]{:S(2)}) %collective-permute-start.5) | collective-permute-done | bytes 262176 | tf_op jit(solution)/shard_map/ppermute | solution.py:226
  23.6 0.0 collective-permute-start.7
  24.3 0.1 pad_add_fusion.place
  24.4 4.1 %collective-permute-done.8.refs_1_.refs_11_ = bf16[2,64,1024]{2,1,0:T(8,128)(2,1)} collective-permute-done((bf16[2,64,1024]{2,1,0:T(8,128)(2,1)S(1)}, bf16[2,64,1024]{2,1,0:T(8,128)(2,1)}, u32[]{:S(2)}, u32[]{:S(2)}) %collective-permute-start.8) | collective-permute-done | bytes 262176 | tf_op jit(solution)/shard_map/ppermute | solution.py:226
  28.5 0.0 collective-permute-start.10
  28.5 2.8 %collective-permute-done.7.refs_0_.refs_10_ = bf16[2,64,1024]{2,1,0:T(8,128)(2,1)} collective-permute-done((bf16[2,64,1024]{2,1,0:T(8,128)(2,1)S(1)}, bf16[2,64,1024]{2,1,0:T(8,128)(2,1)}, u32[]{:S(2)}, u32[]{:S(2)}) %collective-permute-start.7) | collective-permute-done | bytes 262176 | tf_op jit(solution)/shard_map/ppermute | solution.py:226
  31.3 0.0 collective-permute-start.9
  31.3 1.2 copy-done
  32.5 1.2 copy-done.1
  33.8 1.2 copy-done.3
  35.0 1.2 copy-done.4
  36.2 1.2 copy-done.5
  37.4 0.7 copy-done.6
  38.2 11.1 %raw_tokens.1 = (f32[512,1024]{1,0:T(8,128)}, bf16[512,1024]{1,0:T(8,128)(2,1)}, bf16[512,1024]{1,0:T(8,128)(2,1)}, f32[3,8,512]{2,1,0:T(8,128)S(1)}) custom-call(s32[3]{0:T(128)S(1)} %pad_add_fusion.place, bf16[512,1024]{1,0:T(8,128)(2,1)S(1)} %copy-done, bf16[512,1024]{1,0:T(8,128)(2,1)S(1)} %copy-done.3, bf16[512,1024]{1,0:T(8,128)(2,1)S(1)} %copy-done.4, ...), custom_call_target="tpu_custom_call" | custom-call | flops 2684354560 | bytes 10485760 | tf_op jit(solution)/shard_map/raw_tokens/pallas_call | solution.py:71
  49.2 0.9 collective-permute-start.2
  50.2 0.9 collective-permute-done.2.sp_ref
  51.1 0.0 collective-permute-done.10.refs_1_.refs_13_
  51.1 0.0 collective-permute-done.9.refs_0_.refs_12_
  51.1 0.0 collective-permute-done.qp_ref
  51.1 0.0 collective-permute-done.1.gp_ref
  51.1 4.5 %beacon_step4.1 = (bf16[2,64,1024]{2,1,0:T(8,128)(2,1)S(1)}, bf16[2,64,1024]{2,1,0:T(8,128)(2,1)S(1)}, bf16[8,128,1024]{2,1,0:T(8,128)(2,1)}) custom-call(s32[3]{0:T(128)S(1)} %pad_add_fusion.place, bf16[512,1024]{1,0:T(8,128)(2,1)S(1)} %copy-done, bf16[512,1024]{1,0:T(8,128)(2,1)S(1)} %collective-permute-done.qp_ref, bf16[512,1024]{1,0:T(8,128)(2,1)S(1)} %copy-done.2, ...), custom_call_target="tpu_custom_call" | custom-call | flops 1073741824 | bytes 8388608 | tf_op jit(solution)/shard_map/beacon_step4/pallas_call | solution.py:143
  55.6 5.3 %collective-permute-start.12 = (bf16[2,64,1024]{2,1,0:T(8,128)(2,1)S(1)}, bf16[2,64,1024]{2,1,0:T(8,128)(2,1)S(1)}, u32[]{:S(2)}, u32[]{:S(2)}) collective-permute-start(bf16[2,64,1024]{2,1,0:T(8,128)(2,1)S(1)} %get-tuple-element.37), channel_id=1, source_target_pairs={{0,224},{16,48},{32,0},{48,80},{64,32},{80,112},{96,64},{112,144},... | collective-permute-start | bytes 786440 | tf_op jit(solution)/shard_map/ppermute | solution.py:237
  60.9 0.0 collective-permute-start.16
  60.9 5.4 %beacon_step3.1 = (f32[2,64,1024]{2,1,0:T(8,128)S(1)}, f32[2,64,1024]{2,1,0:T(8,128)S(1)}, bf16[8,128,1024]{2,1,0:T(8,128)(2,1)}) custom-call(s32[3]{0:T(128)S(1)} %pad_add_fusion.place, bf16[512,1024]{1,0:T(8,128)(2,1)S(1)} %copy-done, bf16[512,1024]{1,0:T(8,128)(2,1)S(1)} %collective-permute-done.qp_ref, bf16[512,1024]{1,0:T(8,128)(2,1)S(1)} %copy-done.2, ...), custom_call_target="tpu_custom_call" | custom-call | flops 1073741824 | bytes 8388608 | tf_op jit(solution)/shard_map/beacon_step3/pallas_call | solution.py:143
  66.4 4.5 %beacon_step2.1 = (f32[2,64,1024]{2,1,0:T(8,128)S(1)}, f32[2,64,1024]{2,1,0:T(8,128)S(1)}, bf16[8,128,1024]{2,1,0:T(8,128)(2,1)}) custom-call(s32[3]{0:T(128)S(1)} %pad_add_fusion.place, bf16[512,1024]{1,0:T(8,128)(2,1)S(1)} %copy-done, bf16[512,1024]{1,0:T(8,128)(2,1)S(1)} %collective-permute-done.qp_ref, bf16[512,1024]{1,0:T(8,128)(2,1)S(1)} %copy-done.2, ...), custom_call_target="tpu_custom_call" | custom-call | flops 1073741824 | bytes 8388608 | tf_op jit(solution)/shard_map/beacon_step2/pallas_call | solution.py:143
  70.8 5.6 %beacon_step0.1 = (f32[2,64,1024]{2,1,0:T(8,128)S(1)}, bf16[8,64,1024]{2,1,0:T(8,128)(2,1)S(1)}) custom-call(s32[3]{0:T(128)S(1)} %pad_add_fusion.place, bf16[512,1024]{1,0:T(8,128)(2,1)S(1)} %copy-done, bf16[512,1024]{1,0:T(8,128)(2,1)S(1)} %collective-permute-done.qp_ref, bf16[512,1024]{1,0:T(8,128)(2,1)S(1)} %copy-done.2, ...), custom_call_target="tpu_custom_call" | custom-call | flops 536870912 | bytes 8388608 | tf_op jit(solution)/shard_map/beacon_step0/pallas_call | solution.py:143
  76.4 4.5 %beacon_step1.1 = (f32[2,64,1024]{2,1,0:T(8,128)S(1)}, f32[2,64,1024]{2,1,0:T(8,128)S(1)}, bf16[8,128,1024]{2,1,0:T(8,128)(2,1)}) custom-call(s32[3]{0:T(128)S(1)} %pad_add_fusion.place, bf16[512,1024]{1,0:T(8,128)(2,1)S(1)} %copy-done, bf16[512,1024]{1,0:T(8,128)(2,1)S(1)} %collective-permute-done.qp_ref, bf16[512,1024]{1,0:T(8,128)(2,1)S(1)} %copy-done.2, ...), custom_call_target="tpu_custom_call" | custom-call | flops 1073741824 | bytes 8388608 | tf_op jit(solution)/shard_map/beacon_step1/pallas_call | solution.py:143
  80.9 9.4 %query_grad.1 = (f32[512,1024]{1,0:T(8,128)S(1)}, f32[512,1024]{1,0:T(8,128)}) custom-call(f32[512,1024]{1,0:T(8,128)} %get-tuple-element.25.raw_ref, bf16[8,64,1024]{2,1,0:T(8,128)(2,1)S(1)} %get-tuple-element.27.refs_0_, bf16[8,128,1024]{2,1,0:T(8,128)(2,1)} %get-tuple-element.28.refs_1_, bf16[8,128,1024]{2,1,0:T(8,128)(2,1)} %get-tuple-element.29.refs_2_, ...), custom_call_target="tpu_custom_call" | custom-call | flops 1207959552 | bytes 16777216 | tf_op jit(solution)/shard_map/query_grad/pallas_call | solution.py:170
  90.3 0.0 collective-permute-start.11
  90.3 0.0 collective-permute-done.12
  90.3 0.1 add_convert_fusion.7
  90.3 7.5 %collective-permute-start.13 = (bf16[2,64,1024]{2,1,0:T(8,128)(2,1)S(1)}, bf16[2,64,1024]{2,1,0:T(8,128)(2,1)S(1)}, u32[]{:S(2)}, u32[]{:S(2)}) collective-permute-start(bf16[2,64,1024]{2,1,0:T(8,128)(2,1)S(1)} %add_convert_fusion.7), channel_id=1, source_target_pairs={{0,224},{16,48},{32,0},{48,80},{64,32},{80,112},{96,64},{112,144},... | collective-permute-start | bytes 786440 | tf_op jit(solution)/shard_map/ppermute | solution.py:237
  97.8 0.0 collective-permute-done.16
  97.8 0.1 add_convert_fusion.4
  97.9 3.3 %collective-permute-start.17 = (bf16[2,64,1024]{2,1,0:T(8,128)(2,1)S(1)}, bf16[2,64,1024]{2,1,0:T(8,128)(2,1)S(1)}, u32[]{:S(2)}, u32[]{:S(2)}) collective-permute-start(bf16[2,64,1024]{2,1,0:T(8,128)(2,1)S(1)} %add_convert_fusion.4), channel_id=1, source_target_pairs={{0,224},{16,48},{32,0},{48,80},{64,32},{80,112},{96,64},{112,144},... | collective-permute-start | bytes 786440 | tf_op jit(solution)/shard_map/ppermute | solution.py:237
  101.2 0.5 collective-permute-done.13
  101.7 0.1 add_convert_fusion.6
  101.8 3.8 %collective-permute-start.14 = (bf16[2,64,1024]{2,1,0:T(8,128)(2,1)S(1)}, bf16[2,64,1024]{2,1,0:T(8,128)(2,1)S(1)}, u32[]{:S(2)}, u32[]{:S(2)}) collective-permute-start(bf16[2,64,1024]{2,1,0:T(8,128)(2,1)S(1)} %add_convert_fusion.6), channel_id=1, source_target_pairs={{0,224},{16,48},{32,0},{48,80},{64,32},{80,112},{96,64},{112,144},... | collective-permute-start | bytes 786440 | tf_op jit(solution)/shard_map/ppermute | solution.py:237
  105.5 0.0 collective-permute-done.17
  105.5 0.1 add_convert_fusion.3
  105.6 3.3 %collective-permute-start.18 = (bf16[2,64,1024]{2,1,0:T(8,128)(2,1)S(1)}, bf16[2,64,1024]{2,1,0:T(8,128)(2,1)S(1)}, u32[]{:S(2)}, u32[]{:S(2)}) collective-permute-start(bf16[2,64,1024]{2,1,0:T(8,128)(2,1)S(1)} %add_convert_fusion.3), channel_id=1, source_target_pairs={{0,224},{16,48},{32,0},{48,80},{64,32},{80,112},{96,64},{112,144},... | collective-permute-start | bytes 786440 | tf_op jit(solution)/shard_map/ppermute | solution.py:237
  108.9 0.5 collective-permute-done.14
  109.4 0.1 add_convert_fusion.5
  109.5 3.8 %collective-permute-start.15 = (bf16[2,64,1024]{2,1,0:T(8,128)(2,1)S(1)}, bf16[2,64,1024]{2,1,0:T(8,128)(2,1)S(1)}, u32[]{:S(2)}, u32[]{:S(2)}) collective-permute-start(bf16[2,64,1024]{2,1,0:T(8,128)(2,1)S(1)} %add_convert_fusion.5), channel_id=1, source_target_pairs={{0,224},{16,48},{32,0},{48,80},{64,32},{80,112},{96,64},{112,144},... | collective-permute-start | bytes 786440 | tf_op jit(solution)/shard_map/ppermute | solution.py:241
  113.3 0.0 collective-permute-done.18
  113.3 0.1 add_convert_fusion.2
  113.3 0.1 collective-permute-start.19
  113.4 3.7 %collective-permute-done.15 = bf16[2,64,1024]{2,1,0:T(8,128)(2,1)S(1)} collective-permute-done((bf16[2,64,1024]{2,1,0:T(8,128)(2,1)S(1)}, bf16[2,64,1024]{2,1,0:T(8,128)(2,1)S(1)}, u32[]{:S(2)}, u32[]{:S(2)}) %collective-permute-start.15) | collective-permute-done | bytes 262176 | tf_op jit(solution)/shard_map/ppermute | solution.py:241
  117.1 3.3 %collective-permute-done.19 = bf16[2,64,1024]{2,1,0:T(8,128)(2,1)S(1)} collective-permute-done((bf16[2,64,1024]{2,1,0:T(8,128)(2,1)S(1)}, bf16[2,64,1024]{2,1,0:T(8,128)(2,1)S(1)}, u32[]{:S(2)}, u32[]{:S(2)}) %collective-permute-start.19) | collective-permute-done | bytes 262176 | tf_op jit(solution)/shard_map/ppermute | solution.py:242
  120.4 0.1 add_convert_fusion.1
  120.5 0.7 slice_bitcast_fusion
  121.3 0.0 collective-permute-done.11
  121.3 1.3 %add_convert_fusion = bf16[512,1024]{1,0:T(8,128)(2,1)} fusion(f32[512,1024]{1,0:T(8,128)S(1)} %get-tuple-element.32, f32[512,1024]{1,0:T(8,128)S(1)} %collective-permute-done.11), kind=kLoop, calls=%fused_computation | loop fusion | flops 1048576 | bytes 5242880 | tf_op jit(solution)/shard_map/convert_element_type | solution.py:245
  (8 shorter events, 0.0 us)
Async XLA Ops:
  1.6 11.6 %collective-permute-start.4 = (bf16[2,64,1024]{2,1,0:T(8,128)(2,1)S(1)}, bf16[2,64,1024]{2,1,0:T(8,128)(2,1)S(1)}, u32[]{:S(2)}, u32[]{:S(2)}) collective-permute-start(bf16[2,64,1024]{2,1,0:T(8,128)(2,1)S(1)} %pad_maximum_fusion.refs_0_.refs_5_), channel_id=1, source_target_pairs={{16,32},{0,240},{48,64},{32,16},{80,96},{64,48},{112,128},{96,80},... | collective-permute-start | bytes 786440 | tf_op jit(solution)/shard_map/ppermute | solution.py:216
  7.0 7.6 %collective-permute-start.3 = (bf16[2,64,1024]{2,1,0:T(8,128)(2,1)S(1)}, bf16[2,64,1024]{2,1,0:T(8,128)(2,1)S(1)}, u32[]{:S(2)}, u32[]{:S(2)}) collective-permute-start(bf16[2,64,1024]{2,1,0:T(8,128)(2,1)S(1)} %pad_maximum_fusion.refs_0_.refs_5_), channel_id=1, source_target_pairs={{0,32},{16,240},{32,64},{48,16},{64,96},{80,48},{96,128},{112,80},... | collective-permute-start | bytes 786440 | tf_op jit(solution)/shard_map/ppermute | solution.py:216
  7.0 44.1 %collective-permute-start = (bf16[512,1024]{1,0:T(8,128)(2,1)}, bf16[512,1024]{1,0:T(8,128)(2,1)S(1)}, u32[]{:S(2)}, u32[]{:S(2)}) collective-permute-start(bf16[512,1024]{1,0:T(8,128)(2,1)} %qh_ref.9), channel_id=1, source_target_pairs={{0,16},{16,0},{32,48},{48,32},{64,80},{80,64},{96,112},{112,96},{1... | collective-permute-start | bytes 3145736 | tf_op jit(solution)/shard_map/ppermute | solution.py:218
  7.2 43.9 %collective-permute-start.1 = (bf16[512,1024]{1,0:T(8,128)(2,1)}, bf16[512,1024]{1,0:T(8,128)(2,1)S(1)}, u32[]{:S(2)}, u32[]{:S(2)}) collective-permute-start(bf16[512,1024]{1,0:T(8,128)(2,1)} %gh_ref.9), channel_id=1, source_target_pairs={{0,16},{16,0},{32,48},{48,32},{64,80},{80,64},{96,112},{112,96},{1... | collective-permute-start | bytes 3145736 | tf_op jit(solution)/shard_map/ppermute | solution.py:219
  13.2 7.6 %collective-permute-start.6 = (bf16[2,64,1024]{2,1,0:T(8,128)(2,1)S(1)}, bf16[2,64,1024]{2,1,0:T(8,128)(2,1)S(1)}, u32[]{:S(2)}, u32[]{:S(2)}) collective-permute-start(bf16[2,64,1024]{2,1,0:T(8,128)(2,1)S(1)} %collective-permute-done.4.refs_1_.refs_7_), channel_id=1, source_target_pairs={{0,32},{16,240},{32,64},{48,16},{64,96},{80,48},{96,128},{112,80},... | collective-permute-start | bytes 786440 | tf_op jit(solution)/shard_map/ppermute | solution.py:226
  14.6 9.0 %collective-permute-start.5 = (bf16[2,64,1024]{2,1,0:T(8,128)(2,1)S(1)}, bf16[2,64,1024]{2,1,0:T(8,128)(2,1)S(1)}, u32[]{:S(2)}, u32[]{:S(2)}) collective-permute-start(bf16[2,64,1024]{2,1,0:T(8,128)(2,1)S(1)} %collective-permute-done.3.refs_0_.refs_6_), channel_id=1, source_target_pairs={{0,32},{16,240},{32,64},{48,16},{64,96},{80,48},{96,128},{112,80},... | collective-permute-start | bytes 786440 | tf_op jit(solution)/shard_map/ppermute | solution.py:226
  20.8 7.7 %collective-permute-start.8 = (bf16[2,64,1024]{2,1,0:T(8,128)(2,1)S(1)}, bf16[2,64,1024]{2,1,0:T(8,128)(2,1)}, u32[]{:S(2)}, u32[]{:S(2)}) collective-permute-start(bf16[2,64,1024]{2,1,0:T(8,128)(2,1)S(1)} %collective-permute-done.6.refs_1_.refs_9_), channel_id=1, source_target_pairs={{0,32},{16,240},{32,64},{48,16},{64,96},{80,48},{96,128},{112,80},... | collective-permute-start | bytes 786440 | tf_op jit(solution)/shard_map/ppermute | solution.py:226
  23.6 7.7 %collective-permute-start.7 = (bf16[2,64,1024]{2,1,0:T(8,128)(2,1)S(1)}, bf16[2,64,1024]{2,1,0:T(8,128)(2,1)}, u32[]{:S(2)}, u32[]{:S(2)}) collective-permute-start(bf16[2,64,1024]{2,1,0:T(8,128)(2,1)S(1)} %collective-permute-done.5.refs_0_.refs_8_), channel_id=1, source_target_pairs={{0,32},{16,240},{32,64},{48,16},{64,96},{80,48},{96,128},{112,80},... | collective-permute-start | bytes 786440 | tf_op jit(solution)/shard_map/ppermute | solution.py:226
  28.5 22.6 %collective-permute-start.10 = (bf16[2,64,1024]{2,1,0:T(8,128)(2,1)}, bf16[2,64,1024]{2,1,0:T(8,128)(2,1)S(1)}, u32[]{:S(2)}, u32[]{:S(2)}) collective-permute-start(bf16[2,64,1024]{2,1,0:T(8,128)(2,1)} %collective-permute-done.8.refs_1_.refs_11_), channel_id=1, source_target_pairs={{0,32},{16,240},{32,64},{48,16},{64,96},{80,48},{96,128},{112,80},... | collective-permute-start | bytes 786440 | tf_op jit(solution)/shard_map/ppermute | solution.py:226
  31.3 19.8 %collective-permute-start.9 = (bf16[2,64,1024]{2,1,0:T(8,128)(2,1)}, bf16[2,64,1024]{2,1,0:T(8,128)(2,1)S(1)}, u32[]{:S(2)}, u32[]{:S(2)}) collective-permute-start(bf16[2,64,1024]{2,1,0:T(8,128)(2,1)} %collective-permute-done.7.refs_0_.refs_10_), channel_id=1, source_target_pairs={{0,32},{16,240},{32,64},{48,16},{64,96},{80,48},{96,128},{112,80},... | collective-permute-start | bytes 786440 | tf_op jit(solution)/shard_map/ppermute | solution.py:226
  31.3 1.2 %copy-start = (bf16[512,1024]{1,0:T(8,128)(2,1)S(1)}, bf16[512,1024]{1,0:T(8,128)(2,1)}, u32[]{:S(2)}) copy-start(bf16[512,1024]{1,0:T(8,128)(2,1)} %qh_ref.9) | copy-start | bytes 3145732
  32.5 1.2 copy-start.1
  33.8 1.2 copy-start.3
  35.0 1.2 copy-start.4
  36.2 1.2 copy-start.5
  37.4 0.7 copy-start.6
  38.2 12.9 %copy-start.2 = (bf16[512,1024]{1,0:T(8,128)(2,1)S(1)}, bf16[512,1024]{1,0:T(8,128)(2,1)}, u32[]{:S(2)}) copy-start(bf16[512,1024]{1,0:T(8,128)(2,1)} %gh_ref.9) | copy-start | bytes 3145732
  49.2 1.8 %collective-permute-start.2 = (f32[3,8,512]{2,1,0:T(8,128)S(1)}, f32[3,8,512]{2,1,0:T(8,128)S(1)}, u32[]{:S(2)}, u32[]{:S(2)}) collective-permute-start(f32[3,8,512]{2,1,0:T(8,128)S(1)} %get-tuple-element.26.sh_ref), channel_id=1, source_target_pairs={{0,16},{16,0},{32,48},{48,32},{64,80},{80,64},{96,112},{112,96},{1... | collective-permute-start | bytes 147464 | tf_op jit(solution)/shard_map/ppermute | solution.py:223
  55.6 34.7 %collective-permute-start.12 = (bf16[2,64,1024]{2,1,0:T(8,128)(2,1)S(1)}, bf16[2,64,1024]{2,1,0:T(8,128)(2,1)S(1)}, u32[]{:S(2)}, u32[]{:S(2)}) collective-permute-start(bf16[2,64,1024]{2,1,0:T(8,128)(2,1)S(1)} %get-tuple-element.37), channel_id=1, source_target_pairs={{0,224},{16,48},{32,0},{48,80},{64,32},{80,112},{96,64},{112,144},... | collective-permute-start | bytes 786440 | tf_op jit(solution)/shard_map/ppermute | solution.py:237
  60.9 36.9 %collective-permute-start.16 = (bf16[2,64,1024]{2,1,0:T(8,128)(2,1)S(1)}, bf16[2,64,1024]{2,1,0:T(8,128)(2,1)S(1)}, u32[]{:S(2)}, u32[]{:S(2)}) collective-permute-start(bf16[2,64,1024]{2,1,0:T(8,128)(2,1)S(1)} %get-tuple-element.41), channel_id=1, source_target_pairs={{0,224},{16,48},{32,0},{48,80},{64,32},{80,112},{96,64},{112,144},... | collective-permute-start | bytes 786440 | tf_op jit(solution)/shard_map/ppermute | solution.py:237
  90.3 31.0 %collective-permute-start.11 = (f32[512,1024]{1,0:T(8,128)}, f32[512,1024]{1,0:T(8,128)S(1)}, u32[]{:S(2)}, u32[]{:S(2)}) collective-permute-start(f32[512,1024]{1,0:T(8,128)} %get-tuple-element.33), channel_id=1, source_target_pairs={{0,16},{16,0},{32,48},{48,32},{64,80},{80,64},{96,112},{112,96},{1... | collective-permute-start | bytes 6291464 | tf_op jit(solution)/shard_map/ppermute | solution.py:245
  90.3 11.4 %collective-permute-start.13 = (bf16[2,64,1024]{2,1,0:T(8,128)(2,1)S(1)}, bf16[2,64,1024]{2,1,0:T(8,128)(2,1)S(1)}, u32[]{:S(2)}, u32[]{:S(2)}) collective-permute-start(bf16[2,64,1024]{2,1,0:T(8,128)(2,1)S(1)} %add_convert_fusion.7), channel_id=1, source_target_pairs={{0,224},{16,48},{32,0},{48,80},{64,32},{80,112},{96,64},{112,144},... | collective-permute-start | bytes 786440 | tf_op jit(solution)/shard_map/ppermute | solution.py:237
  97.9 7.7 %collective-permute-start.17 = (bf16[2,64,1024]{2,1,0:T(8,128)(2,1)S(1)}, bf16[2,64,1024]{2,1,0:T(8,128)(2,1)S(1)}, u32[]{:S(2)}, u32[]{:S(2)}) collective-permute-start(bf16[2,64,1024]{2,1,0:T(8,128)(2,1)S(1)} %add_convert_fusion.4), channel_id=1, source_target_pairs={{0,224},{16,48},{32,0},{48,80},{64,32},{80,112},{96,64},{112,144},... | collective-permute-start | bytes 786440 | tf_op jit(solution)/shard_map/ppermute | solution.py:237
  101.8 7.7 %collective-permute-start.14 = (bf16[2,64,1024]{2,1,0:T(8,128)(2,1)S(1)}, bf16[2,64,1024]{2,1,0:T(8,128)(2,1)S(1)}, u32[]{:S(2)}, u32[]{:S(2)}) collective-permute-start(bf16[2,64,1024]{2,1,0:T(8,128)(2,1)S(1)} %add_convert_fusion.6), channel_id=1, source_target_pairs={{0,224},{16,48},{32,0},{48,80},{64,32},{80,112},{96,64},{112,144},... | collective-permute-start | bytes 786440 | tf_op jit(solution)/shard_map/ppermute | solution.py:237
  105.6 7.7 %collective-permute-start.18 = (bf16[2,64,1024]{2,1,0:T(8,128)(2,1)S(1)}, bf16[2,64,1024]{2,1,0:T(8,128)(2,1)S(1)}, u32[]{:S(2)}, u32[]{:S(2)}) collective-permute-start(bf16[2,64,1024]{2,1,0:T(8,128)(2,1)S(1)} %add_convert_fusion.3), channel_id=1, source_target_pairs={{0,224},{16,48},{32,0},{48,80},{64,32},{80,112},{96,64},{112,144},... | collective-permute-start | bytes 786440 | tf_op jit(solution)/shard_map/ppermute | solution.py:237
  109.5 7.7 %collective-permute-start.15 = (bf16[2,64,1024]{2,1,0:T(8,128)(2,1)S(1)}, bf16[2,64,1024]{2,1,0:T(8,128)(2,1)S(1)}, u32[]{:S(2)}, u32[]{:S(2)}) collective-permute-start(bf16[2,64,1024]{2,1,0:T(8,128)(2,1)S(1)} %add_convert_fusion.5), channel_id=1, source_target_pairs={{0,224},{16,48},{32,0},{48,80},{64,32},{80,112},{96,64},{112,144},... | collective-permute-start | bytes 786440 | tf_op jit(solution)/shard_map/ppermute | solution.py:241
  113.3 7.1 %collective-permute-start.19 = (bf16[2,64,1024]{2,1,0:T(8,128)(2,1)S(1)}, bf16[2,64,1024]{2,1,0:T(8,128)(2,1)S(1)}, u32[]{:S(2)}, u32[]{:S(2)}) collective-permute-start(bf16[2,64,1024]{2,1,0:T(8,128)(2,1)S(1)} %add_convert_fusion.2), channel_id=1, source_target_pairs={{0,240},{16,32},{32,16},{48,64},{64,48},{80,96},{96,80},{112,128},... | collective-permute-start | bytes 786440 | tf_op jit(solution)/shard_map/ppermute | solution.py:242

commit v2 on v1

v2 whole, which is shorter than its diff:
```python
import functools
import math

import jax
import jax.numpy as jnp
from jax import lax
from jax.experimental import pallas as pl
from jax.experimental.pallas import tpu as pltpu
from jax.sharding import PartitionSpec as P

HD = 128
GROUP = 512
BPC = 64
CHIPS = 8
SCALE = 1.0 / math.sqrt(HD)
LOG2E = math.log2(math.e)
HIDDEN = 1e30
BF = jnp.bfloat16
F32 = jnp.float32


def nt(a, b):
    return lax.dot_general(a, b, (((1,), (1,)), ((), ())), preferred_element_type=F32)


def nn(a, b):
    return lax.dot_general(a, b, (((1,), (0,)), ((), ())), preferred_element_type=F32)


def tn(a, b):
    return lax.dot_general(a, b, (((0,), (0,)), ((), ())), preferred_element_type=F32)


def stats_kernel(
    place, q_any, k_any, v_any, g_any, o_any, ln_any,
    q_ref, k_ref, v_ref, g_ref, st_ref, o_ref, ln_ref, sems,
):
    pairs = ((g_any, g_ref), (o_any, o_ref), (ln_any, ln_ref), (q_any, q_ref), (k_any, k_ref), (v_any, v_ref))
    copies = [pltpu.make_async_copy(src, dst, sems.at[i]) for i, (src, dst) in enumerate(pairs)]
    for copy in copies:
        copy.start()
    st_ref[2] = jnp.full(st_ref.shape[1:], place[2], jnp.int32).astype(F32)
    for copy in copies[:3]:
        copy.wait()
    st_ref[0] = ln_ref[...] * LOG2E
    for h in range(ln_ref.shape[0]):
        c = slice(h * HD, (h + 1) * HD)
        prod = g_ref[:, c].astype(F32) * o_ref[:, c].astype(F32)
        st_ref[1, h : h + 1, :] = jnp.sum(prod.T, axis=0, keepdims=True)
    for copy in copies[3:]:
        copy.wait()


def raw_kernel(q_ref, k_ref, v_ref, g_ref, st_ref, wait, dq_ref, dk_ref, dv_ref):
    block = 256
    tri = lax.broadcasted_iota(jnp.int32, (block, block), 0) <= lax.broadcasted_iota(
        jnp.int32, (block, block), 1
    )
    for h in range(st_ref.shape[1]):
        c = slice(h * HD, (h + 1) * HD)
        q, k, v, g = q_ref[:, c], k_ref[:, c], v_ref[:, c], g_ref[:, c]
        ln, delta = st_ref[0, h : h + 1, :], st_ref[1, h : h + 1, :]
        stripes = []
        for lo in range(0, GROUP, block):
            hi = lo + block
            p = jnp.exp2(nt(k[lo:hi], q[lo:]) * (SCALE * LOG2E) - ln[:, lo:])
            head = jnp.where(tri, p[:, :block], 0.0)
            p = head if hi == GROUP else jnp.concatenate([head, p[:, block:]], axis=1)
            ds = (p * (nt(v[lo:hi], g[lo:]) - delta[:, lo:])).astype(BF)
            dv_ref[lo:hi, c] = nn(p.astype(BF), g[lo:]).astype(BF)
            dk_ref[lo:hi, c] = (nn(ds, q[lo:]) * SCALE).astype(BF)
            stripes.append(ds)
        for lo in range(0, GROUP, block):
            hi = lo + block
            parts = [part[:, lo - i * block : hi - i * block] for i, part in enumerate(stripes[: hi // block])]
            ds = parts[0] if len(parts) == 1 else jnp.concatenate(parts, axis=0)
            dq_ref[lo:hi, c] = (tn(k[:hi], ds) * SCALE).T


SMEM = pl.BlockSpec(memory_space=pltpu.SMEM)
VMEM = pl.BlockSpec(memory_space=pltpu.VMEM)
ANY = pl.BlockSpec(memory_space=pl.ANY)


def stats_call(place, arrays):
    heads = arrays[-1].shape[0]
    wide = (GROUP, heads * HD)
    return pl.pallas_call(
        stats_kernel,
        in_specs=[SMEM] + [ANY] * 6,
        out_specs=[VMEM] * 5,
        out_shape=[jax.ShapeDtypeStruct(wide, BF)] * 4
        + [jax.ShapeDtypeStruct((3, heads, GROUP), F32)],
        scratch_shapes=[
            pltpu.VMEM(wide, BF),
            pltpu.VMEM((heads, GROUP), F32),
            pltpu.SemaphoreType.DMA((6,)),
        ],
        compiler_params=pltpu.CompilerParams(vmem_limit_bytes=16 << 20),
        cost_estimate=pl.CostEstimate(
            flops=2 * heads * GROUP * HD, bytes_accessed=8 << 20, transcendentals=0
        ),
        name="stats",
    )(place, *[pltpu.with_memory_space_constraint(x, pltpu.HBM) for x in arrays])


def raw_call(queries, keys, values, out_grad, stats, wait):
    heads = stats.shape[1]
    wide = queries.shape
    return pl.pallas_call(
        raw_kernel,
        in_specs=[VMEM] * 5 + [ANY],
        out_specs=[VMEM] * 3,
        out_shape=[jax.ShapeDtypeStruct(wide, kind) for kind in (F32, BF, BF)],
        compiler_params=pltpu.CompilerParams(vmem_limit_bytes=16 << 20),
        cost_estimate=pl.CostEstimate(
            flops=10 * heads * GROUP * GROUP * HD, bytes_accessed=10 << 20, transcendentals=heads * GROUP * GROUP
        ),
        name="raw_tokens",
    )(queries, keys, values, out_grad, stats, wait)


def beacon_kernel(shifts, waits, place, qh_ref, qp_ref, gh_ref, gp_ref, sh_ref, sp_ref, *refs):
    count = len(shifts)
    pieces, refs = refs[:count], refs[count + waits :]
    outs, ds_ref = refs[:count], refs[count]
    z, core = place[0], place[1]
    chunks = [z + shift for shift in shifts]
    sides = ((qh_ref, gh_ref, sh_ref, 2 * z + core), (qp_ref, gp_ref, sp_ref, 2 * z + 1 - core))

    def work():
        far = [
            [
                jnp.where((chunk >= 0) & (2 * chunk + core <= group), group - 2 * chunk - core, 2 * CHIPS)
                for chunk in chunks
            ]
            for *_, group in sides
        ]
        for h in range(sh_ref.shape[1]):
            c = slice(h * HD, (h + 1) * HD)
            kk = jnp.concatenate([ref[0, :, c] for ref in pieces], axis=0)
            vv = jnp.concatenate([ref[1, :, c] for ref in pieces], axis=0)
            dk = dv = None
            for side, (q_ref, g_ref, st_ref, _) in enumerate(sides):
                q, g = q_ref[:, c], g_ref[:, c]
                ln, delta, reach = (st_ref[i, h : h + 1, :] for i in range(3))
                bias = jnp.concatenate(
                    [
                        jnp.broadcast_to(
                            jnp.where(reach > jnp.full((1, GROUP), d, jnp.int32).astype(F32), ln, HIDDEN),
                            (BPC, GROUP),
                        )
                        for d in far[side]
                    ],
                    axis=0,
                )
                p = jnp.exp2(nt(kk, q) * (SCALE * LOG2E) - bias)
                ds = (p * (nt(vv, g) - delta)).astype(BF)
                ds_ref[h, :, side * GROUP : (side + 1) * GROUP] = ds
                dv_part, dk_part = nn(p.astype(BF), g), nn(ds, q)
                dk, dv = (dk_part, dv_part) if dk is None else (dk + dk_part, dv + dv_part)
            dk = dk * SCALE
            for i, ref in enumerate(outs):
                ref[0, :, c] = dk[i * BPC : (i + 1) * BPC].astype(ref.dtype)
                ref[1, :, c] = dv[i * BPC : (i + 1) * BPC].astype(ref.dtype)

    if 0 in shifts:
        work()
        return
    valid = functools.reduce(jnp.logical_or, [chunk >= 0 for chunk in chunks])
    pl.when(valid)(work)

    @pl.when(jnp.logical_not(valid))
    def _():
        for ref in outs:
            ref[...] = jnp.zeros_like(ref)
        ds_ref[...] = jnp.zeros_like(ds_ref)


def beacon_call(place, sides, parts, waits, name):
    pieces, shifts, kinds = zip(*parts, strict=True)
    heads = sides[4].shape[1]
    count = len(pieces)
    items = heads * 2 * GROUP * count * BPC
    return pl.pallas_call(
        functools.partial(beacon_kernel, shifts, len(waits)),
        in_specs=[SMEM] + [VMEM] * (6 + count) + [ANY] * len(waits),
        out_specs=[VMEM] * (count + 1),
        out_shape=[jax.ShapeDtypeStruct((2, BPC, heads * HD), kind) for kind in kinds]
        + [jax.ShapeDtypeStruct((heads, count * BPC, 2 * GROUP), BF)],
        compiler_params=pltpu.CompilerParams(vmem_limit_bytes=16 << 20),
        cost_estimate=pl.CostEstimate(flops=8 * items * HD, bytes_accessed=8 << 20, transcendentals=items),
        name=name,
    )(place, *sides, *pieces, *waits)


def query_kernel(steps, *refs):
    ds_refs, k_refs, outs = refs[:steps], refs[steps:-2], refs[-2:]
    for h in range(ds_refs[0].shape[0]):
        c = slice(h * HD, (h + 1) * HD)
        kk = jnp.concatenate([ref[0, :, c] for ref in k_refs], axis=0)
        for side, out in enumerate(outs):
            ds = jnp.concatenate([ref[h, :, side * GROUP : (side + 1) * GROUP] for ref in ds_refs], axis=0)
            out[:, c] = (tn(kk, ds) * SCALE).T.astype(out.dtype)


def query_call(ds_list, pieces):
    heads = ds_list[0].shape[0]
    rows = sum(ds.shape[1] for ds in ds_list)
    return pl.pallas_call(
        functools.partial(query_kernel, len(ds_list)),
        in_specs=[VMEM] * (len(ds_list) + len(pieces)),
        out_specs=[VMEM] * 2,
        out_shape=[jax.ShapeDtypeStruct((GROUP, heads * HD), kind) for kind in (F32, BF)],
        compiler_params=pltpu.CompilerParams(vmem_limit_bytes=16 << 20),
        cost_estimate=pl.CostEstimate(
            flops=2 * heads * rows * 2 * GROUP * HD, bytes_accessed=16 << 20, transcendentals=0
        ),
        name="query_grad",
    )(*ds_list, *pieces)


def join(array, *after):
    return pl.pallas_call(
        lambda *refs: None,
        in_specs=[ANY] * (1 + len(after)),
        out_specs=ANY,
        out_shape=jax.ShapeDtypeStruct(array.shape, array.dtype),
        input_output_aliases={0: 0},
        compiler_params=pltpu.CompilerParams(vmem_limit_bytes=1 << 20),
        name="join",
    )(array, *after)


def both(a, b, *after):
    a = join(a, b, *after)
    return a, join(b, a)


def at(z, core):
    return 2 * (z % CHIPS) + core


SWAP = [(at(z, core), at(z, 1 - core)) for z in range(CHIPS) for core in (0, 1)]


UP = [(at(z, core), at(z + 1, core)) for z in range(CHIPS) for core in (0, 1)]
FAR = [(at(z, core), at(z + 4, core)) for z in range(CHIPS - 4) for core in (0, 1)]
DOWN = [(at(z, core), at(z - 1, core)) for z in range(CHIPS) for core in (0, 1)]


def local(
    queries, keys, values, out_grad, forward_out, log_norm, beacon_keys, beacon_values, beacon_reach
):
    ctx = lax.axis_index("ctx").astype(jnp.int32)
    place = jnp.stack([ctx // 2, ctx % 2, beacon_reach[0].astype(jnp.int32)])
    send = functools.partial(lax.ppermute, axis_name="ctx")
    own = jnp.stack([beacon_keys, beacon_values])
    a1, b1, d4 = send(own, perm=UP), send(own, perm=DOWN), send(own, perm=FAR)
    queries_other, grad_other = send(queries, perm=SWAP), send(out_grad, perm=SWAP)
    q_home, k_home, v_home, g_home, stats = stats_call(
        place, (queries, keys, values, out_grad, forward_out, log_norm)
    )
    sides = (q_home, queries_other, g_home, grad_other, stats, send(stats, perm=SWAP))
    a1, b1 = both(a1, b1, stats)
    a2, b2 = send(a1, perm=UP), send(b1, perm=DOWN)
    t1a, t1b, t0, ds1 = beacon_call(
        place, sides, ((a1, -1, F32), (b1, 1 - CHIPS, F32), (own, 0, F32)), (), "beacons_near"
    )
    a2, b2 = both(a2, b2, ds1)
    a3, b3 = send(a2, perm=UP), send(b2, perm=DOWN)
    t4, ds4 = beacon_call(place, sides, ((d4, -4, BF),), (a2, b2), "beacons_far")
    a3, b3 = both(a3, b3, t4)

    def plus(arrived, term):
        return (arrived.astype(F32) + term).astype(BF)

    a = send(t4, perm=DOWN)
    t3a, b, ds3 = beacon_call(place, sides, ((a3, -3, F32), (b3, 3 - CHIPS, BF)), (t4,), "beacons_third")
    a, b = both(a, b)
    a, b = send(plus(a, t3a), perm=DOWN), send(b, perm=UP)
    t2a, t2b, ds2 = beacon_call(
        place, sides, ((a2, -2, F32), (b2, 2 - CHIPS, F32)), (t3a,), "beacons_second"
    )
    a, b = both(a, b, ds2)
    a, b = send(plus(a, t2a), perm=DOWN), send(plus(b, t2b), perm=UP)
    dq_home, dq_other = query_call((ds1, ds2, ds3, ds4), (a1, b1, own, a2, b2, a3, b3, d4))
    a, b = both(a, b, dq_other)
    a, b = send(plus(a, t1a), perm=DOWN), send(plus(b, t1b), perm=UP)
    dq_raw, key_grad, value_grad = raw_call(q_home, k_home, v_home, g_home, stats, dq_other)
    query_grad = (dq_raw + dq_home + send(dq_other, perm=SWAP).astype(F32)).astype(BF)
    total = (join(t0, query_grad) + (a.astype(F32) + b.astype(F32))).astype(BF)
    return query_grad, key_grad, value_grad, total[0], total[1]


def solution(mesh):
    tokens = P(("dp", "ctx"), "head")
    in_specs = (tokens,) * 5 + (P("head", ("dp", "ctx")), tokens, tokens, P(("dp", "ctx")))
    return jax.shard_map(local, mesh=mesh, in_specs=in_specs, out_specs=(tokens,) * 5, check_vma=False)
```

time: 124 us -> 79.8 us (0.64); the launches traced: 123 us -> 79.7 us
  Pallas kernels: 44.9 us -> 17.5 us
  local copies, waits for them, and re-layouts: 7.56 us -> 0.72 us
  waiting for transfers between devices: 32 us -> 27.3 us
  starting transfers between devices: 33.9 us -> 30.6 us
    pallas_call x7 -> x20, Pallas kernels: 44.9 us -> 17.5 us  [the longest x4 7.02 us: beacon_call(): pl.pallas_call(functools.partial(beacon_kernel, shifts, len(waits)), in_s...]
    unnamed x14 -> x2, local copies, waits for them, and re-layouts: 6.84 us -> 0.01 us
    ppermute x20 -> x18, waiting for transfers between devices: 32 us -> 27.3 us  [the longest x2 6.3 us: local(): a, b = (send(plus(a, t1a), perm=DOWN), send(plus(b, t1b), perm=UP))]
    ppermute x20 -> x18, starting transfers between devices: 33.9 us -> 30.6 us  [the longest x3 9.55 us: local(): a1, b1, d4 = (send(own, perm=UP), send(own, perm=DOWN), send(own, perm=FAR))]
  transfers between devices with their start and end apart: 20 -> 18, of which waited for: 11 -> 10; matrix products, arithmetic and copies ran while one was open for 1% -> 2% of each run, Pallas kernels for 33% -> 22%
where the time goes in v2:
time: 79.8 us; the launch traced here: 79.7 us
  starting transfers between devices  30.6 us (38%)
  waiting for transfers between devices  27.3 us (34%)
  Pallas kernels  17.5 us (22%)
  other arithmetic  2.08 us (3%)
  between operations  1.49 us (2%)
    ppermute x3, starting transfers between devices, local(): a1, b1, d4 = (send(own, perm=UP), send(own, perm=DOWN), send(own, perm=FAR))  9.55 us
    ppermute x1, starting transfers between devices, local(): a = send(t4, perm=DOWN)  9.19 us
    pallas_call x4, Pallas kernels, beacon_call(): pl.pallas_call(functools.partial(beacon_kernel, shifts, len(waits)), in_s...  7.02 us
    ppermute x2, waiting for transfers between devices, local(): a, b = (send(plus(a, t1a), perm=DOWN), send(plus(b, t1b), perm=UP))  6.3 us
    pallas_call x1, Pallas kernels, raw_call(): pl.pallas_call(raw_kernel, in_specs=[VMEM] * 5 + [ANY], out_specs=[VMEM]...  5.66 us
    ppermute x2, waiting for transfers between devices, local(): a, b = (send(plus(a, t3a), perm=DOWN), send(b, perm=UP))  5.62 us
    ppermute x3, waiting for transfers between devices, local(): a1, b1, d4 = (send(own, perm=UP), send(own, perm=DOWN), send(own, perm=FAR))  5.4 us
    ppermute x1, waiting for transfers between devices, local(): a = send(t4, perm=DOWN)  4.09 us
  transfers between devices with their start and end apart: 18, of which 10 were waited for; matrix products, arithmetic and copies ran while one was open for 2% of the time, Pallas kernels for 22%

profile of v2, /device:TPU:6, one launch (start us, length us, event | category | flops | bytes accessed | tf_op | source)
XLA Modules:
  0.0 79.7 jit_solution(16440676012226627792)
XLA Ops:
  0.6 0.1 collective-permute-start
  0.7 0.5 collective-permute-start.1
  1.2 1.0 %pad_maximum_fusion.refs_2_.refs_6_ = bf16[2,64,1024]{2,1,0:T(8,128)(2,1)S(1)} fusion(bf16[1,64,1024]{2,1,0:T(8,128)(2,1)} %bitcast.8, bf16[1,64,1024]{2,1,0:T(8,128)(2,1)} %bitcast.9), kind=kLoop, calls=%fused_computation.7 | loop fusion | flops 131072 | bytes 524288 | tf_op jit(solution)/shard_map/stack | solution.py:258
  2.2 5.9 %collective-permute-start.4 = (bf16[2,64,1024]{2,1,0:T(8,128)(2,1)S(1)}, bf16[2,64,1024]{2,1,0:T(8,128)(2,1)S(1)}, u32[]{:S(2)}, u32[]{:S(2)}) collective-permute-start(bf16[2,64,1024]{2,1,0:T(8,128)(2,1)S(1)} %pad_maximum_fusion.refs_2_.refs_6_), channel_id=1, source_target_pairs={{0,224},{16,240},{32,0},{48,16},{64,32},{80,48},{96,64},{112,80},{... | collective-permute-start | bytes 786440 | tf_op jit(solution)/shard_map/ppermute | solution.py:259
  8.2 0.0 collective-permute-start.3
  8.8 0.1 pad_add_fusion.place
  8.9 3.1 %stats.1 = (bf16[512,1024]{1,0:T(8,128)(2,1)S(1)}, bf16[512,1024]{1,0:T(8,128)(2,1)S(1)}, bf16[512,1024]{1,0:T(8,128)(2,1)S(1)}, bf16[512,1024]{1,0:T(8,128)(2,1)S(1)}, f32[3,8,512]{2,1,0:T(8,128)S(1)}) custom-call(s32[3]{0:T(128)S(1)} %pad_add_fusion.place, bf16[512,1024]{1,0:T(8,128)(2,1)} %q_any.1, bf16[512,1024]{1,0:T(8,128)(2,1)} %k_any.1, ...), custom_call_target="tpu_custom_call" | custom-call | flops 1048576 | bytes 8388608 | tf_op jit(solution)/shard_map/stats/pallas_call | solution.py:88
  12.0 2.0 %collective-permute-done.4.refs_1_.refs_0_ = bf16[2,64,1024]{2,1,0:T(8,128)(2,1)S(1)} collective-permute-done((bf16[2,64,1024]{2,1,0:T(8,128)(2,1)S(1)}, bf16[2,64,1024]{2,1,0:T(8,128)(2,1)S(1)}, u32[]{:S(2)}, u32[]{:S(2)}) %collective-permute-start.4) | collective-permute-done | bytes 262176 | tf_op jit(solution)/shard_map/ppermute | solution.py:259
  14.0 3.4 %collective-permute-done.3.refs_0_ = bf16[2,64,1024]{2,1,0:T(8,128)(2,1)S(1)} collective-permute-done((bf16[2,64,1024]{2,1,0:T(8,128)(2,1)S(1)}, bf16[2,64,1024]{2,1,0:T(8,128)(2,1)S(1)}, u32[]{:S(2)}, u32[]{:S(2)}) %collective-permute-start.3) | collective-permute-done | bytes 262176 | tf_op jit(solution)/shard_map/ppermute | solution.py:259
  17.4 0.3 collective-permute-start.6
  17.7 1.7 %collective-permute-start.5 = (bf16[2,64,1024]{2,1,0:T(8,128)(2,1)S(1)}, bf16[2,64,1024]{2,1,0:T(8,128)(2,1)S(1)}, u32[]{:S(2)}, u32[]{:S(2)}) collective-permute-start(bf16[2,64,1024]{2,1,0:T(8,128)(2,1)S(1)} %join.13.refs_1_.refs_0_.refs_4_), channel_id=1, source_target_pairs={{0,32},{16,48},{32,64},{48,80},{64,96},{80,112},{96,128},{112,144}... | collective-permute-start | bytes 786440 | tf_op jit(solution)/shard_map/ppermute | solution.py:266
  19.4 0.0 collective-permute-start.2
  19.4 1.2 %collective-permute-done.2.sp_ref = f32[3,8,512]{2,1,0:T(8,128)S(1)} collective-permute-done((f32[3,8,512]{2,1,0:T(8,128)S(1)}, f32[3,8,512]{2,1,0:T(8,128)S(1)}, u32[]{:S(2)}, u32[]{:S(2)}) %collective-permute-start.2) | collective-permute-done | bytes 49184 | tf_op jit(solution)/shard_map/ppermute | solution.py:264
  20.7 3.6 %collective-permute-start.9 = (bf16[2,64,1024]{2,1,0:T(8,128)(2,1)S(1)}, bf16[2,64,1024]{2,1,0:T(8,128)(2,1)S(1)}, u32[]{:S(2)}, u32[]{:S(2)}) collective-permute-start(bf16[2,64,1024]{2,1,0:T(8,128)(2,1)S(1)} %pad_maximum_fusion.refs_2_.refs_6_), channel_id=1, source_target_pairs={{0,128},{16,144},{32,160},{48,176},{64,192},{80,208},{96,224},{112... | collective-permute-start | bytes 786440 | tf_op jit(solution)/shard_map/ppermute | solution.py:259
  24.3 0.0 collective-permute-done.qp_ref
  24.3 0.0 collective-permute-done.1.gp_ref
  24.3 4.5 %beacons_near.1 = (f32[2,64,1024]{2,1,0:T(8,128)S(1)}, f32[2,64,1024]{2,1,0:T(8,128)S(1)}, f32[2,64,1024]{2,1,0:T(8,128)S(1)}, bf16[8,192,1024]{2,1,0:T(8,128)(2,1)S(1)}) custom-call(s32[3]{0:T(128)S(1)} %pad_add_fusion.place, bf16[512,1024]{1,0:T(8,128)(2,1)S(1)} %get-tuple-element.27.qh_ref.q_ref, bf16[512,1024]{1,0:T(8,128)(2,1)S(1)} %collective-permute-done.qp_ref, ...), custom_call_target="tpu_custom_call" | custom-call | flops 1610612736 | bytes 8388608 | tf_op jit(solution)/shard_map/beacons_near/pallas_call | solution.py:185
  28.8 0.0 collective-permute-done.6.refs_1_.refs_0_
  28.8 0.0 collective-permute-done.5.refs_0_
  28.8 0.1 collective-permute-start.8
  28.9 2.0 %collective-permute-start.7 = (bf16[2,64,1024]{2,1,0:T(8,128)(2,1)S(1)}, bf16[2,64,1024]{2,1,0:T(8,128)(2,1)S(1)}, u32[]{:S(2)}, u32[]{:S(2)}) collective-permute-start(bf16[2,64,1024]{2,1,0:T(8,128)(2,1)S(1)} %join.15.refs_1_.refs_0_.refs_7_), channel_id=1, source_target_pairs={{0,32},{16,48},{32,64},{48,80},{64,96},{80,112},{96,128},{112,144}... | collective-permute-start | bytes 786440 | tf_op jit(solution)/shard_map/ppermute | solution.py:271
  30.9 0.0 collective-permute-done.9.refs_0_.refs_11_
  30.9 0.8 %beacons_far.1 = (bf16[2,64,1024]{2,1,0:T(8,128)(2,1)S(1)}, bf16[8,64,1024]{2,1,0:T(8,128)(2,1)S(1)}) custom-call(s32[3]{0:T(128)S(1)} %pad_add_fusion.place, bf16[512,1024]{1,0:T(8,128)(2,1)S(1)} %get-tuple-element.27.qh_ref.q_ref, bf16[512,1024]{1,0:T(8,128)(2,1)S(1)} %collective-permute-done.qp_ref, bf16[512,1024]{1,0:T(8,128)(2,1)S(1)} %get-tuple-element.30.gh_ref.g_ref, ...), custom_call_target="tpu_custom_call" | custom-call | flops 536870912 | bytes 8388608 | tf_op jit(solution)/shard_map/beacons_far/pallas_call | solution.py:185
  31.8 9.2 %collective-permute-start.11 = (bf16[2,64,1024]{2,1,0:T(8,128)(2,1)S(1)}, bf16[2,64,1024]{2,1,0:T(8,128)(2,1)S(1)}, u32[]{:S(2)}, u32[]{:S(2)}) collective-permute-start(bf16[2,64,1024]{2,1,0:T(8,128)(2,1)S(1)} %get-tuple-element.33.refs_2_), channel_id=1, source_target_pairs={{0,224},{16,240},{32,0},{48,16},{64,32},{80,48},{96,64},{112,80},{... | collective-permute-start | bytes 786440 | tf_op jit(solution)/shard_map/ppermute | solution.py:278
  41.0 2.1 %collective-permute-done.8.refs_1_.refs_0_ = bf16[2,64,1024]{2,1,0:T(8,128)(2,1)S(1)} collective-permute-done((bf16[2,64,1024]{2,1,0:T(8,128)(2,1)S(1)}, bf16[2,64,1024]{2,1,0:T(8,128)(2,1)S(1)}, u32[]{:S(2)}, u32[]{:S(2)}) %collective-permute-start.8) | collective-permute-done | bytes 262176 | tf_op jit(solution)/shard_map/ppermute | solution.py:271
  43.1 0.0 collective-permute-done.7.refs_0_
  43.1 0.7 beacons_third.1
  43.8 4.1 %collective-permute-done.11.refs_0_ = bf16[2,64,1024]{2,1,0:T(8,128)(2,1)S(1)} collective-permute-done((bf16[2,64,1024]{2,1,0:T(8,128)(2,1)S(1)}, bf16[2,64,1024]{2,1,0:T(8,128)(2,1)S(1)}, u32[]{:S(2)}, u32[]{:S(2)}) %collective-permute-start.11) | collective-permute-done | bytes 262176 | tf_op jit(solution)/shard_map/ppermute | solution.py:278
  47.9 0.1 add_convert_fusion.6
  48.0 2.7 %collective-permute-start.12 = (bf16[2,64,1024]{2,1,0:T(8,128)(2,1)S(1)}, bf16[2,64,1024]{2,1,0:T(8,128)(2,1)S(1)}, u32[]{:S(2)}, u32[]{:S(2)}) collective-permute-start(bf16[2,64,1024]{2,1,0:T(8,128)(2,1)S(1)} %add_convert_fusion.6), channel_id=1, source_target_pairs={{0,224},{16,240},{32,0},{48,16},{64,32},{80,48},{96,64},{112,80},{... | collective-permute-start | bytes 786440 | tf_op jit(solution)/shard_map/ppermute | solution.py:281
  50.7 0.0 collective-permute-start.13
  50.7 1.0 %beacons_second.1 = (f32[2,64,1024]{2,1,0:T(8,128)S(1)}, f32[2,64,1024]{2,1,0:T(8,128)S(1)}, bf16[8,128,1024]{2,1,0:T(8,128)(2,1)S(1)}) custom-call(s32[3]{0:T(128)S(1)} %pad_add_fusion.place, bf16[512,1024]{1,0:T(8,128)(2,1)S(1)} %get-tuple-element.27.qh_ref.q_ref, bf16[512,1024]{1,0:T(8,128)(2,1)S(1)} %collective-permute-done.qp_ref, ...), custom_call_target="tpu_custom_call" | custom-call | flops 1073741824 | bytes 8388608 | tf_op jit(solution)/shard_map/beacons_second/pallas_call | solution.py:185
  51.7 1.7 %query_grad.1 = (f32[512,1024]{1,0:T(8,128)S(1)}, bf16[512,1024]{1,0:T(8,128)(2,1)S(1)}) custom-call(bf16[8,192,1024]{2,1,0:T(8,128)(2,1)S(1)} %get-tuple-element.32.refs_2_.refs_0_, bf16[8,128,1024]{2,1,0:T(8,128)(2,1)S(1)} %get-tuple-element.35.refs_1_.refs_2_, bf16[8,128,1024]{2,1,0:T(8,128)(2,1)S(1)} %get-tuple-element.36.refs_2_, ...), custom_call_target="tpu_custom_call" | custom-call | flops 1073741824 | bytes 16777216 | tf_op jit(solution)/shard_map/query_grad/pallas_call | solution.py:210
  53.4 0.1 collective-permute-start.10
  53.5 2.2 %collective-permute-done.12.refs_0_ = bf16[2,64,1024]{2,1,0:T(8,128)(2,1)S(1)} collective-permute-done((bf16[2,64,1024]{2,1,0:T(8,128)(2,1)S(1)}, bf16[2,64,1024]{2,1,0:T(8,128)(2,1)S(1)}, u32[]{:S(2)}, u32[]{:S(2)}) %collective-permute-start.12) | collective-permute-done | bytes 262176 | tf_op jit(solution)/shard_map/ppermute | solution.py:281
  55.7 3.4 %collective-permute-done.13.refs_1_.refs_0_ = bf16[2,64,1024]{2,1,0:T(8,128)(2,1)S(1)} collective-permute-done((bf16[2,64,1024]{2,1,0:T(8,128)(2,1)S(1)}, bf16[2,64,1024]{2,1,0:T(8,128)(2,1)S(1)}, u32[]{:S(2)}, u32[]{:S(2)}) %collective-permute-start.13) | collective-permute-done | bytes 262176 | tf_op jit(solution)/shard_map/ppermute | solution.py:281
  59.1 0.1 add_convert_fusion.5
  59.2 0.7 collective-permute-start.14
  59.9 0.1 add_convert_fusion.4
  59.9 1.5 %collective-permute-start.15 = (bf16[2,64,1024]{2,1,0:T(8,128)(2,1)S(1)}, bf16[2,64,1024]{2,1,0:T(8,128)(2,1)S(1)}, u32[]{:S(2)}, u32[]{:S(2)}) collective-permute-start(bf16[2,64,1024]{2,1,0:T(8,128)(2,1)S(1)} %add_convert_fusion.4), channel_id=1, source_target_pairs={{0,32},{16,48},{32,64},{48,80},{64,96},{80,112},{96,128},{112,144}... | collective-permute-start | bytes 786440 | tf_op jit(solution)/shard_map/ppermute | solution.py:286
  61.4 5.7 %raw_tokens.1 = (f32[512,1024]{1,0:T(8,128)S(1)}, bf16[512,1024]{1,0:T(8,128)(2,1)}, bf16[512,1024]{1,0:T(8,128)(2,1)}) custom-call(bf16[512,1024]{1,0:T(8,128)(2,1)S(1)} %get-tuple-element.27.qh_ref.q_ref, bf16[512,1024]{1,0:T(8,128)(2,1)S(1)} %get-tuple-element.28.k_ref, bf16[512,1024]{1,0:T(8,128)(2,1)S(1)} %get-tuple-element.29.v_ref, ...), custom_call_target="tpu_custom_call" | custom-call | flops 2684354560 | bytes 10485760 | tf_op jit(solution)/shard_map/raw_tokens/pallas_call | solution.py:110
  67.1 0.0 collective-permute-done.14.refs_0_
  67.1 2.5 %collective-permute-done.15.refs_1_.refs_0_ = bf16[2,64,1024]{2,1,0:T(8,128)(2,1)S(1)} collective-permute-done((bf16[2,64,1024]{2,1,0:T(8,128)(2,1)S(1)}, bf16[2,64,1024]{2,1,0:T(8,128)(2,1)S(1)}, u32[]{:S(2)}, u32[]{:S(2)}) %collective-permute-start.15) | collective-permute-done | bytes 262176 | tf_op jit(solution)/shard_map/ppermute | solution.py:286
  69.6 0.1 add_convert_fusion.3
  69.7 0.2 collective-permute-start.16
  69.9 0.1 add_convert_fusion.2
  70.0 2.0 %collective-permute-start.17 = (bf16[2,64,1024]{2,1,0:T(8,128)(2,1)S(1)}, bf16[2,64,1024]{2,1,0:T(8,128)(2,1)S(1)}, u32[]{:S(2)}, u32[]{:S(2)}) collective-permute-start(bf16[2,64,1024]{2,1,0:T(8,128)(2,1)S(1)} %add_convert_fusion.2), channel_id=1, source_target_pairs={{0,32},{16,48},{32,64},{48,80},{64,96},{80,112},{96,128},{112,144}... | collective-permute-start | bytes 786440 | tf_op jit(solution)/shard_map/ppermute | solution.py:289
  71.9 0.0 collective-permute-done.10
  71.9 0.6 add_convert_fusion.refs_1_
  72.5 0.0 copy-start
  72.6 4.8 %collective-permute-done.16 = bf16[2,64,1024]{2,1,0:T(8,128)(2,1)S(1)} collective-permute-done((bf16[2,64,1024]{2,1,0:T(8,128)(2,1)S(1)}, bf16[2,64,1024]{2,1,0:T(8,128)(2,1)S(1)}, u32[]{:S(2)}, u32[]{:S(2)}) %collective-permute-start.16) | collective-permute-done | bytes 262176 | tf_op jit(solution)/shard_map/ppermute | solution.py:289
  77.3 1.5 %collective-permute-done.17 = bf16[2,64,1024]{2,1,0:T(8,128)(2,1)S(1)} collective-permute-done((bf16[2,64,1024]{2,1,0:T(8,128)(2,1)S(1)}, bf16[2,64,1024]{2,1,0:T(8,128)(2,1)S(1)}, u32[]{:S(2)}, u32[]{:S(2)}) %collective-permute-start.17) | collective-permute-done | bytes 262176 | tf_op jit(solution)/shard_map/ppermute | solution.py:289
  78.9 0.1 add_convert_fusion.1
  79.0 0.7 slice_bitcast_fusion
  79.7 0.0 copy-done
  (13 shorter events, 0.0 us)
Async XLA Ops:
  0.6 23.7 %collective-permute-start = (bf16[512,1024]{1,0:T(8,128)(2,1)}, bf16[512,1024]{1,0:T(8,128)(2,1)S(1)}, u32[]{:S(2)}, u32[]{:S(2)}) collective-permute-start(bf16[512,1024]{1,0:T(8,128)(2,1)} %q_any.1), channel_id=1, source_target_pairs={{0,16},{16,0},{32,48},{48,32},{64,80},{80,64},{96,112},{112,96},{1... | collective-permute-start | bytes 3145736 | tf_op jit(solution)/shard_map/ppermute | solution.py:260
  0.7 23.6 %collective-permute-start.1 = (bf16[512,1024]{1,0:T(8,128)(2,1)}, bf16[512,1024]{1,0:T(8,128)(2,1)S(1)}, u32[]{:S(2)}, u32[]{:S(2)}) collective-permute-start(bf16[512,1024]{1,0:T(8,128)(2,1)} %g_any.1), channel_id=1, source_target_pairs={{0,16},{16,0},{32,48},{48,32},{64,80},{80,64},{96,112},{112,96},{1... | collective-permute-start | bytes 3145736 | tf_op jit(solution)/shard_map/ppermute | solution.py:260
  2.2 11.8 %collective-permute-start.4 = (bf16[2,64,1024]{2,1,0:T(8,128)(2,1)S(1)}, bf16[2,64,1024]{2,1,0:T(8,128)(2,1)S(1)}, u32[]{:S(2)}, u32[]{:S(2)}) collective-permute-start(bf16[2,64,1024]{2,1,0:T(8,128)(2,1)S(1)} %pad_maximum_fusion.refs_2_.refs_6_), channel_id=1, source_target_pairs={{0,224},{16,240},{32,0},{48,16},{64,32},{80,48},{96,64},{112,80},{... | collective-permute-start | bytes 786440 | tf_op jit(solution)/shard_map/ppermute | solution.py:259
  8.2 9.2 %collective-permute-start.3 = (bf16[2,64,1024]{2,1,0:T(8,128)(2,1)S(1)}, bf16[2,64,1024]{2,1,0:T(8,128)(2,1)S(1)}, u32[]{:S(2)}, u32[]{:S(2)}) collective-permute-start(bf16[2,64,1024]{2,1,0:T(8,128)(2,1)S(1)} %pad_maximum_fusion.refs_2_.refs_6_), channel_id=1, source_target_pairs={{0,32},{16,48},{32,64},{48,80},{64,96},{80,112},{96,128},{112,144}... | collective-permute-start | bytes 786440 | tf_op jit(solution)/shard_map/ppermute | solution.py:259
  17.4 11.4 %collective-permute-start.6 = (bf16[2,64,1024]{2,1,0:T(8,128)(2,1)S(1)}, bf16[2,64,1024]{2,1,0:T(8,128)(2,1)S(1)}, u32[]{:S(2)}, u32[]{:S(2)}) collective-permute-start(bf16[2,64,1024]{2,1,0:T(8,128)(2,1)S(1)} %join.14.refs_1_.refs_5_), channel_id=1, source_target_pairs={{0,224},{16,240},{32,0},{48,16},{64,32},{80,48},{96,64},{112,80},{... | collective-permute-start | bytes 786440 | tf_op jit(solution)/shard_map/ppermute | solution.py:266
  17.7 11.1 %collective-permute-start.5 = (bf16[2,64,1024]{2,1,0:T(8,128)(2,1)S(1)}, bf16[2,64,1024]{2,1,0:T(8,128)(2,1)S(1)}, u32[]{:S(2)}, u32[]{:S(2)}) collective-permute-start(bf16[2,64,1024]{2,1,0:T(8,128)(2,1)S(1)} %join.13.refs_1_.refs_0_.refs_4_), channel_id=1, source_target_pairs={{0,32},{16,48},{32,64},{48,80},{64,96},{80,112},{96,128},{112,144}... | collective-permute-start | bytes 786440 | tf_op jit(solution)/shard_map/ppermute | solution.py:266
  19.4 1.2 %collective-permute-start.2 = (f32[3,8,512]{2,1,0:T(8,128)S(1)}, f32[3,8,512]{2,1,0:T(8,128)S(1)}, u32[]{:S(2)}, u32[]{:S(2)}) collective-permute-start(f32[3,8,512]{2,1,0:T(8,128)S(1)} %get-tuple-element.31.refs_2_.sh_ref.st_ref), channel_id=1, source_target_pairs={{0,16},{16,0},{32,48},{48,32},{64,80},{80,64},{96,112},{112,96},{1... | collective-permute-start | bytes 147464 | tf_op jit(solution)/shard_map/ppermute | solution.py:264
  20.7 10.3 %collective-permute-start.9 = (bf16[2,64,1024]{2,1,0:T(8,128)(2,1)S(1)}, bf16[2,64,1024]{2,1,0:T(8,128)(2,1)S(1)}, u32[]{:S(2)}, u32[]{:S(2)}) collective-permute-start(bf16[2,64,1024]{2,1,0:T(8,128)(2,1)S(1)} %pad_maximum_fusion.refs_2_.refs_6_), channel_id=1, source_target_pairs={{0,128},{16,144},{32,160},{48,176},{64,192},{80,208},{96,224},{112... | collective-permute-start | bytes 786440 | tf_op jit(solution)/shard_map/ppermute | solution.py:259
  28.8 14.3 %collective-permute-start.8 = (bf16[2,64,1024]{2,1,0:T(8,128)(2,1)S(1)}, bf16[2,64,1024]{2,1,0:T(8,128)(2,1)S(1)}, u32[]{:S(2)}, u32[]{:S(2)}) collective-permute-start(bf16[2,64,1024]{2,1,0:T(8,128)(2,1)S(1)} %join.16.refs_2_.refs_1_.refs_8_), channel_id=1, source_target_pairs={{0,224},{16,240},{32,0},{48,16},{64,32},{80,48},{96,64},{112,80},{... | collective-permute-start | bytes 786440 | tf_op jit(solution)/shard_map/ppermute | solution.py:271
  28.9 14.2 %collective-permute-start.7 = (bf16[2,64,1024]{2,1,0:T(8,128)(2,1)S(1)}, bf16[2,64,1024]{2,1,0:T(8,128)(2,1)S(1)}, u32[]{:S(2)}, u32[]{:S(2)}) collective-permute-start(bf16[2,64,1024]{2,1,0:T(8,128)(2,1)S(1)} %join.15.refs_1_.refs_0_.refs_7_), channel_id=1, source_target_pairs={{0,32},{16,48},{32,64},{48,80},{64,96},{80,112},{96,128},{112,144}... | collective-permute-start | bytes 786440 | tf_op jit(solution)/shard_map/ppermute | solution.py:271
  31.8 16.2 %collective-permute-start.11 = (bf16[2,64,1024]{2,1,0:T(8,128)(2,1)S(1)}, bf16[2,64,1024]{2,1,0:T(8,128)(2,1)S(1)}, u32[]{:S(2)}, u32[]{:S(2)}) collective-permute-start(bf16[2,64,1024]{2,1,0:T(8,128)(2,1)S(1)} %get-tuple-element.33.refs_2_), channel_id=1, source_target_pairs={{0,224},{16,240},{32,0},{48,16},{64,32},{80,48},{96,64},{112,80},{... | collective-permute-start | bytes 786440 | tf_op jit(solution)/shard_map/ppermute | solution.py:278
  48.0 7.7 %collective-permute-start.12 = (bf16[2,64,1024]{2,1,0:T(8,128)(2,1)S(1)}, bf16[2,64,1024]{2,1,0:T(8,128)(2,1)S(1)}, u32[]{:S(2)}, u32[]{:S(2)}) collective-permute-start(bf16[2,64,1024]{2,1,0:T(8,128)(2,1)S(1)} %add_convert_fusion.6), channel_id=1, source_target_pairs={{0,224},{16,240},{32,0},{48,16},{64,32},{80,48},{96,64},{112,80},{... | collective-permute-start | bytes 786440 | tf_op jit(solution)/shard_map/ppermute | solution.py:281
  50.7 8.4 %collective-permute-start.13 = (bf16[2,64,1024]{2,1,0:T(8,128)(2,1)S(1)}, bf16[2,64,1024]{2,1,0:T(8,128)(2,1)S(1)}, u32[]{:S(2)}, u32[]{:S(2)}) collective-permute-start(bf16[2,64,1024]{2,1,0:T(8,128)(2,1)S(1)} %join.21), channel_id=1, source_target_pairs={{0,32},{16,48},{32,64},{48,80},{64,96},{80,112},{96,128},{112,144}... | collective-permute-start | bytes 786440 | tf_op jit(solution)/shard_map/ppermute | solution.py:281
  53.4 18.5 %collective-permute-start.10 = (bf16[512,1024]{1,0:T(8,128)(2,1)S(1)}, bf16[512,1024]{1,0:T(8,128)(2,1)S(1)}, u32[]{:S(2)}, u32[]{:S(2)}) collective-permute-start(bf16[512,1024]{1,0:T(8,128)(2,1)S(1)} %get-tuple-element.38.wait.refs_2_), channel_id=1, source_target_pairs={{0,16},{16,0},{32,48},{48,32},{64,80},{80,64},{96,112},{112,96},{1... | collective-permute-start | bytes 3145736 | tf_op jit(solution)/shard_map/ppermute | solution.py:291
  59.2 7.9 %collective-permute-start.14 = (bf16[2,64,1024]{2,1,0:T(8,128)(2,1)S(1)}, bf16[2,64,1024]{2,1,0:T(8,128)(2,1)S(1)}, u32[]{:S(2)}, u32[]{:S(2)}) collective-permute-start(bf16[2,64,1024]{2,1,0:T(8,128)(2,1)S(1)} %add_convert_fusion.5), channel_id=1, source_target_pairs={{0,224},{16,240},{32,0},{48,16},{64,32},{80,48},{96,64},{112,80},{... | collective-permute-start | bytes 786440 | tf_op jit(solution)/shard_map/ppermute | solution.py:286
  59.9 9.7 %collective-permute-start.15 = (bf16[2,64,1024]{2,1,0:T(8,128)(2,1)S(1)}, bf16[2,64,1024]{2,1,0:T(8,128)(2,1)S(1)}, u32[]{:S(2)}, u32[]{:S(2)}) collective-permute-start(bf16[2,64,1024]{2,1,0:T(8,128)(2,1)S(1)} %add_convert_fusion.4), channel_id=1, source_target_pairs={{0,32},{16,48},{32,64},{48,80},{64,96},{80,112},{96,128},{112,144}... | collective-permute-start | bytes 786440 | tf_op jit(solution)/shard_map/ppermute | solution.py:286
  69.7 7.7 %collective-permute-start.16 = (bf16[2,64,1024]{2,1,0:T(8,128)(2,1)S(1)}, bf16[2,64,1024]{2,1,0:T(8,128)(2,1)S(1)}, u32[]{:S(2)}, u32[]{:S(2)}) collective-permute-start(bf16[2,64,1024]{2,1,0:T(8,128)(2,1)S(1)} %add_convert_fusion.3), channel_id=1, source_target_pairs={{0,224},{16,240},{32,0},{48,16},{64,32},{80,48},{96,64},{112,80},{... | collective-permute-start | bytes 786440 | tf_op jit(solution)/shard_map/ppermute | solution.py:289
  70.0 8.9 %collective-permute-start.17 = (bf16[2,64,1024]{2,1,0:T(8,128)(2,1)S(1)}, bf16[2,64,1024]{2,1,0:T(8,128)(2,1)S(1)}, u32[]{:S(2)}, u32[]{:S(2)}) collective-permute-start(bf16[2,64,1024]{2,1,0:T(8,128)(2,1)S(1)} %add_convert_fusion.2), channel_id=1, source_target_pairs={{0,32},{16,48},{32,64},{48,80},{64,96},{80,112},{96,128},{112,144}... | collective-permute-start | bytes 786440 | tf_op jit(solution)/shard_map/ppermute | solution.py:289
  72.5 7.2 %copy-start = (bf16[512,1024]{1,0:T(8,128)(2,1)}, bf16[512,1024]{1,0:T(8,128)(2,1)S(1)}, u32[]{:S(2)}) copy-start(bf16[512,1024]{1,0:T(8,128)(2,1)S(1)} %add_convert_fusion.refs_1_) | copy-start | bytes 3145732

commit v3 on v2

--- a/solution.py
+++ b/solution.py
@@ -245,7 +245,6 @@
 
 
 UP = [(at(z, core), at(z + 1, core)) for z in range(CHIPS) for core in (0, 1)]
-FAR = [(at(z, core), at(z + 4, core)) for z in range(CHIPS - 4) for core in (0, 1)]
 DOWN = [(at(z, core), at(z - 1, core)) for z in range(CHIPS) for core in (0, 1)]
 
 
@@ -256,40 +255,39 @@
     place = jnp.stack([ctx // 2, ctx % 2, beacon_reach[0].astype(jnp.int32)])
     send = functools.partial(lax.ppermute, axis_name="ctx")
     own = jnp.stack([beacon_keys, beacon_values])
-    a1, b1, d4 = send(own, perm=UP), send(own, perm=DOWN), send(own, perm=FAR)
+    a1, b1 = send(own, perm=UP), send(own, perm=DOWN)
     queries_other, grad_other = send(queries, perm=SWAP), send(out_grad, perm=SWAP)
     q_home, k_home, v_home, g_home, stats = stats_call(
         place, (queries, keys, values, out_grad, forward_out, log_norm)
     )
     sides = (q_home, queries_other, g_home, grad_other, stats, send(stats, perm=SWAP))
-    a1, b1 = both(a1, b1, stats)
+    a1, b1 = both(a1, b1, sides[5])
     a2, b2 = send(a1, perm=UP), send(b1, perm=DOWN)
     t1a, t1b, t0, ds1 = beacon_call(
         place, sides, ((a1, -1, F32), (b1, 1 - CHIPS, F32), (own, 0, F32)), (), "beacons_near"
     )
     a2, b2 = both(a2, b2, ds1)
     a3, b3 = send(a2, perm=UP), send(b2, perm=DOWN)
-    t4, ds4 = beacon_call(place, sides, ((d4, -4, BF),), (a2, b2), "beacons_far")
-    a3, b3 = both(a3, b3, t4)
+    t2a, t2b, ds2 = beacon_call(place, sides, ((a2, -2, F32), (b2, 2 - CHIPS, F32)), (), "beacons_second")
+    a3, b3 = both(a3, b3, ds2)
+    a4 = send(a3, perm=UP)
+    t4, ds4 = beacon_call(place, sides, ((a4, -4, BF),), (), "beacons_far")
 
     def plus(arrived, term):
         return (arrived.astype(F32) + term).astype(BF)
 
     a = send(t4, perm=DOWN)
     t3a, b, ds3 = beacon_call(place, sides, ((a3, -3, F32), (b3, 3 - CHIPS, BF)), (t4,), "beacons_third")
-    a, b = both(a, b)
+    dq_home, dq_other = query_call((ds1, ds2, ds3, ds4), (a1, b1, own, a2, b2, a3, b3, a4))
+    a, b = both(a, b, dq_other)
     a, b = send(plus(a, t3a), perm=DOWN), send(b, perm=UP)
-    t2a, t2b, ds2 = beacon_call(
-        place, sides, ((a2, -2, F32), (b2, 2 - CHIPS, F32)), (t3a,), "beacons_second"
-    )
-    a, b = both(a, b, ds2)
+    dq_raw, key_grad, value_grad = raw_call(q_home, k_home, v_home, g_home, stats, dq_other)
+    a, b = both(a, b, dq_raw)
     a, b = send(plus(a, t2a), perm=DOWN), send(plus(b, t2b), perm=UP)
-    dq_home, dq_other = query_call((ds1, ds2, ds3, ds4), (a1, b1, own, a2, b2, a3, b3, d4))
-    a, b = both(a, b, dq_other)
+    query_grad = (dq_raw + dq_home + send(dq_other, perm=SWAP).astype(F32)).astype(BF)
+    a, b = both(a, b, query_grad)
     a, b = send(plus(a, t1a), perm=DOWN), send(plus(b, t1b), perm=UP)
-    dq_raw, key_grad, value_grad = raw_call(q_home, k_home, v_home, g_home, stats, dq_other)
-    query_grad = (dq_raw + dq_home + send(dq_other, perm=SWAP).astype(F32)).astype(BF)
-    total = (join(t0, query_grad) + (a.astype(F32) + b.astype(F32))).astype(BF)
+    total = (t0 + (a.astype(F32) + b.astype(F32))).astype(BF)
     return query_grad, key_grad, value_grad, total[0], total[1]
 
 

time: 79.8 us -> 77.6 us (0.972)
  starting transfers between devices: 30.6 us -> 24.9 us
  waiting for transfers between devices: 27.3 us -> 30.5 us
    ppermute x1, starting transfers between devices: 9.19 us -> 2.48 us  [local(): a = send(t4, perm=DOWN)]
    ppermute x2, waiting for transfers between devices: 5.62 us -> 0.01 us  [local(): a, b = (send(plus(a, t3a), perm=DOWN), send(b, perm=UP))]
    ppermute x3, waiting for transfers between devices: 5.4 us -> 10.7 us  [the longest x1 6.64 us: local(): a4 = send(a3, perm=UP)]
    ppermute x1, waiting for transfers between devices: 4.09 us -> 1.16 us  [local(): a = send(t4, perm=DOWN)]
    ppermute x2, waiting for transfers between devices: 2.14 us -> 4.9 us  [local(): a3, b3 = (send(a2, perm=UP), send(b2, perm=DOWN))]
    ppermute x3, starting transfers between devices: 9.55 us -> 6.87 us  [the longest x2 5.93 us: local(): a1, b1 = (send(own, perm=UP), send(own, perm=DOWN))]
    ppermute x2, waiting for transfers between devices: 0.01 us -> 2.16 us  [local(): a2, b2 = (send(a1, perm=UP), send(b1, perm=DOWN))]
    ppermute x2, waiting for transfers between devices: 2.54 us -> 4.58 us  [local(): a, b = (send(plus(a, t2a), perm=DOWN), send(plus(b, t2b), perm=UP))]
  transfers between devices with their start and end apart: 18 -> 18, of which waited for: 10 -> 13; matrix products, arithmetic and copies ran while one was open for 2% -> 2% of each run, Pallas kernels for 22% -> 22%
where the time goes in v3:
time: 77.6 us; the launch traced here: 77 us
  waiting for transfers between devices  30.5 us (39%)
  starting transfers between devices  24.9 us (32%)
  Pallas kernels  17.3 us (22%)
  other arithmetic  2.1 us (3%)
  between operations  1.48 us (2%)
    pallas_call x4, Pallas kernels, beacon_call(): pl.pallas_call(functools.partial(beacon_kernel, shifts, len(waits)), in_s...  6.8 us
    ppermute x1, waiting for transfers between devices, local(): a4 = send(a3, perm=UP)  6.64 us
    ppermute x2, starting transfers between devices, local(): a1, b1 = (send(own, perm=UP), send(own, perm=DOWN))  5.93 us
    ppermute x2, waiting for transfers between devices, local(): a, b = (send(plus(a, t1a), perm=DOWN), send(plus(b, t1b), perm=UP))  5.77 us
    pallas_call x1, Pallas kernels, raw_call(): pl.pallas_call(raw_kernel, in_specs=[VMEM] * 5 + [ANY], out_specs=[VMEM]...  5.68 us
    ppermute x2, waiting for transfers between devices, local(): a3, b3 = (send(a2, perm=UP), send(b2, perm=DOWN))  4.9 us
    ppermute x2, waiting for transfers between devices, local(): a, b = (send(plus(a, t2a), perm=DOWN), send(plus(b, t2b), perm=UP))  4.58 us
    ppermute x2, waiting for transfers between devices, local(): a1, b1 = (send(own, perm=UP), send(own, perm=DOWN))  4.08 us
  transfers between devices with their start and end apart: 18, of which 13 were waited for; matrix products, arithmetic and copies ran while one was open for 2% of the time, Pallas kernels for 22%

profile of v3, /device:TPU:6, one launch (start us, length us, event | category | flops | bytes accessed | tf_op | source)
XLA Modules:
  0.0 77.0 jit_solution(5563989799380261846)
XLA Ops:
  0.6 0.1 collective-permute-start
  0.7 0.5 collective-permute-start.1
  1.2 1.0 %pad_maximum_fusion.refs_2_.refs_6_ = bf16[2,64,1024]{2,1,0:T(8,128)(2,1)S(1)} fusion(bf16[1,64,1024]{2,1,0:T(8,128)(2,1)} %bitcast.8, bf16[1,64,1024]{2,1,0:T(8,128)(2,1)} %bitcast.9), kind=kLoop, calls=%fused_computation.7 | loop fusion | flops 131072 | bytes 524288 | tf_op jit(solution)/shard_map/stack | solution.py:257
  2.2 5.9 %collective-permute-start.4 = (bf16[2,64,1024]{2,1,0:T(8,128)(2,1)S(1)}, bf16[2,64,1024]{2,1,0:T(8,128)(2,1)S(1)}, u32[]{:S(2)}, u32[]{:S(2)}) collective-permute-start(bf16[2,64,1024]{2,1,0:T(8,128)(2,1)S(1)} %pad_maximum_fusion.refs_2_.refs_6_), channel_id=1, source_target_pairs={{0,224},{16,240},{32,0},{48,16},{64,32},{80,48},{96,64},{112,80},{... | collective-permute-start | bytes 786440 | tf_op jit(solution)/shard_map/ppermute | solution.py:258
  8.2 0.0 collective-permute-start.3
  8.8 0.1 pad_add_fusion.place
  8.9 3.1 %stats.1 = (bf16[512,1024]{1,0:T(8,128)(2,1)S(1)}, bf16[512,1024]{1,0:T(8,128)(2,1)S(1)}, bf16[512,1024]{1,0:T(8,128)(2,1)S(1)}, bf16[512,1024]{1,0:T(8,128)(2,1)S(1)}, f32[3,8,512]{2,1,0:T(8,128)S(1)}) custom-call(s32[3]{0:T(128)S(1)} %pad_add_fusion.place, bf16[512,1024]{1,0:T(8,128)(2,1)} %q_any.1, bf16[512,1024]{1,0:T(8,128)(2,1)} %k_any.1, ...), custom_call_target="tpu_custom_call" | custom-call | flops 1048576 | bytes 8388608 | tf_op jit(solution)/shard_map/stats/pallas_call | solution.py:88
  12.0 0.1 collective-permute-start.2
  12.1 1.2 %collective-permute-done.2.refs_2_.sp_ref = f32[3,8,512]{2,1,0:T(8,128)S(1)} collective-permute-done((f32[3,8,512]{2,1,0:T(8,128)S(1)}, f32[3,8,512]{2,1,0:T(8,128)S(1)}, u32[]{:S(2)}, u32[]{:S(2)}) %collective-permute-start.2) | collective-permute-done | bytes 49184 | tf_op jit(solution)/shard_map/ppermute | solution.py:263
  13.3 0.7 collective-permute-done.4.refs_1_.refs_0_
  14.0 3.4 %collective-permute-done.3.refs_0_ = bf16[2,64,1024]{2,1,0:T(8,128)(2,1)S(1)} collective-permute-done((bf16[2,64,1024]{2,1,0:T(8,128)(2,1)S(1)}, bf16[2,64,1024]{2,1,0:T(8,128)(2,1)S(1)}, u32[]{:S(2)}, u32[]{:S(2)}) %collective-permute-start.3) | collective-permute-done | bytes 262176 | tf_op jit(solution)/shard_map/ppermute | solution.py:258
  17.4 0.3 collective-permute-start.6
  17.7 1.7 %collective-permute-start.5 = (bf16[2,64,1024]{2,1,0:T(8,128)(2,1)S(1)}, bf16[2,64,1024]{2,1,0:T(8,128)(2,1)S(1)}, u32[]{:S(2)}, u32[]{:S(2)}) collective-permute-start(bf16[2,64,1024]{2,1,0:T(8,128)(2,1)S(1)} %join.12.refs_1_.refs_0_.refs_4_), channel_id=1, source_target_pairs={{0,32},{16,48},{32,64},{48,80},{64,96},{80,112},{96,128},{112,144}... | collective-permute-start | bytes 786440 | tf_op jit(solution)/shard_map/ppermute | solution.py:265
  19.4 0.0 collective-permute-done.qp_ref
  19.4 0.0 collective-permute-done.1.gp_ref
  19.4 4.5 %beacons_near.1 = (f32[2,64,1024]{2,1,0:T(8,128)S(1)}, f32[2,64,1024]{2,1,0:T(8,128)S(1)}, f32[2,64,1024]{2,1,0:T(8,128)S(1)}, bf16[8,192,1024]{2,1,0:T(8,128)(2,1)S(1)}) custom-call(s32[3]{0:T(128)S(1)} %pad_add_fusion.place, bf16[512,1024]{1,0:T(8,128)(2,1)S(1)} %get-tuple-element.27.qh_ref.q_ref, bf16[512,1024]{1,0:T(8,128)(2,1)S(1)} %collective-permute-done.qp_ref, ...), custom_call_target="tpu_custom_call" | custom-call | flops 1610612736 | bytes 8388608 | tf_op jit(solution)/shard_map/beacons_near/pallas_call | solution.py:185
  23.9 0.6 collective-permute-done.6.refs_1_.refs_0_
  24.6 1.5 %collective-permute-done.5.refs_0_ = bf16[2,64,1024]{2,1,0:T(8,128)(2,1)S(1)} collective-permute-done((bf16[2,64,1024]{2,1,0:T(8,128)(2,1)S(1)}, bf16[2,64,1024]{2,1,0:T(8,128)(2,1)S(1)}, u32[]{:S(2)}, u32[]{:S(2)}) %collective-permute-start.5) | collective-permute-done | bytes 262176 | tf_op jit(solution)/shard_map/ppermute | solution.py:265
  26.1 0.3 collective-permute-start.8
  26.4 1.7 %collective-permute-start.7 = (bf16[2,64,1024]{2,1,0:T(8,128)(2,1)S(1)}, bf16[2,64,1024]{2,1,0:T(8,128)(2,1)S(1)}, u32[]{:S(2)}, u32[]{:S(2)}) collective-permute-start(bf16[2,64,1024]{2,1,0:T(8,128)(2,1)S(1)} %join.14.refs_1_.refs_0_.refs_7_), channel_id=1, source_target_pairs={{0,32},{16,48},{32,64},{48,80},{64,96},{80,112},{96,128},{112,144}... | collective-permute-start | bytes 786440 | tf_op jit(solution)/shard_map/ppermute | solution.py:270
  28.1 0.9 %beacons_second.1 = (f32[2,64,1024]{2,1,0:T(8,128)S(1)}, f32[2,64,1024]{2,1,0:T(8,128)S(1)}, bf16[8,128,1024]{2,1,0:T(8,128)(2,1)S(1)}) custom-call(s32[3]{0:T(128)S(1)} %pad_add_fusion.place, bf16[512,1024]{1,0:T(8,128)(2,1)S(1)} %get-tuple-element.27.qh_ref.q_ref, bf16[512,1024]{1,0:T(8,128)(2,1)S(1)} %collective-permute-done.qp_ref, ...), custom_call_target="tpu_custom_call" | custom-call | flops 1073741824 | bytes 8388608 | tf_op jit(solution)/shard_map/beacons_second/pallas_call | solution.py:185
  29.1 3.4 %collective-permute-done.8.refs_1_.refs_0_ = bf16[2,64,1024]{2,1,0:T(8,128)(2,1)S(1)} collective-permute-done((bf16[2,64,1024]{2,1,0:T(8,128)(2,1)S(1)}, bf16[2,64,1024]{2,1,0:T(8,128)(2,1)S(1)}, u32[]{:S(2)}, u32[]{:S(2)}) %collective-permute-start.8) | collective-permute-done | bytes 262176 | tf_op jit(solution)/shard_map/ppermute | solution.py:270
  32.5 1.5 %collective-permute-done.7.refs_0_ = bf16[2,64,1024]{2,1,0:T(8,128)(2,1)S(1)} collective-permute-done((bf16[2,64,1024]{2,1,0:T(8,128)(2,1)S(1)}, bf16[2,64,1024]{2,1,0:T(8,128)(2,1)S(1)}, u32[]{:S(2)}, u32[]{:S(2)}) %collective-permute-start.7) | collective-permute-done | bytes 262176 | tf_op jit(solution)/shard_map/ppermute | solution.py:270
  34.0 0.9 %collective-permute-start.9 = (bf16[2,64,1024]{2,1,0:T(8,128)(2,1)S(1)}, bf16[2,64,1024]{2,1,0:T(8,128)(2,1)S(1)}, u32[]{:S(2)}, u32[]{:S(2)}) collective-permute-start(bf16[2,64,1024]{2,1,0:T(8,128)(2,1)S(1)} %join.16.refs_1_.refs_0_.refs_9_), channel_id=1, source_target_pairs={{0,32},{16,48},{32,64},{48,80},{64,96},{80,112},{96,128},{112,144}... | collective-permute-start | bytes 786440 | tf_op jit(solution)/shard_map/ppermute | solution.py:273
  34.9 6.6 %collective-permute-done.9.refs_0_.refs_11_ = bf16[2,64,1024]{2,1,0:T(8,128)(2,1)S(1)} collective-permute-done((bf16[2,64,1024]{2,1,0:T(8,128)(2,1)S(1)}, bf16[2,64,1024]{2,1,0:T(8,128)(2,1)S(1)}, u32[]{:S(2)}, u32[]{:S(2)}) %collective-permute-start.9) | collective-permute-done | bytes 262176 | tf_op jit(solution)/shard_map/ppermute | solution.py:273
  41.5 0.6 beacons_far.1
  42.2 2.5 %collective-permute-start.11 = (bf16[2,64,1024]{2,1,0:T(8,128)(2,1)S(1)}, bf16[2,64,1024]{2,1,0:T(8,128)(2,1)S(1)}, u32[]{:S(2)}, u32[]{:S(2)}) collective-permute-start(bf16[2,64,1024]{2,1,0:T(8,128)(2,1)S(1)} %get-tuple-element.34.refs_2_), channel_id=1, source_target_pairs={{0,224},{16,240},{32,0},{48,16},{64,32},{80,48},{96,64},{112,80},{... | collective-permute-start | bytes 786440 | tf_op jit(solution)/shard_map/ppermute | solution.py:279
  44.7 0.7 beacons_third.1
  45.4 1.7 %query_grad.1 = (f32[512,1024]{1,0:T(8,128)S(1)}, bf16[512,1024]{1,0:T(8,128)(2,1)S(1)}) custom-call(bf16[8,192,1024]{2,1,0:T(8,128)(2,1)S(1)} %get-tuple-element.32.refs_2_.refs_0_, bf16[8,128,1024]{2,1,0:T(8,128)(2,1)S(1)} %get-tuple-element.33.refs_2_.refs_1_, bf16[8,128,1024]{2,1,0:T(8,128)(2,1)S(1)} %get-tuple-element.35.refs_2_, ...), custom_call_target="tpu_custom_call" | custom-call | flops 1073741824 | bytes 16777216 | tf_op jit(solution)/shard_map/query_grad/pallas_call | solution.py:210
  47.2 0.3 collective-permute-start.10
  47.5 1.2 %collective-permute-done.11.refs_0_ = bf16[2,64,1024]{2,1,0:T(8,128)(2,1)S(1)} collective-permute-done((bf16[2,64,1024]{2,1,0:T(8,128)(2,1)S(1)}, bf16[2,64,1024]{2,1,0:T(8,128)(2,1)S(1)}, u32[]{:S(2)}, u32[]{:S(2)}) %collective-permute-start.11) | collective-permute-done | bytes 262176 | tf_op jit(solution)/shard_map/ppermute | solution.py:279
  48.6 0.1 add_convert_fusion.6
  48.7 0.1 collective-permute-start.13
  48.8 3.7 %collective-permute-start.12 = (bf16[2,64,1024]{2,1,0:T(8,128)(2,1)S(1)}, bf16[2,64,1024]{2,1,0:T(8,128)(2,1)S(1)}, u32[]{:S(2)}, u32[]{:S(2)}) collective-permute-start(bf16[2,64,1024]{2,1,0:T(8,128)(2,1)S(1)} %add_convert_fusion.6), channel_id=1, source_target_pairs={{0,224},{16,240},{32,0},{48,16},{64,32},{80,48},{96,64},{112,80},{... | collective-permute-start | bytes 786440 | tf_op jit(solution)/shard_map/ppermute | solution.py:283
  52.5 5.7 %raw_tokens.1 = (f32[512,1024]{1,0:T(8,128)S(1)}, bf16[512,1024]{1,0:T(8,128)(2,1)}, bf16[512,1024]{1,0:T(8,128)(2,1)}) custom-call(bf16[512,1024]{1,0:T(8,128)(2,1)S(1)} %get-tuple-element.27.qh_ref.q_ref, bf16[512,1024]{1,0:T(8,128)(2,1)S(1)} %get-tuple-element.28.k_ref, bf16[512,1024]{1,0:T(8,128)(2,1)S(1)} %get-tuple-element.29.v_ref, ...), custom_call_target="tpu_custom_call" | custom-call | flops 2684354560 | bytes 10485760 | tf_op jit(solution)/shard_map/raw_tokens/pallas_call | solution.py:110
  58.2 0.0 collective-permute-done.13.refs_1_.refs_0_
  58.2 0.0 collective-permute-done.12.refs_0_
  58.2 0.1 add_convert_fusion.4
  58.3 0.1 collective-permute-start.15
  58.4 0.1 add_convert_fusion.5
  58.4 3.3 %collective-permute-start.14 = (bf16[2,64,1024]{2,1,0:T(8,128)(2,1)S(1)}, bf16[2,64,1024]{2,1,0:T(8,128)(2,1)S(1)}, u32[]{:S(2)}, u32[]{:S(2)}) collective-permute-start(bf16[2,64,1024]{2,1,0:T(8,128)(2,1)S(1)} %add_convert_fusion.5), channel_id=1, source_target_pairs={{0,224},{16,240},{32,0},{48,16},{64,32},{80,48},{96,64},{112,80},{... | collective-permute-start | bytes 786440 | tf_op jit(solution)/shard_map/ppermute | solution.py:286
  61.7 0.0 collective-permute-done.10
  61.7 0.6 add_convert_fusion.refs_2_
  62.4 0.0 copy-start
  62.4 3.8 %collective-permute-done.15.refs_1_.refs_0_ = bf16[2,64,1024]{2,1,0:T(8,128)(2,1)S(1)} collective-permute-done((bf16[2,64,1024]{2,1,0:T(8,128)(2,1)S(1)}, bf16[2,64,1024]{2,1,0:T(8,128)(2,1)S(1)}, u32[]{:S(2)}, u32[]{:S(2)}) %collective-permute-start.15) | collective-permute-done | bytes 262176 | tf_op jit(solution)/shard_map/ppermute | solution.py:286
  66.2 0.8 collective-permute-done.14.refs_0_
  67.0 0.1 add_convert_fusion.3
  67.0 0.1 add_convert_fusion.2
  67.1 0.0 copy-done
  67.1 2.7 %collective-permute-start.17 = (bf16[2,64,1024]{2,1,0:T(8,128)(2,1)S(1)}, bf16[2,64,1024]{2,1,0:T(8,128)(2,1)S(1)}, u32[]{:S(2)}, u32[]{:S(2)}) collective-permute-start(bf16[2,64,1024]{2,1,0:T(8,128)(2,1)S(1)} %add_convert_fusion.2), channel_id=1, source_target_pairs={{0,32},{16,48},{32,64},{48,80},{64,96},{80,112},{96,128},{112,144}... | collective-permute-start | bytes 786440 | tf_op jit(solution)/shard_map/ppermute | solution.py:289
  69.8 0.6 collective-permute-start.16
  70.4 4.3 %collective-permute-done.17 = bf16[2,64,1024]{2,1,0:T(8,128)(2,1)S(1)} collective-permute-done((bf16[2,64,1024]{2,1,0:T(8,128)(2,1)S(1)}, bf16[2,64,1024]{2,1,0:T(8,128)(2,1)S(1)}, u32[]{:S(2)}, u32[]{:S(2)}) %collective-permute-start.17) | collective-permute-done | bytes 262176 | tf_op jit(solution)/shard_map/ppermute | solution.py:289
  74.8 1.4 %collective-permute-done.16 = bf16[2,64,1024]{2,1,0:T(8,128)(2,1)S(1)} collective-permute-done((bf16[2,64,1024]{2,1,0:T(8,128)(2,1)S(1)}, bf16[2,64,1024]{2,1,0:T(8,128)(2,1)S(1)}, u32[]{:S(2)}, u32[]{:S(2)}) %collective-permute-start.16) | collective-permute-done | bytes 262176 | tf_op jit(solution)/shard_map/ppermute | solution.py:289
  76.2 0.1 add_convert_fusion.1
  76.3 0.7 slice_bitcast_fusion
  (12 shorter events, 0.0 us)
Async XLA Ops:
  0.6 18.8 %collective-permute-start = (bf16[512,1024]{1,0:T(8,128)(2,1)}, bf16[512,1024]{1,0:T(8,128)(2,1)S(1)}, u32[]{:S(2)}, u32[]{:S(2)}) collective-permute-start(bf16[512,1024]{1,0:T(8,128)(2,1)} %q_any.1), channel_id=1, source_target_pairs={{0,16},{16,0},{32,48},{48,32},{64,80},{80,64},{96,112},{112,96},{1... | collective-permute-start | bytes 3145736 | tf_op jit(solution)/shard_map/ppermute | solution.py:259
  0.7 18.7 %collective-permute-start.1 = (bf16[512,1024]{1,0:T(8,128)(2,1)}, bf16[512,1024]{1,0:T(8,128)(2,1)S(1)}, u32[]{:S(2)}, u32[]{:S(2)}) collective-permute-start(bf16[512,1024]{1,0:T(8,128)(2,1)} %g_any.1), channel_id=1, source_target_pairs={{0,16},{16,0},{32,48},{48,32},{64,80},{80,64},{96,112},{112,96},{1... | collective-permute-start | bytes 3145736 | tf_op jit(solution)/shard_map/ppermute | solution.py:259
  2.2 11.8 %collective-permute-start.4 = (bf16[2,64,1024]{2,1,0:T(8,128)(2,1)S(1)}, bf16[2,64,1024]{2,1,0:T(8,128)(2,1)S(1)}, u32[]{:S(2)}, u32[]{:S(2)}) collective-permute-start(bf16[2,64,1024]{2,1,0:T(8,128)(2,1)S(1)} %pad_maximum_fusion.refs_2_.refs_6_), channel_id=1, source_target_pairs={{0,224},{16,240},{32,0},{48,16},{64,32},{80,48},{96,64},{112,80},{... | collective-permute-start | bytes 786440 | tf_op jit(solution)/shard_map/ppermute | solution.py:258
  8.2 9.2 %collective-permute-start.3 = (bf16[2,64,1024]{2,1,0:T(8,128)(2,1)S(1)}, bf16[2,64,1024]{2,1,0:T(8,128)(2,1)S(1)}, u32[]{:S(2)}, u32[]{:S(2)}) collective-permute-start(bf16[2,64,1024]{2,1,0:T(8,128)(2,1)S(1)} %pad_maximum_fusion.refs_2_.refs_6_), channel_id=1, source_target_pairs={{0,32},{16,48},{32,64},{48,80},{64,96},{80,112},{96,128},{112,144}... | collective-permute-start | bytes 786440 | tf_op jit(solution)/shard_map/ppermute | solution.py:258
  12.0 1.3 %collective-permute-start.2 = (f32[3,8,512]{2,1,0:T(8,128)S(1)}, f32[3,8,512]{2,1,0:T(8,128)S(1)}, u32[]{:S(2)}, u32[]{:S(2)}) collective-permute-start(f32[3,8,512]{2,1,0:T(8,128)S(1)} %get-tuple-element.31.sh_ref.st_ref), channel_id=1, source_target_pairs={{0,16},{16,0},{32,48},{48,32},{64,80},{80,64},{96,112},{112,96},{1... | collective-permute-start | bytes 147464 | tf_op jit(solution)/shard_map/ppermute | solution.py:263
  17.4 7.2 %collective-permute-start.6 = (bf16[2,64,1024]{2,1,0:T(8,128)(2,1)S(1)}, bf16[2,64,1024]{2,1,0:T(8,128)(2,1)S(1)}, u32[]{:S(2)}, u32[]{:S(2)}) collective-permute-start(bf16[2,64,1024]{2,1,0:T(8,128)(2,1)S(1)} %join.13.refs_1_.refs_5_), channel_id=1, source_target_pairs={{0,224},{16,240},{32,0},{48,16},{64,32},{80,48},{96,64},{112,80},{... | collective-permute-start | bytes 786440 | tf_op jit(solution)/shard_map/ppermute | solution.py:265
  17.7 8.4 %collective-permute-start.5 = (bf16[2,64,1024]{2,1,0:T(8,128)(2,1)S(1)}, bf16[2,64,1024]{2,1,0:T(8,128)(2,1)S(1)}, u32[]{:S(2)}, u32[]{:S(2)}) collective-permute-start(bf16[2,64,1024]{2,1,0:T(8,128)(2,1)S(1)} %join.12.refs_1_.refs_0_.refs_4_), channel_id=1, source_target_pairs={{0,32},{16,48},{32,64},{48,80},{64,96},{80,112},{96,128},{112,144}... | collective-permute-start | bytes 786440 | tf_op jit(solution)/shard_map/ppermute | solution.py:265
  26.1 6.4 %collective-permute-start.8 = (bf16[2,64,1024]{2,1,0:T(8,128)(2,1)S(1)}, bf16[2,64,1024]{2,1,0:T(8,128)(2,1)S(1)}, u32[]{:S(2)}, u32[]{:S(2)}) collective-permute-start(bf16[2,64,1024]{2,1,0:T(8,128)(2,1)S(1)} %join.15.refs_1_.refs_8_), channel_id=1, source_target_pairs={{0,224},{16,240},{32,0},{48,16},{64,32},{80,48},{96,64},{112,80},{... | collective-permute-start | bytes 786440 | tf_op jit(solution)/shard_map/ppermute | solution.py:270
  26.4 7.6 %collective-permute-start.7 = (bf16[2,64,1024]{2,1,0:T(8,128)(2,1)S(1)}, bf16[2,64,1024]{2,1,0:T(8,128)(2,1)S(1)}, u32[]{:S(2)}, u32[]{:S(2)}) collective-permute-start(bf16[2,64,1024]{2,1,0:T(8,128)(2,1)S(1)} %join.14.refs_1_.refs_0_.refs_7_), channel_id=1, source_target_pairs={{0,32},{16,48},{32,64},{48,80},{64,96},{80,112},{96,128},{112,144}... | collective-permute-start | bytes 786440 | tf_op jit(solution)/shard_map/ppermute | solution.py:270
  34.0 7.6 %collective-permute-start.9 = (bf16[2,64,1024]{2,1,0:T(8,128)(2,1)S(1)}, bf16[2,64,1024]{2,1,0:T(8,128)(2,1)S(1)}, u32[]{:S(2)}, u32[]{:S(2)}) collective-permute-start(bf16[2,64,1024]{2,1,0:T(8,128)(2,1)S(1)} %join.16.refs_1_.refs_0_.refs_9_), channel_id=1, source_target_pairs={{0,32},{16,48},{32,64},{48,80},{64,96},{80,112},{96,128},{112,144}... | collective-permute-start | bytes 786440 | tf_op jit(solution)/shard_map/ppermute | solution.py:273
  42.2 6.5 %collective-permute-start.11 = (bf16[2,64,1024]{2,1,0:T(8,128)(2,1)S(1)}, bf16[2,64,1024]{2,1,0:T(8,128)(2,1)S(1)}, u32[]{:S(2)}, u32[]{:S(2)}) collective-permute-start(bf16[2,64,1024]{2,1,0:T(8,128)(2,1)S(1)} %get-tuple-element.34.refs_2_), channel_id=1, source_target_pairs={{0,224},{16,240},{32,0},{48,16},{64,32},{80,48},{96,64},{112,80},{... | collective-permute-start | bytes 786440 | tf_op jit(solution)/shard_map/ppermute | solution.py:279
  47.2 14.6 %collective-permute-start.10 = (bf16[512,1024]{1,0:T(8,128)(2,1)S(1)}, bf16[512,1024]{1,0:T(8,128)(2,1)S(1)}, u32[]{:S(2)}, u32[]{:S(2)}) collective-permute-start(bf16[512,1024]{1,0:T(8,128)(2,1)S(1)} %get-tuple-element.37.wait.refs_2_), channel_id=1, source_target_pairs={{0,16},{16,0},{32,48},{48,32},{64,80},{80,64},{96,112},{112,96},{1... | collective-permute-start | bytes 3145736 | tf_op jit(solution)/shard_map/ppermute | solution.py:287
  48.7 9.5 %collective-permute-start.13 = (bf16[2,64,1024]{2,1,0:T(8,128)(2,1)S(1)}, bf16[2,64,1024]{2,1,0:T(8,128)(2,1)S(1)}, u32[]{:S(2)}, u32[]{:S(2)}) collective-permute-start(bf16[2,64,1024]{2,1,0:T(8,128)(2,1)S(1)} %join.19), channel_id=1, source_target_pairs={{0,32},{16,48},{32,64},{48,80},{64,96},{80,112},{96,128},{112,144}... | collective-permute-start | bytes 786440 | tf_op jit(solution)/shard_map/ppermute | solution.py:283
  48.8 9.4 %collective-permute-start.12 = (bf16[2,64,1024]{2,1,0:T(8,128)(2,1)S(1)}, bf16[2,64,1024]{2,1,0:T(8,128)(2,1)S(1)}, u32[]{:S(2)}, u32[]{:S(2)}) collective-permute-start(bf16[2,64,1024]{2,1,0:T(8,128)(2,1)S(1)} %add_convert_fusion.6), channel_id=1, source_target_pairs={{0,224},{16,240},{32,0},{48,16},{64,32},{80,48},{96,64},{112,80},{... | collective-permute-start | bytes 786440 | tf_op jit(solution)/shard_map/ppermute | solution.py:283
  58.3 7.9 %collective-permute-start.15 = (bf16[2,64,1024]{2,1,0:T(8,128)(2,1)S(1)}, bf16[2,64,1024]{2,1,0:T(8,128)(2,1)S(1)}, u32[]{:S(2)}, u32[]{:S(2)}) collective-permute-start(bf16[2,64,1024]{2,1,0:T(8,128)(2,1)S(1)} %add_convert_fusion.4), channel_id=1, source_target_pairs={{0,32},{16,48},{32,64},{48,80},{64,96},{80,112},{96,128},{112,144}... | collective-permute-start | bytes 786440 | tf_op jit(solution)/shard_map/ppermute | solution.py:286
  58.4 8.5 %collective-permute-start.14 = (bf16[2,64,1024]{2,1,0:T(8,128)(2,1)S(1)}, bf16[2,64,1024]{2,1,0:T(8,128)(2,1)S(1)}, u32[]{:S(2)}, u32[]{:S(2)}) collective-permute-start(bf16[2,64,1024]{2,1,0:T(8,128)(2,1)S(1)} %add_convert_fusion.5), channel_id=1, source_target_pairs={{0,224},{16,240},{32,0},{48,16},{64,32},{80,48},{96,64},{112,80},{... | collective-permute-start | bytes 786440 | tf_op jit(solution)/shard_map/ppermute | solution.py:286
  62.4 4.7 %copy-start = (bf16[512,1024]{1,0:T(8,128)(2,1)}, bf16[512,1024]{1,0:T(8,128)(2,1)S(1)}, u32[]{:S(2)}) copy-start(bf16[512,1024]{1,0:T(8,128)(2,1)S(1)} %add_convert_fusion.refs_2_) | copy-start | bytes 3145732
  67.1 7.7 %collective-permute-start.17 = (bf16[2,64,1024]{2,1,0:T(8,128)(2,1)S(1)}, bf16[2,64,1024]{2,1,0:T(8,128)(2,1)S(1)}, u32[]{:S(2)}, u32[]{:S(2)}) collective-permute-start(bf16[2,64,1024]{2,1,0:T(8,128)(2,1)S(1)} %add_convert_fusion.2), channel_id=1, source_target_pairs={{0,32},{16,48},{32,64},{48,80},{64,96},{80,112},{96,128},{112,144}... | collective-permute-start | bytes 786440 | tf_op jit(solution)/shard_map/ppermute | solution.py:289
  69.8 6.4 %collective-permute-start.16 = (bf16[2,64,1024]{2,1,0:T(8,128)(2,1)S(1)}, bf16[2,64,1024]{2,1,0:T(8,128)(2,1)S(1)}, u32[]{:S(2)}, u32[]{:S(2)}) collective-permute-start(bf16[2,64,1024]{2,1,0:T(8,128)(2,1)S(1)} %add_convert_fusion.3), channel_id=1, source_target_pairs={{0,224},{16,240},{32,0},{48,16},{64,32},{80,48},{96,64},{112,80},{... | collective-permute-start | bytes 786440 | tf_op jit(solution)/shard_map/ppermute | solution.py:289

commit v4 on v3

--- a/solution.py
+++ b/solution.py
@@ -31,11 +31,21 @@
     return lax.dot_general(a, b, (((0,), (0,)), ((), ())), preferred_element_type=F32)
 
 
+def split(x, y):
+    zero = jnp.zeros_like(x)
+    return jnp.concatenate([jnp.concatenate([x, zero], axis=1), jnp.concatenate([zero, y], axis=1)], axis=0)
+
+
+def stacked(x, y, b):
+    rows = x.shape[0]
+    both_heads = nn(jnp.concatenate([x, y], axis=0), b)
+    return both_heads[:rows, :HD], both_heads[rows:, HD:]
+
+
 def stats_kernel(
-    place, q_any, k_any, v_any, g_any, o_any, ln_any,
-    q_ref, k_ref, v_ref, g_ref, st_ref, o_ref, ln_ref, sems,
+    place, q_any, g_any, o_any, ln_any, q_ref, g_ref, st_ref, o_ref, ln_ref, sems
 ):
-    pairs = ((g_any, g_ref), (o_any, o_ref), (ln_any, ln_ref), (q_any, q_ref), (k_any, k_ref), (v_any, v_ref))
+    pairs = ((g_any, g_ref), (o_any, o_ref), (ln_any, ln_ref), (q_any, q_ref))
     copies = [pltpu.make_async_copy(src, dst, sems.at[i]) for i, (src, dst) in enumerate(pairs)]
     for copy in copies:
         copy.start()
@@ -56,25 +66,34 @@
     tri = lax.broadcasted_iota(jnp.int32, (block, block), 0) <= lax.broadcasted_iota(
         jnp.int32, (block, block), 1
     )
-    for h in range(st_ref.shape[1]):
-        c = slice(h * HD, (h + 1) * HD)
-        q, k, v, g = q_ref[:, c], k_ref[:, c], v_ref[:, c], g_ref[:, c]
-        ln, delta = st_ref[0, h : h + 1, :], st_ref[1, h : h + 1, :]
-        stripes = []
+    for h in range(0, st_ref.shape[1], 2):
+        wide = slice(h * HD, (h + 2) * HD)
+        q, k, v, g = q_ref[:, wide], k_ref[:, wide], v_ref[:, wide], g_ref[:, wide]
+        ks, vs = ([x[:, :HD], x[:, HD:]] for x in (k, v))
+        stripes = [[], []]
         for lo in range(0, GROUP, block):
             hi = lo + block
-            p = jnp.exp2(nt(k[lo:hi], q[lo:]) * (SCALE * LOG2E) - ln[:, lo:])
-            head = jnp.where(tri, p[:, :block], 0.0)
-            p = head if hi == GROUP else jnp.concatenate([head, p[:, block:]], axis=1)
-            ds = (p * (nt(v[lo:hi], g[lo:]) - delta[:, lo:])).astype(BF)
-            dv_ref[lo:hi, c] = nn(p.astype(BF), g[lo:]).astype(BF)
-            dk_ref[lo:hi, c] = (nn(ds, q[lo:]) * SCALE).astype(BF)
-            stripes.append(ds)
-        for lo in range(0, GROUP, block):
-            hi = lo + block
-            parts = [part[:, lo - i * block : hi - i * block] for i, part in enumerate(stripes[: hi // block])]
-            ds = parts[0] if len(parts) == 1 else jnp.concatenate(parts, axis=0)
-            dq_ref[lo:hi, c] = (tn(k[:hi], ds) * SCALE).T
+            s = nt(split(ks[0][lo:hi], ks[1][lo:hi]), q[lo:])
+            d = nt(split(vs[0][lo:hi], vs[1][lo:hi]), g[lo:])
+            weights, dscores = [], []
+            for i in range(2):
+                ln, delta = st_ref[0, h + i : h + i + 1, lo:], st_ref[1, h + i : h + i + 1, lo:]
+                p = jnp.exp2(s[i * block : (i + 1) * block] * (SCALE * LOG2E) - ln)
+                head = jnp.where(tri, p[:, :block], 0.0)
+                p = head if hi == GROUP else jnp.concatenate([head, p[:, block:]], axis=1)
+                dscores.append((p * (d[i * block : (i + 1) * block] - delta)).astype(BF))
+                weights.append(p.astype(BF))
+                stripes[i].append(dscores[i])
+            dv, dk = stacked(*weights, g[lo:]), stacked(*dscores, q[lo:])
+            dv_ref[lo:hi, wide] = jnp.concatenate(dv, axis=1).astype(BF)
+            dk_ref[lo:hi, wide] = (jnp.concatenate(dk, axis=1) * SCALE).astype(BF)
+        for i in range(2):
+            c = slice((h + i) * HD, (h + i + 1) * HD)
+            for lo in range(0, GROUP, block):
+                hi = lo + block
+                parts = [x[:, lo - j * block : hi - j * block] for j, x in enumerate(stripes[i][: hi // block])]
+                ds = parts[0] if len(parts) == 1 else jnp.concatenate(parts, axis=0)
+                dq_ref[lo:hi, c] = (tn(ks[i][:hi], ds) * SCALE).T
 
 
 SMEM = pl.BlockSpec(memory_space=pltpu.SMEM)
@@ -87,14 +106,14 @@
     wide = (GROUP, heads * HD)
     return pl.pallas_call(
         stats_kernel,
-        in_specs=[SMEM] + [ANY] * 6,
-        out_specs=[VMEM] * 5,
-        out_shape=[jax.ShapeDtypeStruct(wide, BF)] * 4
+        in_specs=[SMEM] + [ANY] * 4,
+        out_specs=[VMEM] * 3,
+        out_shape=[jax.ShapeDtypeStruct(wide, BF)] * 2
         + [jax.ShapeDtypeStruct((3, heads, GROUP), F32)],
         scratch_shapes=[
             pltpu.VMEM(wide, BF),
             pltpu.VMEM((heads, GROUP), F32),
-            pltpu.SemaphoreType.DMA((6,)),
+            pltpu.SemaphoreType.DMA((4,)),
         ],
         compiler_params=pltpu.CompilerParams(vmem_limit_bytes=16 << 20),
         cost_estimate=pl.CostEstimate(
@@ -102,6 +121,29 @@
         ),
         name="stats",
     )(place, *[pltpu.with_memory_space_constraint(x, pltpu.HBM) for x in arrays])
+
+
+def load_kernel(k_any, v_any, wait, k_ref, v_ref, sems):
+    copies = [
+        pltpu.make_async_copy(src, dst, sems.at[i]) for i, (src, dst) in enumerate(((k_any, k_ref), (v_any, v_ref)))
+    ]
+    for copy in copies:
+        copy.start()
+    for copy in copies:
+        copy.wait()
+
+
+def load_call(keys, values, wait):
+    return pl.pallas_call(
+        load_kernel,
+        in_specs=[ANY] * 3,
+        out_specs=[VMEM] * 2,
+        out_shape=[jax.ShapeDtypeStruct(keys.shape, BF)] * 2,
+        scratch_shapes=[pltpu.SemaphoreType.DMA((2,))],
+        compiler_params=pltpu.CompilerParams(vmem_limit_bytes=8 << 20),
+        cost_estimate=pl.CostEstimate(flops=0, bytes_accessed=4 << 20, transcendentals=0),
+        name="load",
+    )(*[pltpu.with_memory_space_constraint(x, pltpu.HBM) for x in (keys, values)], wait)
 
 
 def raw_call(queries, keys, values, out_grad, stats, wait):
@@ -136,33 +178,47 @@
             ]
             for *_, group in sides
         ]
-        for h in range(sh_ref.shape[1]):
-            c = slice(h * HD, (h + 1) * HD)
-            kk = jnp.concatenate([ref[0, :, c] for ref in pieces], axis=0)
-            vv = jnp.concatenate([ref[1, :, c] for ref in pieces], axis=0)
-            dk = dv = None
+        for h in range(0, sh_ref.shape[1], 2):
+            wide = slice(h * HD, (h + 2) * HD)
+            cs = [slice((h + i) * HD, (h + i + 1) * HD) for i in range(2)]
+            rows = count * BPC
+            kk = [jnp.concatenate([ref[0, :, c] for ref in pieces], axis=0) for c in cs]
+            vv = [jnp.concatenate([ref[1, :, c] for ref in pieces], axis=0) for c in cs]
+            if count > 1:
+                kk, vv = split(*kk), split(*vv)
+            total = None
             for side, (q_ref, g_ref, st_ref, _) in enumerate(sides):
-                q, g = q_ref[:, c], g_ref[:, c]
-                ln, delta, reach = (st_ref[i, h : h + 1, :] for i in range(3))
-                bias = jnp.concatenate(
-                    [
-                        jnp.broadcast_to(
-                            jnp.where(reach > jnp.full((1, GROUP), d, jnp.int32).astype(F32), ln, HIDDEN),
-                            (BPC, GROUP),
-                        )
-                        for d in far[side]
-                    ],
-                    axis=0,
-                )
-                p = jnp.exp2(nt(kk, q) * (SCALE * LOG2E) - bias)
-                ds = (p * (nt(vv, g) - delta)).astype(BF)
-                ds_ref[h, :, side * GROUP : (side + 1) * GROUP] = ds
-                dv_part, dk_part = nn(p.astype(BF), g), nn(ds, q)
-                dk, dv = (dk_part, dv_part) if dk is None else (dk + dk_part, dv + dv_part)
-            dk = dk * SCALE
-            for i, ref in enumerate(outs):
-                ref[0, :, c] = dk[i * BPC : (i + 1) * BPC].astype(ref.dtype)
-                ref[1, :, c] = dv[i * BPC : (i + 1) * BPC].astype(ref.dtype)
+                q, g = q_ref[:, wide], g_ref[:, wide]
+                if count > 1:
+                    s, d = nt(kk, q), nt(vv, g)
+                    s, d = (s[:rows], s[rows:]), (d[:rows], d[rows:])
+                else:
+                    s = nt(kk[0], q[:, :HD]), nt(kk[1], q[:, HD:])
+                    d = nt(vv[0], g[:, :HD]), nt(vv[1], g[:, HD:])
+                weights, dscores = [], []
+                for i in range(2):
+                    ln, delta, reach = (st_ref[n, h + i : h + i + 1, :] for n in range(3))
+                    bias = jnp.concatenate(
+                        [
+                            jnp.broadcast_to(
+                                jnp.where(reach > jnp.full((1, GROUP), f, jnp.int32).astype(F32), ln, HIDDEN),
+                                (BPC, GROUP),
+                            )
+                            for f in far[side]
+                        ],
+                        axis=0,
+                    )
+                    p = jnp.exp2(s[i] * (SCALE * LOG2E) - bias)
+                    dscores.append((p * (d[i] - delta)).astype(BF))
+                    weights.append(p.astype(BF))
+                    ds_ref[h + i, :, side * GROUP : (side + 1) * GROUP] = dscores[i]
+                parts = stacked(*dscores, q) + stacked(*weights, g)
+                total = parts if total is None else [x + y for x, y in zip(total, parts, strict=True)]
+            for i, c in enumerate(cs):
+                dk, dv = total[i] * SCALE, total[2 + i]
+                for n, ref in enumerate(outs):
+                    ref[0, :, c] = dk[n * BPC : (n + 1) * BPC].astype(ref.dtype)
+                    ref[1, :, c] = dv[n * BPC : (n + 1) * BPC].astype(ref.dtype)
 
     if 0 in shifts:
         work()
@@ -257,9 +313,7 @@
     own = jnp.stack([beacon_keys, beacon_values])
     a1, b1 = send(own, perm=UP), send(own, perm=DOWN)
     queries_other, grad_other = send(queries, perm=SWAP), send(out_grad, perm=SWAP)
-    q_home, k_home, v_home, g_home, stats = stats_call(
-        place, (queries, keys, values, out_grad, forward_out, log_norm)
-    )
+    q_home, g_home, stats = stats_call(place, (queries, out_grad, forward_out, log_norm))
     sides = (q_home, queries_other, g_home, grad_other, stats, send(stats, perm=SWAP))
     a1, b1 = both(a1, b1, sides[5])
     a2, b2 = send(a1, perm=UP), send(b1, perm=DOWN)
@@ -271,15 +325,16 @@
     t2a, t2b, ds2 = beacon_call(place, sides, ((a2, -2, F32), (b2, 2 - CHIPS, F32)), (), "beacons_second")
     a3, b3 = both(a3, b3, ds2)
     a4 = send(a3, perm=UP)
-    t4, ds4 = beacon_call(place, sides, ((a4, -4, BF),), (), "beacons_far")
+    t3a, t3b, ds3 = beacon_call(place, sides, ((a3, -3, F32), (b3, 3 - CHIPS, BF)), (), "beacons_third")
+    t4, ds4 = beacon_call(place, sides, ((a4, -4, BF),), (ds3,), "beacons_far")
 
     def plus(arrived, term):
         return (arrived.astype(F32) + term).astype(BF)
 
     a = send(t4, perm=DOWN)
-    t3a, b, ds3 = beacon_call(place, sides, ((a3, -3, F32), (b3, 3 - CHIPS, BF)), (t4,), "beacons_third")
     dq_home, dq_other = query_call((ds1, ds2, ds3, ds4), (a1, b1, own, a2, b2, a3, b3, a4))
-    a, b = both(a, b, dq_other)
+    k_home, v_home = load_call(keys, values, t4)
+    a, b = both(a, t3b, dq_other, k_home)
     a, b = send(plus(a, t3a), perm=DOWN), send(b, perm=UP)
     dq_raw, key_grad, value_grad = raw_call(q_home, k_home, v_home, g_home, stats, dq_other)
     a, b = both(a, b, dq_raw)

time: 77.6 us -> 75.4 us (0.972)
  waiting for transfers between devices: 30.5 us -> 28.5 us
  starting transfers between devices: 24.9 us -> 24.1 us
    ppermute x2, waiting for transfers between devices: 5.77 us -> 4.35 us  [local(): a, b = (send(plus(a, t1a), perm=DOWN), send(plus(b, t1b), perm=UP))]
    pallas_call x1 -> x2, Pallas kernels: 3.1 us -> 4.32 us  [the longest x1 2.76 us: stats_call(): pl.pallas_call(stats_kernel, in_specs=[SMEM] + [ANY] * 4, out_specs=[VMEM...]
  transfers between devices with their start and end apart: 18 -> 18, of which waited for: 13 -> 12; matrix products, arithmetic and copies ran while one was open for 2% -> 2% of each run, Pallas kernels for 22% -> 23%
where the time goes in v4:
time: 75.4 us; the launch traced here: 74.9 us
  waiting for transfers between devices  28.5 us (38%)
  starting transfers between devices  24.1 us (32%)
  Pallas kernels  17.9 us (24%)
  other arithmetic  2.11 us (3%)
  between operations  1.48 us (2%)
    pallas_call x4, Pallas kernels, beacon_call(): pl.pallas_call(functools.partial(beacon_kernel, shifts, len(waits)), in_s...  6.51 us
    ppermute x2, starting transfers between devices, local(): a1, b1 = (send(own, perm=UP), send(own, perm=DOWN))  5.93 us
    ppermute x1, waiting for transfers between devices, local(): a4 = send(a3, perm=UP)  5.9 us
    pallas_call x1, Pallas kernels, raw_call(): pl.pallas_call(raw_kernel, in_specs=[VMEM] * 5 + [ANY], out_specs=[VMEM]...  5.34 us
    ppermute x2, waiting for transfers between devices, local(): a3, b3 = (send(a2, perm=UP), send(b2, perm=DOWN))  4.9 us
    ppermute x2, waiting for transfers between devices, local(): a1, b1 = (send(own, perm=UP), send(own, perm=DOWN))  4.42 us
    ppermute x2, waiting for transfers between devices, local(): a, b = (send(plus(a, t1a), perm=DOWN), send(plus(b, t1b), perm=UP))  4.35 us
    ppermute x2, waiting for transfers between devices, local(): a, b = (send(plus(a, t2a), perm=DOWN), send(plus(b, t2b), perm=UP))  4.05 us
  transfers between devices with their start and end apart: 18, of which 12 were waited for; matrix products, arithmetic and copies ran while one was open for 2% of the time, Pallas kernels for 23%

profile of v4, /device:TPU:6, one launch (start us, length us, event | category | flops | bytes accessed | tf_op | source)
XLA Modules:
  0.0 74.9 jit_solution(16211550438256523758)
XLA Ops:
  0.6 0.1 collective-permute-start
  0.7 0.5 collective-permute-start.1
  1.2 1.0 %pad_maximum_fusion.refs_2_.refs_6_ = bf16[2,64,1024]{2,1,0:T(8,128)(2,1)S(1)} fusion(bf16[1,64,1024]{2,1,0:T(8,128)(2,1)} %bitcast.8, bf16[1,64,1024]{2,1,0:T(8,128)(2,1)} %bitcast.9), kind=kLoop, calls=%fused_computation.7 | loop fusion | flops 131072 | bytes 524288 | tf_op jit(solution)/shard_map/stack | solution.py:313
  2.2 5.9 %collective-permute-start.4 = (bf16[2,64,1024]{2,1,0:T(8,128)(2,1)S(1)}, bf16[2,64,1024]{2,1,0:T(8,128)(2,1)S(1)}, u32[]{:S(2)}, u32[]{:S(2)}) collective-permute-start(bf16[2,64,1024]{2,1,0:T(8,128)(2,1)S(1)} %pad_maximum_fusion.refs_2_.refs_6_), channel_id=1, source_target_pairs={{0,224},{16,240},{32,0},{48,16},{64,32},{80,48},{96,64},{112,80},{... | collective-permute-start | bytes 786440 | tf_op jit(solution)/shard_map/ppermute | solution.py:314
  8.2 0.0 collective-permute-start.3
  8.8 0.1 pad_add_fusion.place
  8.9 2.8 %stats.1 = (bf16[512,1024]{1,0:T(8,128)(2,1)S(1)}, bf16[512,1024]{1,0:T(8,128)(2,1)S(1)}, f32[3,8,512]{2,1,0:T(8,128)S(1)}) custom-call(s32[3]{0:T(128)S(1)} %pad_add_fusion.place, bf16[512,1024]{1,0:T(8,128)(2,1)} %q_any.1, bf16[512,1024]{1,0:T(8,128)(2,1)} %g_any.1, bf16[512,1024]{1,0:T(8,128)(2,1)} %o_any.1, f32[8,512]{1,0:T(8,128)} %ln_any.1), custom_call_target="tpu_custom_call" | custom-call | flops 1048576 | bytes 8388608 | tf_op jit(solution)/shard_map/stats/pallas_call | solution.py:107
  11.7 0.1 collective-permute-start.2
  11.8 1.2 %collective-permute-done.2.refs_2_.sp_ref = f32[3,8,512]{2,1,0:T(8,128)S(1)} collective-permute-done((f32[3,8,512]{2,1,0:T(8,128)S(1)}, f32[3,8,512]{2,1,0:T(8,128)S(1)}, u32[]{:S(2)}, u32[]{:S(2)}) %collective-permute-start.2) | collective-permute-done | bytes 49184 | tf_op jit(solution)/shard_map/ppermute | solution.py:317
  13.0 1.0 %collective-permute-done.4.refs_1_.refs_0_ = bf16[2,64,1024]{2,1,0:T(8,128)(2,1)S(1)} collective-permute-done((bf16[2,64,1024]{2,1,0:T(8,128)(2,1)S(1)}, bf16[2,64,1024]{2,1,0:T(8,128)(2,1)S(1)}, u32[]{:S(2)}, u32[]{:S(2)}) %collective-permute-start.4) | collective-permute-done | bytes 262176 | tf_op jit(solution)/shard_map/ppermute | solution.py:314
  14.0 3.4 %collective-permute-done.3.refs_0_ = bf16[2,64,1024]{2,1,0:T(8,128)(2,1)S(1)} collective-permute-done((bf16[2,64,1024]{2,1,0:T(8,128)(2,1)S(1)}, bf16[2,64,1024]{2,1,0:T(8,128)(2,1)S(1)}, u32[]{:S(2)}, u32[]{:S(2)}) %collective-permute-start.3) | collective-permute-done | bytes 262176 | tf_op jit(solution)/shard_map/ppermute | solution.py:314
  17.4 0.3 collective-permute-start.6
  17.7 1.7 %collective-permute-start.5 = (bf16[2,64,1024]{2,1,0:T(8,128)(2,1)S(1)}, bf16[2,64,1024]{2,1,0:T(8,128)(2,1)S(1)}, u32[]{:S(2)}, u32[]{:S(2)}) collective-permute-start(bf16[2,64,1024]{2,1,0:T(8,128)(2,1)S(1)} %join.12.refs_1_.refs_0_.refs_4_), channel_id=1, source_target_pairs={{0,32},{16,48},{32,64},{48,80},{64,96},{80,112},{96,128},{112,144}... | collective-permute-start | bytes 786440 | tf_op jit(solution)/shard_map/ppermute | solution.py:319
  19.4 0.0 collective-permute-done.qp_ref
  19.4 0.0 collective-permute-done.1.gp_ref
  19.4 4.2 %beacons_near.1 = (f32[2,64,1024]{2,1,0:T(8,128)S(1)}, f32[2,64,1024]{2,1,0:T(8,128)S(1)}, f32[2,64,1024]{2,1,0:T(8,128)S(1)}, bf16[8,192,1024]{2,1,0:T(8,128)(2,1)S(1)}) custom-call(s32[3]{0:T(128)S(1)} %pad_add_fusion.place, bf16[512,1024]{1,0:T(8,128)(2,1)S(1)} %get-tuple-element.27.qh_ref.q_ref, bf16[512,1024]{1,0:T(8,128)(2,1)S(1)} %collective-permute-done.qp_ref, ...), custom_call_target="tpu_custom_call" | custom-call | flops 1610612736 | bytes 8388608 | tf_op jit(solution)/shard_map/beacons_near/pallas_call | solution.py:241
  23.7 0.9 %collective-permute-done.6.refs_1_.refs_0_ = bf16[2,64,1024]{2,1,0:T(8,128)(2,1)S(1)} collective-permute-done((bf16[2,64,1024]{2,1,0:T(8,128)(2,1)S(1)}, bf16[2,64,1024]{2,1,0:T(8,128)(2,1)S(1)}, u32[]{:S(2)}, u32[]{:S(2)}) %collective-permute-start.6) | collective-permute-done | bytes 262176 | tf_op jit(solution)/shard_map/ppermute | solution.py:319
  24.6 1.5 %collective-permute-done.5.refs_0_ = bf16[2,64,1024]{2,1,0:T(8,128)(2,1)S(1)} collective-permute-done((bf16[2,64,1024]{2,1,0:T(8,128)(2,1)S(1)}, bf16[2,64,1024]{2,1,0:T(8,128)(2,1)S(1)}, u32[]{:S(2)}, u32[]{:S(2)}) %collective-permute-start.5) | collective-permute-done | bytes 262176 | tf_op jit(solution)/shard_map/ppermute | solution.py:319
  26.1 0.3 collective-permute-start.8
  26.4 1.7 %collective-permute-start.7 = (bf16[2,64,1024]{2,1,0:T(8,128)(2,1)S(1)}, bf16[2,64,1024]{2,1,0:T(8,128)(2,1)S(1)}, u32[]{:S(2)}, u32[]{:S(2)}) collective-permute-start(bf16[2,64,1024]{2,1,0:T(8,128)(2,1)S(1)} %join.14.refs_1_.refs_0_.refs_7_), channel_id=1, source_target_pairs={{0,32},{16,48},{32,64},{48,80},{64,96},{80,112},{96,128},{112,144}... | collective-permute-start | bytes 786440 | tf_op jit(solution)/shard_map/ppermute | solution.py:324
  28.1 0.9 %beacons_second.1 = (f32[2,64,1024]{2,1,0:T(8,128)S(1)}, f32[2,64,1024]{2,1,0:T(8,128)S(1)}, bf16[8,128,1024]{2,1,0:T(8,128)(2,1)S(1)}) custom-call(s32[3]{0:T(128)S(1)} %pad_add_fusion.place, bf16[512,1024]{1,0:T(8,128)(2,1)S(1)} %get-tuple-element.27.qh_ref.q_ref, bf16[512,1024]{1,0:T(8,128)(2,1)S(1)} %collective-permute-done.qp_ref, ...), custom_call_target="tpu_custom_call" | custom-call | flops 1073741824 | bytes 8388608 | tf_op jit(solution)/shard_map/beacons_second/pallas_call | solution.py:241
  29.1 3.4 %collective-permute-done.8.refs_1_.refs_0_ = bf16[2,64,1024]{2,1,0:T(8,128)(2,1)S(1)} collective-permute-done((bf16[2,64,1024]{2,1,0:T(8,128)(2,1)S(1)}, bf16[2,64,1024]{2,1,0:T(8,128)(2,1)S(1)}, u32[]{:S(2)}, u32[]{:S(2)}) %collective-permute-start.8) | collective-permute-done | bytes 262176 | tf_op jit(solution)/shard_map/ppermute | solution.py:324
  32.5 1.5 %collective-permute-done.7.refs_0_ = bf16[2,64,1024]{2,1,0:T(8,128)(2,1)S(1)} collective-permute-done((bf16[2,64,1024]{2,1,0:T(8,128)(2,1)S(1)}, bf16[2,64,1024]{2,1,0:T(8,128)(2,1)S(1)}, u32[]{:S(2)}, u32[]{:S(2)}) %collective-permute-start.7) | collective-permute-done | bytes 262176 | tf_op jit(solution)/shard_map/ppermute | solution.py:324
  34.0 0.9 %collective-permute-start.9 = (bf16[2,64,1024]{2,1,0:T(8,128)(2,1)S(1)}, bf16[2,64,1024]{2,1,0:T(8,128)(2,1)S(1)}, u32[]{:S(2)}, u32[]{:S(2)}) collective-permute-start(bf16[2,64,1024]{2,1,0:T(8,128)(2,1)S(1)} %join.16.refs_1_.refs_0_.refs_9_), channel_id=1, source_target_pairs={{0,32},{16,48},{32,64},{48,80},{64,96},{80,112},{96,128},{112,144}... | collective-permute-start | bytes 786440 | tf_op jit(solution)/shard_map/ppermute | solution.py:327
  34.9 0.7 beacons_third.1
  35.6 5.9 %collective-permute-done.9.refs_0_.refs_11_ = bf16[2,64,1024]{2,1,0:T(8,128)(2,1)S(1)} collective-permute-done((bf16[2,64,1024]{2,1,0:T(8,128)(2,1)S(1)}, bf16[2,64,1024]{2,1,0:T(8,128)(2,1)S(1)}, u32[]{:S(2)}, u32[]{:S(2)}) %collective-permute-start.9) | collective-permute-done | bytes 262176 | tf_op jit(solution)/shard_map/ppermute | solution.py:327
  41.5 0.6 beacons_far.1
  42.2 2.1 %collective-permute-start.11 = (bf16[2,64,1024]{2,1,0:T(8,128)(2,1)S(1)}, bf16[2,64,1024]{2,1,0:T(8,128)(2,1)S(1)}, u32[]{:S(2)}, u32[]{:S(2)}) collective-permute-start(bf16[2,64,1024]{2,1,0:T(8,128)(2,1)S(1)} %get-tuple-element.33.wait), channel_id=1, source_target_pairs={{0,224},{16,240},{32,0},{48,16},{64,32},{80,48},{96,64},{112,80},{... | collective-permute-start | bytes 786440 | tf_op jit(solution)/shard_map/ppermute | solution.py:334
  44.3 1.7 %query_grad.1 = (f32[512,1024]{1,0:T(8,128)S(1)}, bf16[512,1024]{1,0:T(8,128)(2,1)S(1)}) custom-call(bf16[8,192,1024]{2,1,0:T(8,128)(2,1)S(1)} %get-tuple-element.30.refs_2_.refs_0_, bf16[8,128,1024]{2,1,0:T(8,128)(2,1)S(1)} %get-tuple-element.31.refs_2_.refs_1_, bf16[8,128,1024]{2,1,0:T(8,128)(2,1)S(1)} %get-tuple-element.32.refs_1_.refs_2_, ...), custom_call_target="tpu_custom_call" | custom-call | flops 1073741824 | bytes 16777216 | tf_op jit(solution)/shard_map/query_grad/pallas_call | solution.py:266
  46.0 0.1 collective-permute-start.10
  46.1 1.6 %load.1 = (bf16[512,1024]{1,0:T(8,128)(2,1)S(1)}, bf16[512,1024]{1,0:T(8,128)(2,1)S(1)}) custom-call(bf16[512,1024]{1,0:T(8,128)(2,1)} %k_any.1, bf16[512,1024]{1,0:T(8,128)(2,1)} %v_any.1, bf16[2,64,1024]{2,1,0:T(8,128)(2,1)S(1)} %get-tuple-element.33.wait), custom_call_target="tpu_custom_call" | custom-call | bytes 4194304 | tf_op jit(solution)/shard_map/load/pallas_call | solution.py:137
  47.7 0.9 %collective-permute-done.11.refs_0_ = bf16[2,64,1024]{2,1,0:T(8,128)(2,1)S(1)} collective-permute-done((bf16[2,64,1024]{2,1,0:T(8,128)(2,1)S(1)}, bf16[2,64,1024]{2,1,0:T(8,128)(2,1)S(1)}, u32[]{:S(2)}, u32[]{:S(2)}) %collective-permute-start.11) | collective-permute-done | bytes 262176 | tf_op jit(solution)/shard_map/ppermute | solution.py:334
  48.6 0.1 add_convert_fusion.6
  48.7 0.3 collective-permute-start.13
  49.0 3.3 %collective-permute-start.12 = (bf16[2,64,1024]{2,1,0:T(8,128)(2,1)S(1)}, bf16[2,64,1024]{2,1,0:T(8,128)(2,1)S(1)}, u32[]{:S(2)}, u32[]{:S(2)}) collective-permute-start(bf16[2,64,1024]{2,1,0:T(8,128)(2,1)S(1)} %add_convert_fusion.6), channel_id=1, source_target_pairs={{0,224},{16,240},{32,0},{48,16},{64,32},{80,48},{96,64},{112,80},{... | collective-permute-start | bytes 786440 | tf_op jit(solution)/shard_map/ppermute | solution.py:338
  52.3 5.3 %raw_tokens.1 = (f32[512,1024]{1,0:T(8,128)S(1)}, bf16[512,1024]{1,0:T(8,128)(2,1)}, bf16[512,1024]{1,0:T(8,128)(2,1)}) custom-call(bf16[512,1024]{1,0:T(8,128)(2,1)S(1)} %get-tuple-element.27.qh_ref.q_ref, bf16[512,1024]{1,0:T(8,128)(2,1)S(1)} %get-tuple-element.34.k_ref.refs_3_, bf16[512,1024]{1,0:T(8,128)(2,1)S(1)} %get-tuple-element.35.v_ref, ...), custom_call_target="tpu_custom_call" | custom-call | flops 2684354560 | bytes 10485760 | tf_op jit(solution)/shard_map/raw_tokens/pallas_call | solution.py:152
  57.7 0.3 collective-permute-done.13.refs_1_.refs_0_
  58.0 0.0 collective-permute-done.12.refs_0_
  58.0 0.1 add_convert_fusion.4
  58.1 0.1 collective-permute-start.15
  58.2 0.1 add_convert_fusion.5
  58.2 3.3 %collective-permute-start.14 = (bf16[2,64,1024]{2,1,0:T(8,128)(2,1)S(1)}, bf16[2,64,1024]{2,1,0:T(8,128)(2,1)S(1)}, u32[]{:S(2)}, u32[]{:S(2)}) collective-permute-start(bf16[2,64,1024]{2,1,0:T(8,128)(2,1)S(1)} %add_convert_fusion.5), channel_id=1, source_target_pairs={{0,224},{16,240},{32,0},{48,16},{64,32},{80,48},{96,64},{112,80},{... | collective-permute-start | bytes 786440 | tf_op jit(solution)/shard_map/ppermute | solution.py:341
  61.5 0.0 collective-permute-done.10
  61.5 0.6 add_convert_fusion.refs_2_
  62.2 0.0 copy-start
  62.2 4.0 %collective-permute-done.15.refs_1_.refs_0_ = bf16[2,64,1024]{2,1,0:T(8,128)(2,1)S(1)} collective-permute-done((bf16[2,64,1024]{2,1,0:T(8,128)(2,1)S(1)}, bf16[2,64,1024]{2,1,0:T(8,128)(2,1)S(1)}, u32[]{:S(2)}, u32[]{:S(2)}) %collective-permute-start.15) | collective-permute-done | bytes 262176 | tf_op jit(solution)/shard_map/ppermute | solution.py:341
  66.2 0.0 collective-permute-done.14.refs_0_
  66.2 0.1 add_convert_fusion.3
  66.3 0.1 add_convert_fusion.2
  66.4 0.0 copy-done
  66.4 1.2 %collective-permute-start.17 = (bf16[2,64,1024]{2,1,0:T(8,128)(2,1)S(1)}, bf16[2,64,1024]{2,1,0:T(8,128)(2,1)S(1)}, u32[]{:S(2)}, u32[]{:S(2)}) collective-permute-start(bf16[2,64,1024]{2,1,0:T(8,128)(2,1)S(1)} %add_convert_fusion.2), channel_id=1, source_target_pairs={{0,32},{16,48},{32,64},{48,80},{64,96},{80,112},{96,128},{112,144}... | collective-permute-start | bytes 786440 | tf_op jit(solution)/shard_map/ppermute | solution.py:344
  67.6 2.1 %collective-permute-start.16 = (bf16[2,64,1024]{2,1,0:T(8,128)(2,1)S(1)}, bf16[2,64,1024]{2,1,0:T(8,128)(2,1)S(1)}, u32[]{:S(2)}, u32[]{:S(2)}) collective-permute-start(bf16[2,64,1024]{2,1,0:T(8,128)(2,1)S(1)} %add_convert_fusion.3), channel_id=1, source_target_pairs={{0,224},{16,240},{32,0},{48,16},{64,32},{80,48},{96,64},{112,80},{... | collective-permute-start | bytes 786440 | tf_op jit(solution)/shard_map/ppermute | solution.py:344
  69.7 4.3 %collective-permute-done.17 = bf16[2,64,1024]{2,1,0:T(8,128)(2,1)S(1)} collective-permute-done((bf16[2,64,1024]{2,1,0:T(8,128)(2,1)S(1)}, bf16[2,64,1024]{2,1,0:T(8,128)(2,1)S(1)}, u32[]{:S(2)}, u32[]{:S(2)}) %collective-permute-start.17) | collective-permute-done | bytes 262176 | tf_op jit(solution)/shard_map/ppermute | solution.py:344
  74.1 0.0 collective-permute-done.16
  74.1 0.1 add_convert_fusion.1
  74.2 0.7 slice_bitcast_fusion
  (12 shorter events, 0.0 us)
Async XLA Ops:
  0.6 18.8 %collective-permute-start = (bf16[512,1024]{1,0:T(8,128)(2,1)}, bf16[512,1024]{1,0:T(8,128)(2,1)S(1)}, u32[]{:S(2)}, u32[]{:S(2)}) collective-permute-start(bf16[512,1024]{1,0:T(8,128)(2,1)} %q_any.1), channel_id=1, source_target_pairs={{0,16},{16,0},{32,48},{48,32},{64,80},{80,64},{96,112},{112,96},{1... | collective-permute-start | bytes 3145736 | tf_op jit(solution)/shard_map/ppermute | solution.py:315
  0.7 18.7 %collective-permute-start.1 = (bf16[512,1024]{1,0:T(8,128)(2,1)}, bf16[512,1024]{1,0:T(8,128)(2,1)S(1)}, u32[]{:S(2)}, u32[]{:S(2)}) collective-permute-start(bf16[512,1024]{1,0:T(8,128)(2,1)} %g_any.1), channel_id=1, source_target_pairs={{0,16},{16,0},{32,48},{48,32},{64,80},{80,64},{96,112},{112,96},{1... | collective-permute-start | bytes 3145736 | tf_op jit(solution)/shard_map/ppermute | solution.py:315
  2.2 11.8 %collective-permute-start.4 = (bf16[2,64,1024]{2,1,0:T(8,128)(2,1)S(1)}, bf16[2,64,1024]{2,1,0:T(8,128)(2,1)S(1)}, u32[]{:S(2)}, u32[]{:S(2)}) collective-permute-start(bf16[2,64,1024]{2,1,0:T(8,128)(2,1)S(1)} %pad_maximum_fusion.refs_2_.refs_6_), channel_id=1, source_target_pairs={{0,224},{16,240},{32,0},{48,16},{64,32},{80,48},{96,64},{112,80},{... | collective-permute-start | bytes 786440 | tf_op jit(solution)/shard_map/ppermute | solution.py:314
  8.2 9.2 %collective-permute-start.3 = (bf16[2,64,1024]{2,1,0:T(8,128)(2,1)S(1)}, bf16[2,64,1024]{2,1,0:T(8,128)(2,1)S(1)}, u32[]{:S(2)}, u32[]{:S(2)}) collective-permute-start(bf16[2,64,1024]{2,1,0:T(8,128)(2,1)S(1)} %pad_maximum_fusion.refs_2_.refs_6_), channel_id=1, source_target_pairs={{0,32},{16,48},{32,64},{48,80},{64,96},{80,112},{96,128},{112,144}... | collective-permute-start | bytes 786440 | tf_op jit(solution)/shard_map/ppermute | solution.py:314
  11.7 1.3 %collective-permute-start.2 = (f32[3,8,512]{2,1,0:T(8,128)S(1)}, f32[3,8,512]{2,1,0:T(8,128)S(1)}, u32[]{:S(2)}, u32[]{:S(2)}) collective-permute-start(f32[3,8,512]{2,1,0:T(8,128)S(1)} %get-tuple-element.29.sh_ref.st_ref), channel_id=1, source_target_pairs={{0,16},{16,0},{32,48},{48,32},{64,80},{80,64},{96,112},{112,96},{1... | collective-permute-start | bytes 147464 | tf_op jit(solution)/shard_map/ppermute | solution.py:317
  17.4 7.2 %collective-permute-start.6 = (bf16[2,64,1024]{2,1,0:T(8,128)(2,1)S(1)}, bf16[2,64,1024]{2,1,0:T(8,128)(2,1)S(1)}, u32[]{:S(2)}, u32[]{:S(2)}) collective-permute-start(bf16[2,64,1024]{2,1,0:T(8,128)(2,1)S(1)} %join.13.refs_1_.refs_5_), channel_id=1, source_target_pairs={{0,224},{16,240},{32,0},{48,16},{64,32},{80,48},{96,64},{112,80},{... | collective-permute-start | bytes 786440 | tf_op jit(solution)/shard_map/ppermute | solution.py:319
  17.7 8.4 %collective-permute-start.5 = (bf16[2,64,1024]{2,1,0:T(8,128)(2,1)S(1)}, bf16[2,64,1024]{2,1,0:T(8,128)(2,1)S(1)}, u32[]{:S(2)}, u32[]{:S(2)}) collective-permute-start(bf16[2,64,1024]{2,1,0:T(8,128)(2,1)S(1)} %join.12.refs_1_.refs_0_.refs_4_), channel_id=1, source_target_pairs={{0,32},{16,48},{32,64},{48,80},{64,96},{80,112},{96,128},{112,144}... | collective-permute-start | bytes 786440 | tf_op jit(solution)/shard_map/ppermute | solution.py:319
  26.1 6.4 %collective-permute-start.8 = (bf16[2,64,1024]{2,1,0:T(8,128)(2,1)S(1)}, bf16[2,64,1024]{2,1,0:T(8,128)(2,1)S(1)}, u32[]{:S(2)}, u32[]{:S(2)}) collective-permute-start(bf16[2,64,1024]{2,1,0:T(8,128)(2,1)S(1)} %join.15.refs_1_.refs_8_), channel_id=1, source_target_pairs={{0,224},{16,240},{32,0},{48,16},{64,32},{80,48},{96,64},{112,80},{... | collective-permute-start | bytes 786440 | tf_op jit(solution)/shard_map/ppermute | solution.py:324
  26.4 7.6 %collective-permute-start.7 = (bf16[2,64,1024]{2,1,0:T(8,128)(2,1)S(1)}, bf16[2,64,1024]{2,1,0:T(8,128)(2,1)S(1)}, u32[]{:S(2)}, u32[]{:S(2)}) collective-permute-start(bf16[2,64,1024]{2,1,0:T(8,128)(2,1)S(1)} %join.14.refs_1_.refs_0_.refs_7_), channel_id=1, source_target_pairs={{0,32},{16,48},{32,64},{48,80},{64,96},{80,112},{96,128},{112,144}... | collective-permute-start | bytes 786440 | tf_op jit(solution)/shard_map/ppermute | solution.py:324
  34.0 7.6 %collective-permute-start.9 = (bf16[2,64,1024]{2,1,0:T(8,128)(2,1)S(1)}, bf16[2,64,1024]{2,1,0:T(8,128)(2,1)S(1)}, u32[]{:S(2)}, u32[]{:S(2)}) collective-permute-start(bf16[2,64,1024]{2,1,0:T(8,128)(2,1)S(1)} %join.16.refs_1_.refs_0_.refs_9_), channel_id=1, source_target_pairs={{0,32},{16,48},{32,64},{48,80},{64,96},{80,112},{96,128},{112,144}... | collective-permute-start | bytes 786440 | tf_op jit(solution)/shard_map/ppermute | solution.py:327
  42.2 6.5 %collective-permute-start.11 = (bf16[2,64,1024]{2,1,0:T(8,128)(2,1)S(1)}, bf16[2,64,1024]{2,1,0:T(8,128)(2,1)S(1)}, u32[]{:S(2)}, u32[]{:S(2)}) collective-permute-start(bf16[2,64,1024]{2,1,0:T(8,128)(2,1)S(1)} %get-tuple-element.33.wait), channel_id=1, source_target_pairs={{0,224},{16,240},{32,0},{48,16},{64,32},{80,48},{96,64},{112,80},{... | collective-permute-start | bytes 786440 | tf_op jit(solution)/shard_map/ppermute | solution.py:334
  46.0 15.5 %collective-permute-start.10 = (bf16[512,1024]{1,0:T(8,128)(2,1)S(1)}, bf16[512,1024]{1,0:T(8,128)(2,1)S(1)}, u32[]{:S(2)}, u32[]{:S(2)}) collective-permute-start(bf16[512,1024]{1,0:T(8,128)(2,1)S(1)} %get-tuple-element.37.wait.refs_2_), channel_id=1, source_target_pairs={{0,16},{16,0},{32,48},{48,32},{64,80},{80,64},{96,112},{112,96},{1... | collective-permute-start | bytes 3145736 | tf_op jit(solution)/shard_map/ppermute | solution.py:342
  48.7 9.3 %collective-permute-start.13 = (bf16[2,64,1024]{2,1,0:T(8,128)(2,1)S(1)}, bf16[2,64,1024]{2,1,0:T(8,128)(2,1)S(1)}, u32[]{:S(2)}, u32[]{:S(2)}) collective-permute-start(bf16[2,64,1024]{2,1,0:T(8,128)(2,1)S(1)} %join.19), channel_id=1, source_target_pairs={{0,32},{16,48},{32,64},{48,80},{64,96},{80,112},{96,128},{112,144}... | collective-permute-start | bytes 786440 | tf_op jit(solution)/shard_map/ppermute | solution.py:338
  49.0 9.0 %collective-permute-start.12 = (bf16[2,64,1024]{2,1,0:T(8,128)(2,1)S(1)}, bf16[2,64,1024]{2,1,0:T(8,128)(2,1)S(1)}, u32[]{:S(2)}, u32[]{:S(2)}) collective-permute-start(bf16[2,64,1024]{2,1,0:T(8,128)(2,1)S(1)} %add_convert_fusion.6), channel_id=1, source_target_pairs={{0,224},{16,240},{32,0},{48,16},{64,32},{80,48},{96,64},{112,80},{... | collective-permute-start | bytes 786440 | tf_op jit(solution)/shard_map/ppermute | solution.py:338
  58.1 8.2 %collective-permute-start.15 = (bf16[2,64,1024]{2,1,0:T(8,128)(2,1)S(1)}, bf16[2,64,1024]{2,1,0:T(8,128)(2,1)S(1)}, u32[]{:S(2)}, u32[]{:S(2)}) collective-permute-start(bf16[2,64,1024]{2,1,0:T(8,128)(2,1)S(1)} %add_convert_fusion.4), channel_id=1, source_target_pairs={{0,32},{16,48},{32,64},{48,80},{64,96},{80,112},{96,128},{112,144}... | collective-permute-start | bytes 786440 | tf_op jit(solution)/shard_map/ppermute | solution.py:341
  58.2 8.0 %collective-permute-start.14 = (bf16[2,64,1024]{2,1,0:T(8,128)(2,1)S(1)}, bf16[2,64,1024]{2,1,0:T(8,128)(2,1)S(1)}, u32[]{:S(2)}, u32[]{:S(2)}) collective-permute-start(bf16[2,64,1024]{2,1,0:T(8,128)(2,1)S(1)} %add_convert_fusion.5), channel_id=1, source_target_pairs={{0,224},{16,240},{32,0},{48,16},{64,32},{80,48},{96,64},{112,80},{... | collective-permute-start | bytes 786440 | tf_op jit(solution)/shard_map/ppermute | solution.py:341
  62.2 4.2 %copy-start = (bf16[512,1024]{1,0:T(8,128)(2,1)}, bf16[512,1024]{1,0:T(8,128)(2,1)S(1)}, u32[]{:S(2)}) copy-start(bf16[512,1024]{1,0:T(8,128)(2,1)S(1)} %add_convert_fusion.refs_2_) | copy-start | bytes 3145732
  66.4 7.7 %collective-permute-start.17 = (bf16[2,64,1024]{2,1,0:T(8,128)(2,1)S(1)}, bf16[2,64,1024]{2,1,0:T(8,128)(2,1)S(1)}, u32[]{:S(2)}, u32[]{:S(2)}) collective-permute-start(bf16[2,64,1024]{2,1,0:T(8,128)(2,1)S(1)} %add_convert_fusion.2), channel_id=1, source_target_pairs={{0,32},{16,48},{32,64},{48,80},{64,96},{80,112},{96,128},{112,144}... | collective-permute-start | bytes 786440 | tf_op jit(solution)/shard_map/ppermute | solution.py:344
  67.6 6.5 %collective-permute-start.16 = (bf16[2,64,1024]{2,1,0:T(8,128)(2,1)S(1)}, bf16[2,64,1024]{2,1,0:T(8,128)(2,1)S(1)}, u32[]{:S(2)}, u32[]{:S(2)}) collective-permute-start(bf16[2,64,1024]{2,1,0:T(8,128)(2,1)S(1)} %add_convert_fusion.3), channel_id=1, source_target_pairs={{0,224},{16,240},{32,0},{48,16},{64,32},{80,48},{96,64},{112,80},{... | collective-permute-start | bytes 786440 | tf_op jit(solution)/shard_map/ppermute | solution.py:344

commit v5 on v4

--- a/solution.py
+++ b/solution.py
@@ -338,10 +338,10 @@
     a, b = send(plus(a, t3a), perm=DOWN), send(b, perm=UP)
     dq_raw, key_grad, value_grad = raw_call(q_home, k_home, v_home, g_home, stats, dq_other)
     a, b = both(a, b, dq_raw)
-    a, b = send(plus(a, t2a), perm=DOWN), send(plus(b, t2b), perm=UP)
+    b, a = send(plus(b, t2b), perm=UP), send(plus(a, t2a), perm=DOWN)
     query_grad = (dq_raw + dq_home + send(dq_other, perm=SWAP).astype(F32)).astype(BF)
     a, b = both(a, b, query_grad)
-    a, b = send(plus(a, t1a), perm=DOWN), send(plus(b, t1b), perm=UP)
+    b, a = send(plus(b, t1b), perm=UP), send(plus(a, t1a), perm=DOWN)
     total = (t0 + (a.astype(F32) + b.astype(F32))).astype(BF)
     return query_grad, key_grad, value_grad, total[0], total[1]
 

time: 75.4 us -> 75.4 us (level)
  no operation moved by 1% of the time
where the time goes in v5:
time: 75.4 us; the launch traced here: 74.9 us
  waiting for transfers between devices  28.5 us (38%)
  starting transfers between devices  24.1 us (32%)
  Pallas kernels  17.9 us (24%)
  other arithmetic  2.11 us (3%)
  between operations  1.48 us (2%)
    pallas_call x4, Pallas kernels, beacon_call(): pl.pallas_call(functools.partial(beacon_kernel, shifts, len(waits)), in_s...  6.51 us
    ppermute x2, starting transfers between devices, local(): a1, b1 = (send(own, perm=UP), send(own, perm=DOWN))  5.93 us
    ppermute x1, waiting for transfers between devices, local(): a4 = send(a3, perm=UP)  5.9 us
    pallas_call x1, Pallas kernels, raw_call(): pl.pallas_call(raw_kernel, in_specs=[VMEM] * 5 + [ANY], out_specs=[VMEM]...  5.34 us
    ppermute x2, waiting for transfers between devices, local(): a3, b3 = (send(a2, perm=UP), send(b2, perm=DOWN))  4.9 us
    ppermute x2, waiting for transfers between devices, local(): a1, b1 = (send(own, perm=UP), send(own, perm=DOWN))  4.42 us
    ppermute x2, waiting for transfers between devices, local(): b, a = (send(plus(b, t1b), perm=UP), send(plus(a, t1a), perm=DOWN))  4.35 us
    ppermute x2, waiting for transfers between devices, local(): b, a = (send(plus(b, t2b), perm=UP), send(plus(a, t2a), perm=DOWN))  4.05 us
  transfers between devices with their start and end apart: 18, of which 12 were waited for; matrix products, arithmetic and copies ran while one was open for 2% of the time, Pallas kernels for 23%

profile of v5, /device:TPU:6, one launch (start us, length us, event | category | flops | bytes accessed | tf_op | source)
XLA Modules:
  0.0 74.9 jit_solution(16211550438256523758)
XLA Ops:
  0.6 0.1 collective-permute-start
  0.7 0.5 collective-permute-start.1
  1.2 1.0 %pad_maximum_fusion.refs_2_.refs_6_ = bf16[2,64,1024]{2,1,0:T(8,128)(2,1)S(1)} fusion(bf16[1,64,1024]{2,1,0:T(8,128)(2,1)} %bitcast.8, bf16[1,64,1024]{2,1,0:T(8,128)(2,1)} %bitcast.9), kind=kLoop, calls=%fused_computation.7 | loop fusion | flops 131072 | bytes 524288 | tf_op jit(solution)/shard_map/stack | solution.py:313
  2.2 5.9 %collective-permute-start.4 = (bf16[2,64,1024]{2,1,0:T(8,128)(2,1)S(1)}, bf16[2,64,1024]{2,1,0:T(8,128)(2,1)S(1)}, u32[]{:S(2)}, u32[]{:S(2)}) collective-permute-start(bf16[2,64,1024]{2,1,0:T(8,128)(2,1)S(1)} %pad_maximum_fusion.refs_2_.refs_6_), channel_id=1, source_target_pairs={{0,224},{16,240},{32,0},{48,16},{64,32},{80,48},{96,64},{112,80},{... | collective-permute-start | bytes 786440 | tf_op jit(solution)/shard_map/ppermute | solution.py:314
  8.2 0.0 collective-permute-start.3
  8.8 0.1 pad_add_fusion.place
  8.9 2.8 %stats.1 = (bf16[512,1024]{1,0:T(8,128)(2,1)S(1)}, bf16[512,1024]{1,0:T(8,128)(2,1)S(1)}, f32[3,8,512]{2,1,0:T(8,128)S(1)}) custom-call(s32[3]{0:T(128)S(1)} %pad_add_fusion.place, bf16[512,1024]{1,0:T(8,128)(2,1)} %q_any.1, bf16[512,1024]{1,0:T(8,128)(2,1)} %g_any.1, bf16[512,1024]{1,0:T(8,128)(2,1)} %o_any.1, f32[8,512]{1,0:T(8,128)} %ln_any.1), custom_call_target="tpu_custom_call" | custom-call | flops 1048576 | bytes 8388608 | tf_op jit(solution)/shard_map/stats/pallas_call | solution.py:107
  11.7 0.1 collective-permute-start.2
  11.8 1.2 %collective-permute-done.2.refs_2_.sp_ref = f32[3,8,512]{2,1,0:T(8,128)S(1)} collective-permute-done((f32[3,8,512]{2,1,0:T(8,128)S(1)}, f32[3,8,512]{2,1,0:T(8,128)S(1)}, u32[]{:S(2)}, u32[]{:S(2)}) %collective-permute-start.2) | collective-permute-done | bytes 49184 | tf_op jit(solution)/shard_map/ppermute | solution.py:317
  13.0 1.0 %collective-permute-done.4.refs_1_.refs_0_ = bf16[2,64,1024]{2,1,0:T(8,128)(2,1)S(1)} collective-permute-done((bf16[2,64,1024]{2,1,0:T(8,128)(2,1)S(1)}, bf16[2,64,1024]{2,1,0:T(8,128)(2,1)S(1)}, u32[]{:S(2)}, u32[]{:S(2)}) %collective-permute-start.4) | collective-permute-done | bytes 262176 | tf_op jit(solution)/shard_map/ppermute | solution.py:314
  14.0 3.4 %collective-permute-done.3.refs_0_ = bf16[2,64,1024]{2,1,0:T(8,128)(2,1)S(1)} collective-permute-done((bf16[2,64,1024]{2,1,0:T(8,128)(2,1)S(1)}, bf16[2,64,1024]{2,1,0:T(8,128)(2,1)S(1)}, u32[]{:S(2)}, u32[]{:S(2)}) %collective-permute-start.3) | collective-permute-done | bytes 262176 | tf_op jit(solution)/shard_map/ppermute | solution.py:314
  17.4 0.3 collective-permute-start.6
  17.7 1.7 %collective-permute-start.5 = (bf16[2,64,1024]{2,1,0:T(8,128)(2,1)S(1)}, bf16[2,64,1024]{2,1,0:T(8,128)(2,1)S(1)}, u32[]{:S(2)}, u32[]{:S(2)}) collective-permute-start(bf16[2,64,1024]{2,1,0:T(8,128)(2,1)S(1)} %join.12.refs_1_.refs_0_.refs_4_), channel_id=1, source_target_pairs={{0,32},{16,48},{32,64},{48,80},{64,96},{80,112},{96,128},{112,144}... | collective-permute-start | bytes 786440 | tf_op jit(solution)/shard_map/ppermute | solution.py:319
  19.4 0.0 collective-permute-done.qp_ref
  19.4 0.0 collective-permute-done.1.gp_ref
  19.4 4.2 %beacons_near.1 = (f32[2,64,1024]{2,1,0:T(8,128)S(1)}, f32[2,64,1024]{2,1,0:T(8,128)S(1)}, f32[2,64,1024]{2,1,0:T(8,128)S(1)}, bf16[8,192,1024]{2,1,0:T(8,128)(2,1)S(1)}) custom-call(s32[3]{0:T(128)S(1)} %pad_add_fusion.place, bf16[512,1024]{1,0:T(8,128)(2,1)S(1)} %get-tuple-element.27.qh_ref.q_ref, bf16[512,1024]{1,0:T(8,128)(2,1)S(1)} %collective-permute-done.qp_ref, ...), custom_call_target="tpu_custom_call" | custom-call | flops 1610612736 | bytes 8388608 | tf_op jit(solution)/shard_map/beacons_near/pallas_call | solution.py:241
  23.7 0.9 %collective-permute-done.6.refs_1_.refs_0_ = bf16[2,64,1024]{2,1,0:T(8,128)(2,1)S(1)} collective-permute-done((bf16[2,64,1024]{2,1,0:T(8,128)(2,1)S(1)}, bf16[2,64,1024]{2,1,0:T(8,128)(2,1)S(1)}, u32[]{:S(2)}, u32[]{:S(2)}) %collective-permute-start.6) | collective-permute-done | bytes 262176 | tf_op jit(solution)/shard_map/ppermute | solution.py:319
  24.6 1.5 %collective-permute-done.5.refs_0_ = bf16[2,64,1024]{2,1,0:T(8,128)(2,1)S(1)} collective-permute-done((bf16[2,64,1024]{2,1,0:T(8,128)(2,1)S(1)}, bf16[2,64,1024]{2,1,0:T(8,128)(2,1)S(1)}, u32[]{:S(2)}, u32[]{:S(2)}) %collective-permute-start.5) | collective-permute-done | bytes 262176 | tf_op jit(solution)/shard_map/ppermute | solution.py:319
  26.1 0.3 collective-permute-start.8
  26.4 1.7 %collective-permute-start.7 = (bf16[2,64,1024]{2,1,0:T(8,128)(2,1)S(1)}, bf16[2,64,1024]{2,1,0:T(8,128)(2,1)S(1)}, u32[]{:S(2)}, u32[]{:S(2)}) collective-permute-start(bf16[2,64,1024]{2,1,0:T(8,128)(2,1)S(1)} %join.14.refs_1_.refs_0_.refs_7_), channel_id=1, source_target_pairs={{0,32},{16,48},{32,64},{48,80},{64,96},{80,112},{96,128},{112,144}... | collective-permute-start | bytes 786440 | tf_op jit(solution)/shard_map/ppermute | solution.py:324
  28.1 0.9 %beacons_second.1 = (f32[2,64,1024]{2,1,0:T(8,128)S(1)}, f32[2,64,1024]{2,1,0:T(8,128)S(1)}, bf16[8,128,1024]{2,1,0:T(8,128)(2,1)S(1)}) custom-call(s32[3]{0:T(128)S(1)} %pad_add_fusion.place, bf16[512,1024]{1,0:T(8,128)(2,1)S(1)} %get-tuple-element.27.qh_ref.q_ref, bf16[512,1024]{1,0:T(8,128)(2,1)S(1)} %collective-permute-done.qp_ref, ...), custom_call_target="tpu_custom_call" | custom-call | flops 1073741824 | bytes 8388608 | tf_op jit(solution)/shard_map/beacons_second/pallas_call | solution.py:241
  29.1 3.4 %collective-permute-done.8.refs_1_.refs_0_ = bf16[2,64,1024]{2,1,0:T(8,128)(2,1)S(1)} collective-permute-done((bf16[2,64,1024]{2,1,0:T(8,128)(2,1)S(1)}, bf16[2,64,1024]{2,1,0:T(8,128)(2,1)S(1)}, u32[]{:S(2)}, u32[]{:S(2)}) %collective-permute-start.8) | collective-permute-done | bytes 262176 | tf_op jit(solution)/shard_map/ppermute | solution.py:324
  32.5 1.5 %collective-permute-done.7.refs_0_ = bf16[2,64,1024]{2,1,0:T(8,128)(2,1)S(1)} collective-permute-done((bf16[2,64,1024]{2,1,0:T(8,128)(2,1)S(1)}, bf16[2,64,1024]{2,1,0:T(8,128)(2,1)S(1)}, u32[]{:S(2)}, u32[]{:S(2)}) %collective-permute-start.7) | collective-permute-done | bytes 262176 | tf_op jit(solution)/shard_map/ppermute | solution.py:324
  34.0 0.9 %collective-permute-start.9 = (bf16[2,64,1024]{2,1,0:T(8,128)(2,1)S(1)}, bf16[2,64,1024]{2,1,0:T(8,128)(2,1)S(1)}, u32[]{:S(2)}, u32[]{:S(2)}) collective-permute-start(bf16[2,64,1024]{2,1,0:T(8,128)(2,1)S(1)} %join.16.refs_1_.refs_0_.refs_9_), channel_id=1, source_target_pairs={{0,32},{16,48},{32,64},{48,80},{64,96},{80,112},{96,128},{112,144}... | collective-permute-start | bytes 786440 | tf_op jit(solution)/shard_map/ppermute | solution.py:327
  34.9 0.7 beacons_third.1
  35.6 5.9 %collective-permute-done.9.refs_0_.refs_11_ = bf16[2,64,1024]{2,1,0:T(8,128)(2,1)S(1)} collective-permute-done((bf16[2,64,1024]{2,1,0:T(8,128)(2,1)S(1)}, bf16[2,64,1024]{2,1,0:T(8,128)(2,1)S(1)}, u32[]{:S(2)}, u32[]{:S(2)}) %collective-permute-start.9) | collective-permute-done | bytes 262176 | tf_op jit(solution)/shard_map/ppermute | solution.py:327
  41.5 0.6 beacons_far.1
  42.2 2.1 %collective-permute-start.11 = (bf16[2,64,1024]{2,1,0:T(8,128)(2,1)S(1)}, bf16[2,64,1024]{2,1,0:T(8,128)(2,1)S(1)}, u32[]{:S(2)}, u32[]{:S(2)}) collective-permute-start(bf16[2,64,1024]{2,1,0:T(8,128)(2,1)S(1)} %get-tuple-element.33.wait), channel_id=1, source_target_pairs={{0,224},{16,240},{32,0},{48,16},{64,32},{80,48},{96,64},{112,80},{... | collective-permute-start | bytes 786440 | tf_op jit(solution)/shard_map/ppermute | solution.py:334
  44.3 1.7 %query_grad.1 = (f32[512,1024]{1,0:T(8,128)S(1)}, bf16[512,1024]{1,0:T(8,128)(2,1)S(1)}) custom-call(bf16[8,192,1024]{2,1,0:T(8,128)(2,1)S(1)} %get-tuple-element.30.refs_2_.refs_0_, bf16[8,128,1024]{2,1,0:T(8,128)(2,1)S(1)} %get-tuple-element.31.refs_2_.refs_1_, bf16[8,128,1024]{2,1,0:T(8,128)(2,1)S(1)} %get-tuple-element.32.refs_1_.refs_2_, ...), custom_call_target="tpu_custom_call" | custom-call | flops 1073741824 | bytes 16777216 | tf_op jit(solution)/shard_map/query_grad/pallas_call | solution.py:266
  46.0 0.1 collective-permute-start.10
  46.1 1.6 %load.1 = (bf16[512,1024]{1,0:T(8,128)(2,1)S(1)}, bf16[512,1024]{1,0:T(8,128)(2,1)S(1)}) custom-call(bf16[512,1024]{1,0:T(8,128)(2,1)} %k_any.1, bf16[512,1024]{1,0:T(8,128)(2,1)} %v_any.1, bf16[2,64,1024]{2,1,0:T(8,128)(2,1)S(1)} %get-tuple-element.33.wait), custom_call_target="tpu_custom_call" | custom-call | bytes 4194304 | tf_op jit(solution)/shard_map/load/pallas_call | solution.py:137
  47.7 0.9 %collective-permute-done.11.refs_0_ = bf16[2,64,1024]{2,1,0:T(8,128)(2,1)S(1)} collective-permute-done((bf16[2,64,1024]{2,1,0:T(8,128)(2,1)S(1)}, bf16[2,64,1024]{2,1,0:T(8,128)(2,1)S(1)}, u32[]{:S(2)}, u32[]{:S(2)}) %collective-permute-start.11) | collective-permute-done | bytes 262176 | tf_op jit(solution)/shard_map/ppermute | solution.py:334
  48.6 0.1 add_convert_fusion.6
  48.7 0.3 collective-permute-start.13
  49.0 3.3 %collective-permute-start.12 = (bf16[2,64,1024]{2,1,0:T(8,128)(2,1)S(1)}, bf16[2,64,1024]{2,1,0:T(8,128)(2,1)S(1)}, u32[]{:S(2)}, u32[]{:S(2)}) collective-permute-start(bf16[2,64,1024]{2,1,0:T(8,128)(2,1)S(1)} %add_convert_fusion.6), channel_id=1, source_target_pairs={{0,224},{16,240},{32,0},{48,16},{64,32},{80,48},{96,64},{112,80},{... | collective-permute-start | bytes 786440 | tf_op jit(solution)/shard_map/ppermute | solution.py:338
  52.3 5.3 %raw_tokens.1 = (f32[512,1024]{1,0:T(8,128)S(1)}, bf16[512,1024]{1,0:T(8,128)(2,1)}, bf16[512,1024]{1,0:T(8,128)(2,1)}) custom-call(bf16[512,1024]{1,0:T(8,128)(2,1)S(1)} %get-tuple-element.27.qh_ref.q_ref, bf16[512,1024]{1,0:T(8,128)(2,1)S(1)} %get-tuple-element.34.k_ref.refs_3_, bf16[512,1024]{1,0:T(8,128)(2,1)S(1)} %get-tuple-element.35.v_ref, ...), custom_call_target="tpu_custom_call" | custom-call | flops 2684354560 | bytes 10485760 | tf_op jit(solution)/shard_map/raw_tokens/pallas_call | solution.py:152
  57.7 0.3 collective-permute-done.13.refs_1_.refs_0_
  58.0 0.0 collective-permute-done.12.refs_0_
  58.0 0.1 add_convert_fusion.4
  58.1 0.1 collective-permute-start.15
  58.2 0.1 add_convert_fusion.5
  58.2 3.3 %collective-permute-start.14 = (bf16[2,64,1024]{2,1,0:T(8,128)(2,1)S(1)}, bf16[2,64,1024]{2,1,0:T(8,128)(2,1)S(1)}, u32[]{:S(2)}, u32[]{:S(2)}) collective-permute-start(bf16[2,64,1024]{2,1,0:T(8,128)(2,1)S(1)} %add_convert_fusion.5), channel_id=1, source_target_pairs={{0,224},{16,240},{32,0},{48,16},{64,32},{80,48},{96,64},{112,80},{... | collective-permute-start | bytes 786440 | tf_op jit(solution)/shard_map/ppermute | solution.py:341
  61.5 0.0 collective-permute-done.10
  61.5 0.6 add_convert_fusion.refs_2_
  62.2 0.0 copy-start
  62.2 4.0 %collective-permute-done.15.refs_1_.refs_0_ = bf16[2,64,1024]{2,1,0:T(8,128)(2,1)S(1)} collective-permute-done((bf16[2,64,1024]{2,1,0:T(8,128)(2,1)S(1)}, bf16[2,64,1024]{2,1,0:T(8,128)(2,1)S(1)}, u32[]{:S(2)}, u32[]{:S(2)}) %collective-permute-start.15) | collective-permute-done | bytes 262176 | tf_op jit(solution)/shard_map/ppermute | solution.py:341
  66.2 0.0 collective-permute-done.14.refs_0_
  66.2 0.1 add_convert_fusion.3
  66.3 0.1 add_convert_fusion.2
  66.4 0.0 copy-done
  66.4 1.2 %collective-permute-start.17 = (bf16[2,64,1024]{2,1,0:T(8,128)(2,1)S(1)}, bf16[2,64,1024]{2,1,0:T(8,128)(2,1)S(1)}, u32[]{:S(2)}, u32[]{:S(2)}) collective-permute-start(bf16[2,64,1024]{2,1,0:T(8,128)(2,1)S(1)} %add_convert_fusion.2), channel_id=1, source_target_pairs={{0,32},{16,48},{32,64},{48,80},{64,96},{80,112},{96,128},{112,144}... | collective-permute-start | bytes 786440 | tf_op jit(solution)/shard_map/ppermute | solution.py:344
  67.6 2.1 %collective-permute-start.16 = (bf16[2,64,1024]{2,1,0:T(8,128)(2,1)S(1)}, bf16[2,64,1024]{2,1,0:T(8,128)(2,1)S(1)}, u32[]{:S(2)}, u32[]{:S(2)}) collective-permute-start(bf16[2,64,1024]{2,1,0:T(8,128)(2,1)S(1)} %add_convert_fusion.3), channel_id=1, source_target_pairs={{0,224},{16,240},{32,0},{48,16},{64,32},{80,48},{96,64},{112,80},{... | collective-permute-start | bytes 786440 | tf_op jit(solution)/shard_map/ppermute | solution.py:344
  69.7 4.3 %collective-permute-done.17 = bf16[2,64,1024]{2,1,0:T(8,128)(2,1)S(1)} collective-permute-done((bf16[2,64,1024]{2,1,0:T(8,128)(2,1)S(1)}, bf16[2,64,1024]{2,1,0:T(8,128)(2,1)S(1)}, u32[]{:S(2)}, u32[]{:S(2)}) %collective-permute-start.17) | collective-permute-done | bytes 262176 | tf_op jit(solution)/shard_map/ppermute | solution.py:344
  74.1 0.0 collective-permute-done.16
  74.1 0.1 add_convert_fusion.1
  74.2 0.7 slice_bitcast_fusion
  (12 shorter events, 0.0 us)
Async XLA Ops:
  0.6 18.8 %collective-permute-start = (bf16[512,1024]{1,0:T(8,128)(2,1)}, bf16[512,1024]{1,0:T(8,128)(2,1)S(1)}, u32[]{:S(2)}, u32[]{:S(2)}) collective-permute-start(bf16[512,1024]{1,0:T(8,128)(2,1)} %q_any.1), channel_id=1, source_target_pairs={{0,16},{16,0},{32,48},{48,32},{64,80},{80,64},{96,112},{112,96},{1... | collective-permute-start | bytes 3145736 | tf_op jit(solution)/shard_map/ppermute | solution.py:315
  0.7 18.7 %collective-permute-start.1 = (bf16[512,1024]{1,0:T(8,128)(2,1)}, bf16[512,1024]{1,0:T(8,128)(2,1)S(1)}, u32[]{:S(2)}, u32[]{:S(2)}) collective-permute-start(bf16[512,1024]{1,0:T(8,128)(2,1)} %g_any.1), channel_id=1, source_target_pairs={{0,16},{16,0},{32,48},{48,32},{64,80},{80,64},{96,112},{112,96},{1... | collective-permute-start | bytes 3145736 | tf_op jit(solution)/shard_map/ppermute | solution.py:315
  2.2 11.8 %collective-permute-start.4 = (bf16[2,64,1024]{2,1,0:T(8,128)(2,1)S(1)}, bf16[2,64,1024]{2,1,0:T(8,128)(2,1)S(1)}, u32[]{:S(2)}, u32[]{:S(2)}) collective-permute-start(bf16[2,64,1024]{2,1,0:T(8,128)(2,1)S(1)} %pad_maximum_fusion.refs_2_.refs_6_), channel_id=1, source_target_pairs={{0,224},{16,240},{32,0},{48,16},{64,32},{80,48},{96,64},{112,80},{... | collective-permute-start | bytes 786440 | tf_op jit(solution)/shard_map/ppermute | solution.py:314
  8.2 9.2 %collective-permute-start.3 = (bf16[2,64,1024]{2,1,0:T(8,128)(2,1)S(1)}, bf16[2,64,1024]{2,1,0:T(8,128)(2,1)S(1)}, u32[]{:S(2)}, u32[]{:S(2)}) collective-permute-start(bf16[2,64,1024]{2,1,0:T(8,128)(2,1)S(1)} %pad_maximum_fusion.refs_2_.refs_6_), channel_id=1, source_target_pairs={{0,32},{16,48},{32,64},{48,80},{64,96},{80,112},{96,128},{112,144}... | collective-permute-start | bytes 786440 | tf_op jit(solution)/shard_map/ppermute | solution.py:314
  11.7 1.3 %collective-permute-start.2 = (f32[3,8,512]{2,1,0:T(8,128)S(1)}, f32[3,8,512]{2,1,0:T(8,128)S(1)}, u32[]{:S(2)}, u32[]{:S(2)}) collective-permute-start(f32[3,8,512]{2,1,0:T(8,128)S(1)} %get-tuple-element.29.sh_ref.st_ref), channel_id=1, source_target_pairs={{0,16},{16,0},{32,48},{48,32},{64,80},{80,64},{96,112},{112,96},{1... | collective-permute-start | bytes 147464 | tf_op jit(solution)/shard_map/ppermute | solution.py:317
  17.4 7.2 %collective-permute-start.6 = (bf16[2,64,1024]{2,1,0:T(8,128)(2,1)S(1)}, bf16[2,64,1024]{2,1,0:T(8,128)(2,1)S(1)}, u32[]{:S(2)}, u32[]{:S(2)}) collective-permute-start(bf16[2,64,1024]{2,1,0:T(8,128)(2,1)S(1)} %join.13.refs_1_.refs_5_), channel_id=1, source_target_pairs={{0,224},{16,240},{32,0},{48,16},{64,32},{80,48},{96,64},{112,80},{... | collective-permute-start | bytes 786440 | tf_op jit(solution)/shard_map/ppermute | solution.py:319
  17.7 8.4 %collective-permute-start.5 = (bf16[2,64,1024]{2,1,0:T(8,128)(2,1)S(1)}, bf16[2,64,1024]{2,1,0:T(8,128)(2,1)S(1)}, u32[]{:S(2)}, u32[]{:S(2)}) collective-permute-start(bf16[2,64,1024]{2,1,0:T(8,128)(2,1)S(1)} %join.12.refs_1_.refs_0_.refs_4_), channel_id=1, source_target_pairs={{0,32},{16,48},{32,64},{48,80},{64,96},{80,112},{96,128},{112,144}... | collective-permute-start | bytes 786440 | tf_op jit(solution)/shard_map/ppermute | solution.py:319
  26.1 6.4 %collective-permute-start.8 = (bf16[2,64,1024]{2,1,0:T(8,128)(2,1)S(1)}, bf16[2,64,1024]{2,1,0:T(8,128)(2,1)S(1)}, u32[]{:S(2)}, u32[]{:S(2)}) collective-permute-start(bf16[2,64,1024]{2,1,0:T(8,128)(2,1)S(1)} %join.15.refs_1_.refs_8_), channel_id=1, source_target_pairs={{0,224},{16,240},{32,0},{48,16},{64,32},{80,48},{96,64},{112,80},{... | collective-permute-start | bytes 786440 | tf_op jit(solution)/shard_map/ppermute | solution.py:324
  26.4 7.6 %collective-permute-start.7 = (bf16[2,64,1024]{2,1,0:T(8,128)(2,1)S(1)}, bf16[2,64,1024]{2,1,0:T(8,128)(2,1)S(1)}, u32[]{:S(2)}, u32[]{:S(2)}) collective-permute-start(bf16[2,64,1024]{2,1,0:T(8,128)(2,1)S(1)} %join.14.refs_1_.refs_0_.refs_7_), channel_id=1, source_target_pairs={{0,32},{16,48},{32,64},{48,80},{64,96},{80,112},{96,128},{112,144}... | collective-permute-start | bytes 786440 | tf_op jit(solution)/shard_map/ppermute | solution.py:324
  34.0 7.6 %collective-permute-start.9 = (bf16[2,64,1024]{2,1,0:T(8,128)(2,1)S(1)}, bf16[2,64,1024]{2,1,0:T(8,128)(2,1)S(1)}, u32[]{:S(2)}, u32[]{:S(2)}) collective-permute-start(bf16[2,64,1024]{2,1,0:T(8,128)(2,1)S(1)} %join.16.refs_1_.refs_0_.refs_9_), channel_id=1, source_target_pairs={{0,32},{16,48},{32,64},{48,80},{64,96},{80,112},{96,128},{112,144}... | collective-permute-start | bytes 786440 | tf_op jit(solution)/shard_map/ppermute | solution.py:327
  42.2 6.5 %collective-permute-start.11 = (bf16[2,64,1024]{2,1,0:T(8,128)(2,1)S(1)}, bf16[2,64,1024]{2,1,0:T(8,128)(2,1)S(1)}, u32[]{:S(2)}, u32[]{:S(2)}) collective-permute-start(bf16[2,64,1024]{2,1,0:T(8,128)(2,1)S(1)} %get-tuple-element.33.wait), channel_id=1, source_target_pairs={{0,224},{16,240},{32,0},{48,16},{64,32},{80,48},{96,64},{112,80},{... | collective-permute-start | bytes 786440 | tf_op jit(solution)/shard_map/ppermute | solution.py:334
  46.0 15.5 %collective-permute-start.10 = (bf16[512,1024]{1,0:T(8,128)(2,1)S(1)}, bf16[512,1024]{1,0:T(8,128)(2,1)S(1)}, u32[]{:S(2)}, u32[]{:S(2)}) collective-permute-start(bf16[512,1024]{1,0:T(8,128)(2,1)S(1)} %get-tuple-element.37.wait.refs_2_), channel_id=1, source_target_pairs={{0,16},{16,0},{32,48},{48,32},{64,80},{80,64},{96,112},{112,96},{1... | collective-permute-start | bytes 3145736 | tf_op jit(solution)/shard_map/ppermute | solution.py:342
  48.7 9.3 %collective-permute-start.13 = (bf16[2,64,1024]{2,1,0:T(8,128)(2,1)S(1)}, bf16[2,64,1024]{2,1,0:T(8,128)(2,1)S(1)}, u32[]{:S(2)}, u32[]{:S(2)}) collective-permute-start(bf16[2,64,1024]{2,1,0:T(8,128)(2,1)S(1)} %join.19), channel_id=1, source_target_pairs={{0,32},{16,48},{32,64},{48,80},{64,96},{80,112},{96,128},{112,144}... | collective-permute-start | bytes 786440 | tf_op jit(solution)/shard_map/ppermute | solution.py:338
  49.0 9.0 %collective-permute-start.12 = (bf16[2,64,1024]{2,1,0:T(8,128)(2,1)S(1)}, bf16[2,64,1024]{2,1,0:T(8,128)(2,1)S(1)}, u32[]{:S(2)}, u32[]{:S(2)}) collective-permute-start(bf16[2,64,1024]{2,1,0:T(8,128)(2,1)S(1)} %add_convert_fusion.6), channel_id=1, source_target_pairs={{0,224},{16,240},{32,0},{48,16},{64,32},{80,48},{96,64},{112,80},{... | collective-permute-start | bytes 786440 | tf_op jit(solution)/shard_map/ppermute | solution.py:338
  58.1 8.2 %collective-permute-start.15 = (bf16[2,64,1024]{2,1,0:T(8,128)(2,1)S(1)}, bf16[2,64,1024]{2,1,0:T(8,128)(2,1)S(1)}, u32[]{:S(2)}, u32[]{:S(2)}) collective-permute-start(bf16[2,64,1024]{2,1,0:T(8,128)(2,1)S(1)} %add_convert_fusion.4), channel_id=1, source_target_pairs={{0,32},{16,48},{32,64},{48,80},{64,96},{80,112},{96,128},{112,144}... | collective-permute-start | bytes 786440 | tf_op jit(solution)/shard_map/ppermute | solution.py:341
  58.2 8.0 %collective-permute-start.14 = (bf16[2,64,1024]{2,1,0:T(8,128)(2,1)S(1)}, bf16[2,64,1024]{2,1,0:T(8,128)(2,1)S(1)}, u32[]{:S(2)}, u32[]{:S(2)}) collective-permute-start(bf16[2,64,1024]{2,1,0:T(8,128)(2,1)S(1)} %add_convert_fusion.5), channel_id=1, source_target_pairs={{0,224},{16,240},{32,0},{48,16},{64,32},{80,48},{96,64},{112,80},{... | collective-permute-start | bytes 786440 | tf_op jit(solution)/shard_map/ppermute | solution.py:341
  62.2 4.2 %copy-start = (bf16[512,1024]{1,0:T(8,128)(2,1)}, bf16[512,1024]{1,0:T(8,128)(2,1)S(1)}, u32[]{:S(2)}) copy-start(bf16[512,1024]{1,0:T(8,128)(2,1)S(1)} %add_convert_fusion.refs_2_) | copy-start | bytes 3145732
  66.4 7.7 %collective-permute-start.17 = (bf16[2,64,1024]{2,1,0:T(8,128)(2,1)S(1)}, bf16[2,64,1024]{2,1,0:T(8,128)(2,1)S(1)}, u32[]{:S(2)}, u32[]{:S(2)}) collective-permute-start(bf16[2,64,1024]{2,1,0:T(8,128)(2,1)S(1)} %add_convert_fusion.2), channel_id=1, source_target_pairs={{0,32},{16,48},{32,64},{48,80},{64,96},{80,112},{96,128},{112,144}... | collective-permute-start | bytes 786440 | tf_op jit(solution)/shard_map/ppermute | solution.py:344
  67.6 6.5 %collective-permute-start.16 = (bf16[2,64,1024]{2,1,0:T(8,128)(2,1)S(1)}, bf16[2,64,1024]{2,1,0:T(8,128)(2,1)S(1)}, u32[]{:S(2)}, u32[]{:S(2)}) collective-permute-start(bf16[2,64,1024]{2,1,0:T(8,128)(2,1)S(1)} %add_convert_fusion.3), channel_id=1, source_target_pairs={{0,224},{16,240},{32,0},{48,16},{64,32},{80,48},{96,64},{112,80},{... | collective-permute-start | bytes 786440 | tf_op jit(solution)/shard_map/ppermute | solution.py:344
